TPU v7x, 128 devices: a whole 4x4x4 slice. The times are simulated.
128 devices in a mesh: phase: 2 (over core), blk: 64 (over x, y, z).
Axes of the slice: x: 4, y: 4, z: 4, core: 2. Of those that a mesh axis runs over, the one named last changes fastest.
Arguments:
- normals: bfloat16 [128, 65536], P(None, 'blk'), may hold values from -6 to 6
- section_tile_list: bfloat16 [2, 1280, 512, 512], P('phase', 'blk'), may hold values from -0.078125 to 0.078125
- tile_output_block: int32 [2, 1280], P('phase'), may hold values from 0 to 127, as said below
- tile_col: int32 [2, 1280], P('phase', 'blk'), may hold values from 0 to 1
- notional: float32 [65536], P('blk'), may hold values from 1 to 8
- strike: float32 [65536], P('blk'), may hold values from -4 to 4
Outputs:
- tile_sens: bfloat16 [2, 1280, 512, 512], P('phase', 'blk')
- input_adjoint: bfloat16 [2, 128, 65536], P('phase', None, 'blk')
Inputs may be any that keep to these rules, and one draw needn't show every extreme that they name: Within one section, the 20 tiles of one index i of blk (tiles i * 20 to i * 20 + 19) have output blocks on distinct indices of blk, index = tile_output_block // 2.
All inputs are finite; a program needn't handle non-finite values.
Results may differ from a plain program's by a relative error of at most 0.008.
Values may be sent and summed in bfloat16 or wider, within the bound.
No kernel may reach another device: no remote copies, remote signals or barrier semaphores. Data moves between devices by JAX's collectives and lax.ppermute only.
A program may use at most 256 MiB of HBM per device.

v0:
```python
import math

import jax
import jax.numpy as jnp
from jax import lax
from jax.sharding import PartitionSpec as P

MICRO = 2


def shifted(block, axis, distance):
    devices = range(lax.axis_size(axis))
    route = [(i - distance, i) for i in devices if i - distance in devices]
    return lax.ppermute(block, axis, route)


def on_device(normals, section_tile_list, tile_output_block, tile_col, notional, strike):
    blk_count = lax.axis_size("blk")
    me_blk = lax.axis_index("blk")
    phase_index = lax.axis_index("phase")
    my_tiles = section_tile_list[0]
    slot_count = my_tiles.shape[0]
    tile_width = my_tiles.shape[1]
    local_width = normals.shape[1]
    blocks_dev = local_width // tile_width
    scen_all = normals.shape[0]
    rows_all = tile_output_block[0].reshape(blk_count, slot_count)
    my_rows = lax.dynamic_index_in_dim(rows_all, me_blk, 0, keepdims=False)
    columns = tile_col[0]
    owners = my_rows // blocks_dev
    peer_ids = jnp.arange(blk_count, dtype=jnp.int32)
    slot_ids = jnp.arange(slot_count, dtype=jnp.int32)
    match_send = owners[None, :] == peer_ids[:, None]
    send_pos = jnp.sum(jnp.where(match_send, slot_ids[None, :], 0), axis=1)
    send_live = jnp.any(match_send, axis=1)
    match_recv = rows_all // blocks_dev == me_blk
    recv_block = jnp.sum(jnp.where(match_recv, rows_all % blocks_dev, 0), axis=1)
    recv_live = jnp.any(match_recv, axis=1)
    local_ids = jnp.arange(blocks_dev, dtype=jnp.int32)
    recv_select = ((recv_block[None, :] == local_ids[:, None]) & recv_live[None, :]).astype(
        jnp.bfloat16
    )
    column_select = (columns[:, None] == local_ids[None, :]).astype(jnp.float32)
    zero_half = jnp.zeros((), jnp.bfloat16)

    def pick_columns(inputs):
        row_count = inputs.shape[0]
        return jnp.take(inputs.reshape(row_count, blocks_dev, tile_width), columns, axis=1)

    batches = MICRO
    batch_rows = scen_all // batches
    saved_in = jnp.zeros((batches, batch_rows, local_width), jnp.bfloat16)
    kept_output_values = jnp.zeros((batches, batch_rows, local_width), jnp.float32)
    carried = jnp.zeros((batch_rows, local_width), jnp.bfloat16)
    for clock_tick in range(batches + 1):
        batch_index = clock_tick - phase_index
        is_valid = (batch_index >= 0) & (batch_index < batches)
        write_position = jnp.clip(batch_index, 0, batches - 1)
        own_rows = lax.dynamic_slice_in_dim(normals, write_position * batch_rows, batch_rows, 0)
        inputs = jnp.where(phase_index == 0, own_rows, carried)
        forward_row_count = inputs.shape[0]
        picked = pick_columns(inputs)
        products = jnp.einsum(
            "rtk,tkn->rtn", picked, my_tiles, preferred_element_type=jnp.float32
        ).astype(jnp.bfloat16)
        forward_outgoing = jnp.where(
            send_live[None, :, None], jnp.take(products, send_pos, axis=1), zero_half
        )
        incoming = lax.all_to_all(forward_outgoing, "blk", split_axis=1, concat_axis=1, tiled=True)
        forward_summed = jnp.einsum(
            "li,rin->rln", recv_select, incoming, preferred_element_type=jnp.float32
        )
        result = forward_summed.reshape(forward_row_count, local_width)
        saved_in = jnp.where(
            is_valid, lax.dynamic_update_index_in_dim(saved_in, inputs, write_position, 0), saved_in
        )
        kept_output_values = jnp.where(
            is_valid,
            lax.dynamic_update_index_in_dim(kept_output_values, result, write_position, 0),
            kept_output_values,
        )
        if clock_tick < batches:
            carried = shifted(result.astype(jnp.bfloat16), "phase", 1)
    scenario_path_weight = 1.0 / math.sqrt(scen_all)
    carried_grad = jnp.zeros((batch_rows, local_width), jnp.bfloat16)
    adjoint = jnp.zeros((batches, batch_rows, local_width), jnp.bfloat16)
    sensitivity = jnp.zeros((slot_count, tile_width, tile_width), jnp.float32)
    for clock_tick in range(batches + 1):
        batch_index = clock_tick - (1 - phase_index)
        is_valid = (batch_index >= 0) & (batch_index < batches)
        write_position = jnp.clip(batch_index, 0, batches - 1)
        valued_paths = lax.dynamic_index_in_dim(
            kept_output_values, write_position, 0, keepdims=False
        )
        valuation_gradient = (
            notional[None, :]
            * jax.nn.sigmoid(valued_paths - strike[None, :])
            * scenario_path_weight
        ).astype(jnp.bfloat16)
        out_grads = jnp.where(phase_index == 1, valuation_gradient, carried_grad)
        inputs = lax.dynamic_index_in_dim(saved_in, write_position, 0, keepdims=False)
        backward_row_count = out_grads.shape[0]
        grad_blocks = out_grads.reshape(backward_row_count, blocks_dev, tile_width)
        outgoing = jnp.where(
            recv_live[None, :, None], jnp.take(grad_blocks, recv_block, axis=1), zero_half
        )
        returned = lax.all_to_all(outgoing, "blk", split_axis=1, concat_axis=1, tiled=True)
        tile_grads = jnp.take(returned, owners, axis=1)
        input_row_count = tile_grads.shape[0]
        per_tile = jnp.einsum(
            "rtn,tkn->rtk", tile_grads, my_tiles, preferred_element_type=jnp.float32
        )
        summed = jnp.einsum("rtk,tc->rck", per_tile, column_select, precision=lax.Precision.HIGHEST)
        in_grads = summed.reshape(input_row_count, local_width).astype(jnp.bfloat16)
        adjoint = jnp.where(
            is_valid, lax.dynamic_update_index_in_dim(adjoint, in_grads, write_position, 0), adjoint
        )
        sens_part = jnp.einsum(
            "rtk,rtn->tkn", pick_columns(inputs), tile_grads, preferred_element_type=jnp.float32
        )
        sensitivity = sensitivity + jnp.where(is_valid, sens_part, 0.0)
        if clock_tick < batches:
            carried_grad = shifted(in_grads, "phase", -1)
    return (sensitivity.astype(jnp.bfloat16)[None], adjoint.reshape(1, scen_all, local_width))


def solution(mesh):
    return jax.shard_map(
        on_device,
        mesh=mesh,
        in_specs=(
            P(None, "blk"),
            P("phase", "blk", None, None),
            P("phase", None),
            P("phase", "blk"),
            P("blk"),
            P("blk"),
        ),
        out_specs=(P("phase", "blk", None, None), P("phase", None, "blk")),
        check_vma=False,
    )
```

profile of v0, /device:TPU:1, one launch (start us, length us, event | category | flops | bytes accessed | tf_op | source)
XLA Modules:
  0.0 525.5 jit_solution(12129376575222274780)
XLA Ops:
  5.5 5.9 %fusion.49 = bf16[64,20,512]{2,0,1:T(8,128)(2,1)S(1)} fusion(bf16[1,20,512,512]{3,2,1,0:T(8,128)(2,1)} %param.15, bf16[20,64,512]{2,1,0:T(8,128)(2,1)S(1)} %gather_fusion, pred[20]{0:T(512)(128)(4,1)S(1)} %compare_and_fusion.2), kind=kOutput, calls=%fused_computation.55 | convolution fusion | flops 672399360 | bytes 13107220 | tf_op jit(solution)/shard_map/rtk,tkn->rtn/dot_general | solution.py:63
  11.4 2.8 gather_fusion.1
  14.2 4.0 bitcast_select_fusion.5
  18.3 12.2 %all-to-all-start = ((bf16[64,64,512]{2,0,1:T(8,128)(2,1)}), bf16[64,64,512]{2,0,1:T(8,128)(2,1)}, u32[]{:S(2)}, u32[]{:S(2)}) async-start(bf16[64,64,512]{2,0,1:T(8,128)(2,1)} %bitcast_select_fusion.5), calls=%async_computation | async-start | bytes 8388608 | tf_op jit(solution)/shard_map/all_to_all | solution.py:69
  30.6 50.8 %all-to-all-done = bf16[64,64,512]{2,0,1:T(8,128)(2,1)} async-done(((bf16[64,64,512]{2,0,1:T(8,128)(2,1)}), bf16[64,64,512]{2,0,1:T(8,128)(2,1)}, u32[]{:S(2)}, u32[]{:S(2)}) %all-to-all-start) | async-done | bytes 4194336 | tf_op jit(solution)/shard_map/all_to_all | solution.py:69
  81.5 4.6 select_bitcast_fusion
  86.1 1.3 collective-permute-start
  87.4 2.7 collective-permute-done
  90.8 5.9 %fusion.46 = bf16[64,20,512]{2,0,1:T(8,128)(2,1)S(1)} fusion(bf16[1,20,512,512]{3,2,1,0:T(8,128)(2,1)} %param.15, bf16[20,64,512]{2,1,0:T(8,128)(2,1)S(1)} %gather_fusion.2, pred[20]{0:T(512)(128)(4,1)S(1)} %compare_and_fusion.2), kind=kOutput, calls=%fused_computation.54 | convolution fusion | flops 672399360 | bytes 13107220 | tf_op jit(solution)/shard_map/rtk,tkn->rtn/dot_general | solution.py:63
  96.8 2.8 gather_fusion.3
  99.6 2.7 bitcast_select_fusion.4
  102.3 64.2 %all_to_all.30 = bf16[64,64,512]{2,0,1:T(8,128)(2,1)S(1)} all-to-all(bf16[64,64,512]{2,0,1:T(8,128)(2,1)S(1)} %bitcast_select_fusion.4), channel_id=1, replica_groups=mesh['phase'=2,'blk'=64] {'blk'}, dimensions={1} | all-to-all | bytes 8388608 | tf_op jit(solution)/shard_map/all_to_all | solution.py:69
  166.4 3.1 fusion.155
  170.9 3.4 collective-permute-done.1
  175.1 5.9 %fusion.43 = bf16[64,20,512]{2,0,1:T(8,128)(2,1)S(1)} fusion(bf16[1,20,512,512]{3,2,1,0:T(8,128)(2,1)} %param.15, bf16[20,64,512]{2,1,0:T(8,128)(2,1)S(1)} %gather_fusion.5, pred[20]{0:T(512)(128)(4,1)S(1)} %compare_and_fusion.2), kind=kOutput, calls=%fused_computation.53 | convolution fusion | flops 672399360 | bytes 13107220 | tf_op jit(solution)/shard_map/rtk,tkn->rtn/dot_general | solution.py:63
  181.0 2.8 gather_fusion.6
  183.8 4.0 bitcast_select_fusion.3
  187.9 6.4 %all-to-all-start.2 = ((bf16[64,64,512]{2,0,1:T(8,128)(2,1)}), bf16[64,64,512]{2,0,1:T(8,128)(2,1)}, u32[]{:S(2)}, u32[]{:S(2)}) async-start(bf16[64,64,512]{2,0,1:T(8,128)(2,1)} %bitcast_select_fusion.3), calls=%async_computation.2 | async-start | bytes 8388608 | tf_op jit(solution)/shard_map/all_to_all | solution.py:69
  195.0 51.9 %all-to-all-done.2 = bf16[64,64,512]{2,0,1:T(8,128)(2,1)} async-done(((bf16[64,64,512]{2,0,1:T(8,128)(2,1)}), bf16[64,64,512]{2,0,1:T(8,128)(2,1)}, u32[]{:S(2)}, u32[]{:S(2)}) %all-to-all-start.2) | async-done | bytes 4194336 | tf_op jit(solution)/shard_map/all_to_all | solution.py:69
  246.9 4.5 fusion.81
  252.1 2.8 gather_fusion.7
  255.0 4.0 bitcast_select_fusion.2
  259.0 14.5 %all-to-all-start.3 = ((bf16[64,64,512]{2,0,1:T(8,128)(2,1)}), bf16[64,64,512]{2,0,1:T(8,128)(2,1)}, u32[]{:S(2)}, u32[]{:S(2)}) async-start(bf16[64,64,512]{2,0,1:T(8,128)(2,1)} %bitcast_select_fusion.2), calls=%async_computation.3 | async-start | bytes 8388608 | tf_op jit(solution)/shard_map/all_to_all | solution.py:107
  274.3 48.2 %all-to-all-done.3 = bf16[64,64,512]{2,0,1:T(8,128)(2,1)} async-done(((bf16[64,64,512]{2,0,1:T(8,128)(2,1)}), bf16[64,64,512]{2,0,1:T(8,128)(2,1)}, u32[]{:S(2)}, u32[]{:S(2)}) %all-to-all-start.3) | async-done | bytes 4194336 | tf_op jit(solution)/shard_map/all_to_all | solution.py:107
  322.4 2.8 gather_fusion.8
  325.3 7.3 %fusion.25 = f32[64,20,512]{2,0,1:T(8,128)S(1)} fusion(bf16[1,20,512,512]{3,2,1,0:T(8,128)(2,1)} %param.15, bf16[20,64,512]{2,1,0:T(8,128)(2,1)S(1)} %gather_fusion.8, pred[20]{0:T(512)(128)(4,1)S(1)} %get-tuple-element.4), kind=kOutput, calls=%fused_computation.47 | convolution fusion | flops 671744000 | bytes 14417940 | tf_op jit(solution)/shard_map/rtn,tkn->rtk/dot_general | solution.py:110
  332.5 2.6 fusion.84
  335.1 5.4 %collective-permute-start.2 = (bf16[64,1024]{1,0:T(8,128)(2,1)S(1)}, bf16[64,1024]{1,0:T(8,128)(2,1)S(1)}, u32[]{:S(2)}, u32[]{:S(2)}) collective-permute-start(bf16[64,1024]{1,0:T(8,128)(2,1)S(1)} %bitcast.230), channel_id=1, source_target_pairs={{64,0},{65,1},{66,2},{67,3},{68,4},{69,5},{70,6},{71,7},{72,8},{73... | collective-permute-start | bytes 393224 | tf_op jit(solution)/shard_map/ppermute | solution.py:14
  341.6 2.8 gather_fusion.10
  344.4 2.7 bitcast_select_fusion.1
  347.1 60.6 %all_to_all.31 = bf16[64,64,512]{2,0,1:T(8,128)(2,1)} all-to-all(bf16[64,64,512]{2,0,1:T(8,128)(2,1)S(1)} %bitcast_select_fusion.1), channel_id=1, replica_groups=mesh['phase'=2,'blk'=64] {'blk'}, dimensions={1} | all-to-all | bytes 8388608 | tf_op jit(solution)/shard_map/all_to_all | solution.py:107
  407.7 2.9 gather_fusion.11
  410.7 7.3 %fusion.28 = f32[64,20,512]{2,0,1:T(8,128)S(1)} fusion(bf16[1,20,512,512]{3,2,1,0:T(8,128)(2,1)} %param.15, bf16[20,64,512]{2,1,0:T(8,128)(2,1)S(1)} %gather_fusion.11, pred[20]{0:T(512)(128)(4,1)S(1)} %get-tuple-element.4), kind=kOutput, calls=%fused_computation.48 | convolution fusion | flops 671744000 | bytes 14417940 | tf_op jit(solution)/shard_map/rtn,tkn->rtk/dot_general | solution.py:110
  418.0 2.6 fusion.87
  421.2 4.8 collective-permute-start.3
  427.1 3.0 gather_fusion.13
  430.0 4.0 bitcast_select_fusion
  434.0 6.1 %all-to-all-start.5 = ((bf16[64,64,512]{2,0,1:T(8,128)(2,1)}), bf16[64,64,512]{2,0,1:T(8,128)(2,1)}, u32[]{:S(2)}, u32[]{:S(2)}) async-start(bf16[64,64,512]{2,0,1:T(8,128)(2,1)} %bitcast_select_fusion), calls=%async_computation.5 | async-start | bytes 8388608 | tf_op jit(solution)/shard_map/all_to_all | solution.py:107
  440.5 1.9 gather_fusion.4
  442.5 2.0 gather_fusion.9
  444.5 1.9 gather_fusion.12
  446.7 10.7 %fusion.60 = f32[20,512,512]{2,1,0:T(8,128)} fusion(bf16[20,64,512]{2,1,0:T(8,128)(2,1)} %gather_fusion.4, pred[20]{0:T(512)(128)(4,1)S(1)} %compare_and_fusion.2, bf16[20,64,512]{2,1,0:T(8,128)(2,1)S(1)} %gather_fusion.8, pred[20]{0:T(512)(128)(4,1)S(1)} %get-tuple-element.4), kind=kOutput, calls=%fused_computation.64 | convolution fusion | flops 672399360 | bytes 23593000 | tf_op jit(solution)/shard_map/rtk,rtn->tkn/dot_general | solution.py:118
  457.5 10.6 %fusion.56 = f32[20,512,512]{2,1,0:T(8,128)} fusion(bf16[20,64,512]{2,1,0:T(8,128)(2,1)} %gather_fusion.9, pred[20]{0:T(512)(128)(4,1)S(1)} %compare_and_fusion.2, bf16[20,64,512]{2,1,0:T(8,128)(2,1)S(1)} %gather_fusion.11, pred[20]{0:T(512)(128)(4,1)S(1)} %get-tuple-element.4), kind=kOutput, calls=%fused_computation.60 | convolution fusion | flops 672399360 | bytes 23593000 | tf_op jit(solution)/shard_map/rtk,rtn->tkn/dot_general | solution.py:118
  468.1 25.2 %all-to-all-done.5 = bf16[64,64,512]{2,0,1:T(8,128)(2,1)} async-done(((bf16[64,64,512]{2,0,1:T(8,128)(2,1)}), bf16[64,64,512]{2,0,1:T(8,128)(2,1)}, u32[]{:S(2)}, u32[]{:S(2)}) %all-to-all-start.5) | async-done | bytes 4194336 | tf_op jit(solution)/shard_map/all_to_all | solution.py:107
  493.4 2.9 gather_fusion.14
  496.3 7.3 %fusion.31 = f32[64,20,512]{2,0,1:T(8,128)S(1)} fusion(bf16[1,20,512,512]{3,2,1,0:T(8,128)(2,1)} %param.15, bf16[20,64,512]{2,1,0:T(8,128)(2,1)S(1)} %gather_fusion.14, pred[20]{0:T(512)(128)(4,1)S(1)} %get-tuple-element.4), kind=kOutput, calls=%fused_computation.49 | convolution fusion | flops 671744000 | bytes 14417940 | tf_op jit(solution)/shard_map/rtn,tkn->rtk/dot_general | solution.py:110
  503.6 2.6 fusion.93
  506.3 18.7 %fusion = bf16[1,20,512,512]{3,2,1,0:T(8,128)(2,1)} fusion(f32[20,512,512]{2,1,0:T(8,128)} %fusion.56, f32[20,512,512]{2,1,0:T(8,128)} %fusion.60, pred[]{:T(512)S(6)} %and.95, pred[]{:T(512)S(6)} %and.94, pred[]{:T(512)S(6)} %and.84, bf16[20,64,512]{2,1,0:T(8,128)(2,1)S(1)} %copy-done, pred[20]{0:T(512)(128)(4,1)S(1)} %compare_and_fusion.2, ...), kind=kOutput, calls=%fused_computation.16 | convolution fusion | flops 703856640 | bytes 55050284 | tf_op jit(solution)/shard_map/rtk,rtn->tkn/dot_general | solution.py:118
  (116 shorter events, 13.1 us)
Async XLA Ops:
  2.8 2.0 copy-start.10
  3.2 163.3 %copy-start.21 = (s32[64]{0:T(128)}, s32[64]{0:T(128)S(1)}, u32[]{:S(2)}) copy-start(s32[64]{0:T(128)S(1)} %get-tuple-element.12) | copy-start | bytes 772
  3.8 170.6 %copy-start.13 = (s32[1024]{0:T(1024)}, s32[1024]{0:T(1024)S(1)}, u32[]{:S(2)}) copy-start(s32[1024]{0:T(1024)S(1)} %pad_clamp_fusion.3) | copy-start | bytes 12292
  18.3 63.2 %all-to-all-start = ((bf16[64,64,512]{2,0,1:T(8,128)(2,1)}), bf16[64,64,512]{2,0,1:T(8,128)(2,1)}, u32[]{:S(2)}, u32[]{:S(2)}) async-start(bf16[64,64,512]{2,0,1:T(8,128)(2,1)} %bitcast_select_fusion.5), calls=%async_computation | async-start | bytes 8388608 | tf_op jit(solution)/shard_map/all_to_all | solution.py:69
  30.6 224.4 %copy-start.14 = (pred[64]{0:T(512)(128)(4,1)}, pred[64]{0:T(512)(128)(4,1)S(1)}, u32[]{:S(2)}) copy-start(pred[64]{0:T(512)(128)(4,1)S(1)} %reduce_or.19) | copy-start | bytes 196
  30.6 59.5 %copy-start.8 = (bf16[128,1024]{1,0:T(8,128)(2,1)S(1)}, bf16[128,1024]{1,0:T(8,128)(2,1)}, u32[]{:S(2)}) copy-start(bf16[128,1024]{1,0:T(8,128)(2,1)} %param.14) | copy-start | bytes 786436
  86.1 4.0 collective-permute-start
  169.6 4.7 collective-permute-start.1
  174.4 6.6 %copy-start.1 = (bf16[2,64,1024]{2,1,0:T(8,128)(2,1)}, bf16[2,64,1024]{2,1,0:T(8,128)(2,1)S(1)}, u32[]{:S(2)}) copy-start(bf16[2,64,1024]{2,1,0:T(8,128)(2,1)S(1)} %get-tuple-element.8) | copy-start | bytes 786436
  187.9 6.4 %copy-start.12 = (f32[1024]{0:T(1024)S(1)}, f32[1024]{0:T(1024)}, u32[]{:S(2)}) copy-start(f32[1024]{0:T(1024)} %param.18) | copy-start | bytes 12292
  187.9 6.5 %copy-start.11 = (f32[1024]{0:T(1024)S(1)}, f32[1024]{0:T(1024)}, u32[]{:S(2)}) copy-start(f32[1024]{0:T(1024)} %param.19) | copy-start | bytes 12292
  187.9 6.8 %copy-start.9 = (f32[64,2,512]{2,1,0:T(2,128)S(1)}, f32[64,2,512]{2,1,0:T(2,128)}, u32[]{:S(2)}) copy-start(f32[64,2,512]{2,1,0:T(2,128)} %get-tuple-element.22) | copy-start | bytes 786436
  187.9 59.1 %all-to-all-start.2 = ((bf16[64,64,512]{2,0,1:T(8,128)(2,1)}), bf16[64,64,512]{2,0,1:T(8,128)(2,1)}, u32[]{:S(2)}, u32[]{:S(2)}) async-start(bf16[64,64,512]{2,0,1:T(8,128)(2,1)} %bitcast_select_fusion.3), calls=%async_computation.2 | async-start | bytes 8388608 | tf_op jit(solution)/shard_map/all_to_all | solution.py:69
  194.3 52.7 %copy-start.22 = (s32[64]{0:T(128)S(1)}, s32[64]{0:T(128)}, u32[]{:S(2)}) copy-start(s32[64]{0:T(128)} %copy-done.21) | copy-start | bytes 772
  194.4 147.2 %copy-start.19 = (s32[1024]{0:T(1024)}, s32[1024]{0:T(1024)S(1)}, u32[]{:S(2)}) copy-start(s32[1024]{0:T(1024)S(1)} %pad_clamp_fusion.1) | copy-start | bytes 12292
  252.1 2.8 copy-start.17
  259.0 63.4 %all-to-all-start.3 = ((bf16[64,64,512]{2,0,1:T(8,128)(2,1)}), bf16[64,64,512]{2,0,1:T(8,128)(2,1)}, u32[]{:S(2)}, u32[]{:S(2)}) async-start(bf16[64,64,512]{2,0,1:T(8,128)(2,1)} %bitcast_select_fusion.2), calls=%async_computation.3 | async-start | bytes 8388608 | tf_op jit(solution)/shard_map/all_to_all | solution.py:107
  274.2 58.3 %copy-start.20 = (s32[1024]{0:T(1024)}, s32[1024]{0:T(1024)S(1)}, u32[]{:S(2)}) copy-start(s32[1024]{0:T(1024)S(1)} %pad_clamp_fusion) | copy-start | bytes 12292
  325.2 7.3 %copy-start.23 = (s32[1,20]{1,0:T(1,128)S(1)}, s32[1,20]{1,0:T(1,128)}, u32[]{:S(2)}) copy-start(s32[1,20]{1,0:T(1,128)} %param.17) | copy-start | bytes 244
  335.1 9.3 %copy-start.3 = (bf16[2,64,512]{2,0,1:T(2,128)(2,1)}, bf16[2,64,512]{2,0,1:T(2,128)(2,1)S(1)}, u32[]{:S(2)}) copy-start(bf16[2,64,512]{2,0,1:T(2,128)(2,1)S(1)} %fusion.84) | copy-start | bytes 393220
  335.1 6.3 %collective-permute-start.2 = (bf16[64,1024]{1,0:T(8,128)(2,1)S(1)}, bf16[64,1024]{1,0:T(8,128)(2,1)S(1)}, u32[]{:S(2)}, u32[]{:S(2)}) collective-permute-start(bf16[64,1024]{1,0:T(8,128)(2,1)S(1)} %bitcast.230), channel_id=1, source_target_pairs={{64,0},{65,1},{66,2},{67,3},{68,4},{69,5},{70,6},{71,7},{72,8},{73... | collective-permute-start | bytes 393224 | tf_op jit(solution)/shard_map/ppermute | solution.py:14
  341.6 2.8 copy-start.15
  410.7 7.3 %copy-start.24 = (s32[1,20]{1,0:T(1,128)S(1)}, s32[1,20]{1,0:T(1,128)}, u32[]{:S(2)}) copy-start(s32[1,20]{1,0:T(1,128)} %param.17) | copy-start | bytes 244
  420.5 0.7 copy-start.5
  421.2 5.7 %collective-permute-start.3 = (bf16[64,1024]{1,0:T(8,128)(2,1)S(1)}, bf16[64,1024]{1,0:T(8,128)(2,1)S(1)}, u32[]{:S(2)}, u32[]{:S(2)}) collective-permute-start(bf16[64,1024]{1,0:T(8,128)(2,1)S(1)} %bitcast.229), channel_id=1, source_target_pairs={{64,0},{65,1},{66,2},{67,3},{68,4},{69,5},{70,6},{71,7},{72,8},{73... | collective-permute-start | bytes 393224 | tf_op jit(solution)/shard_map/ppermute | solution.py:14
  427.0 3.0 copy-start.16
  427.1 3.0 copy-start.18
  434.0 6.1 %copy-start.2 = (bf16[2,64,1024]{2,1,0:T(8,128)(2,1)S(1)}, bf16[2,64,1024]{2,1,0:T(8,128)(2,1)}, u32[]{:S(2)}) copy-start(bf16[2,64,1024]{2,1,0:T(8,128)(2,1)} %copy-done.1) | copy-start | bytes 786436
  434.0 59.3 %all-to-all-start.5 = ((bf16[64,64,512]{2,0,1:T(8,128)(2,1)}), bf16[64,64,512]{2,0,1:T(8,128)(2,1)}, u32[]{:S(2)}, u32[]{:S(2)}) async-start(bf16[64,64,512]{2,0,1:T(8,128)(2,1)} %bitcast_select_fusion), calls=%async_computation.5 | async-start | bytes 8388608 | tf_op jit(solution)/shard_map/all_to_all | solution.py:107
  442.5 4.0 copy-start.4
  446.7 10.7 %copy-start.6 = (bf16[2,64,512]{2,0,1:T(2,128)(2,1)S(1)}, bf16[2,64,512]{2,0,1:T(2,128)(2,1)}, u32[]{:S(2)}) copy-start(bf16[2,64,512]{2,0,1:T(2,128)(2,1)} %copy-done.5) | copy-start | bytes 393220
  496.3 7.3 %copy-start.25 = (s32[1,20]{1,0:T(1,128)S(1)}, s32[1,20]{1,0:T(1,128)}, u32[]{:S(2)}) copy-start(s32[1,20]{1,0:T(1,128)} %param.17) | copy-start | bytes 244
  503.6 2.7 copy-start
  506.3 18.7 %copy-start.7 = (bf16[2,64,1024]{2,1,0:T(8,128)(2,1)}, bf16[2,64,1024]{2,1,0:T(8,128)(2,1)S(1)}, u32[]{:S(2)}) copy-start(bf16[2,64,1024]{2,1,0:T(8,128)(2,1)S(1)} %select_dynamic-update-slice_fusion.2) | copy-start | bytes 786436
where the time goes:
time: 536 us; the launch traced here: 525 us
  waiting for transfers between devices  184 us (34%)
  blocking collectives  125 us (23%)
  matrix products  99.5 us (19%)
  starting transfers between devices  52 us (10%)
  local copies, waits for them, and re-layouts  36.2 us (7%)
  other arithmetic  26.9 us (5%)
    all_to_all x2, waiting for transfers between devices, on_device(): lax.all_to_all(forward_outgoing, 'blk', split_axis=1, concat_axis=1, tile...  103 us
    all_to_all x2, waiting for transfers between devices, on_device(): lax.all_to_all(outgoing, 'blk', split_axis=1, concat_axis=1, tiled=True)  73.4 us
    all_to_all x1, blocking collectives, on_device(): lax.all_to_all(forward_outgoing, 'blk', split_axis=1, concat_axis=1, tile...  64.2 us
    all_to_all x1, blocking collectives, on_device(): lax.all_to_all(outgoing, 'blk', split_axis=1, concat_axis=1, tiled=True)  60.6 us
    dot_general x3, matrix products, on_device(): jnp.einsum('rtk,rtn->tkn', pick_columns(inputs), tile_grads, preferred_el...  40 us
    dot_general x3, matrix products, on_device(): jnp.einsum('rtn,tkn->rtk', tile_grads, my_tiles, preferred_element_type=j...  21.8 us
    all_to_all x2, starting transfers between devices, on_device(): lax.all_to_all(outgoing, 'blk', split_axis=1, concat_axis=1, tiled=True)  20.6 us
    all_to_all x2, starting transfers between devices, on_device(): lax.all_to_all(forward_outgoing, 'blk', split_axis=1, concat_axis=1, tile...  18.6 us
  transfers between devices with their start and end apart: 8, of which 8 were waited for; matrix products, arithmetic and copies ran while one was open for 6% of the time, Pallas kernels for 0%

commit v1 on v0

v1 whole, which is shorter than its diff:
```python
import functools
import math

import jax
import jax.numpy as jnp
from jax import lax
from jax.experimental import pallas as pl
from jax.experimental.pallas import tpu as pltpu
from jax.sharding import PartitionSpec as P

SLICE = 8
VMEM_LIMIT = 48 * 1024 * 1024


def params(**kw):
    return pltpu.CompilerParams(vmem_limit_bytes=VMEM_LIMIT, **kw)


def products_body(cols, x, tiles, out, *, first, width):
    step = pl.program_id(0)
    parts = []
    for u in range(2):
        col = cols[first + 2 * step + u]
        picked = x[:, pl.ds(pl.multiple_of(col * width, width), width)]
        product = jnp.dot(picked, tiles[u], preferred_element_type=jnp.float32)
        parts.append(product.T.reshape(width // SLICE, SLICE, x.shape[0]))
    both = jnp.concatenate(parts, axis=1).astype(jnp.bfloat16)
    out[:, pl.ds(pl.multiple_of(2 * SLICE * step, 2 * SLICE), 2 * SLICE), :] = both


def products(cols, x, tiles, first, count):
    width = tiles.shape[1]
    scen = x.shape[0]
    return pl.pallas_call(
        functools.partial(products_body, first=first, width=width),
        grid=(count // 2,),
        in_specs=[
            pl.BlockSpec(memory_space=pltpu.SMEM),
            pl.BlockSpec(x.shape, lambda g: (0, 0)),
            pl.BlockSpec((2, width, width), lambda g: (g + first // 2, 0, 0)),
        ],
        out_specs=pl.BlockSpec((width // SLICE, count * SLICE, scen), lambda g: (0, 0, 0)),
        out_shape=jax.ShapeDtypeStruct((width // SLICE, count * SLICE, scen), jnp.bfloat16),
        compiler_params=params(),
        name="products",
    )(cols, x, tiles)


def add_up_body(idx, data, out, *, count):
    out[...] = jnp.zeros_like(out)

    @pl.loop(0, data.shape[0])
    def _(i):
        values = data[i].astype(jnp.float32)
        places = [idx[i * count + t] for t in range(count)]
        sums = [
            out[places[t]] + values[t * SLICE : (t + 1) * SLICE] for t in range(count)
        ]
        for t in range(count):
            out[places[t]] = sums[t]


def add_up(idx, data, blocks):
    count = data.shape[1] // SLICE
    return pl.pallas_call(
        functools.partial(add_up_body, count=count),
        in_specs=[pl.BlockSpec(memory_space=pltpu.SMEM), pl.BlockSpec(memory_space=pltpu.VMEM)],
        out_specs=pl.BlockSpec(memory_space=pltpu.VMEM),
        out_shape=jax.ShapeDtypeStruct((blocks, SLICE, data.shape[2]), jnp.float32),
        compiler_params=params(),
        name="add_up",
    )(idx, data)


def hand_out(idx, held, out, count):
    @pl.loop(0, out.shape[0])
    def _(i):
        for t in range(0, count, 2):
            pair = [held[idx[i * count + t]], held[idx[i * count + t + 1]]]
            rows = jnp.concatenate(pair, axis=0).astype(jnp.bfloat16)
            out[i, t * SLICE : (t + 2) * SLICE, :] = rows


def value_and_hand_out_body(idx, mine, other, notional, strike, out, held, *, count, weight):
    @pl.loop(0, held.shape[0], step=8)
    def _(b):
        for k in range(8):
            moneyness = mine[b + k] + other[b + k]
            held[b + k] = notional[b + k] * jax.nn.sigmoid(moneyness - strike[b + k]) * weight

    hand_out(idx, held, out, count)


def value_and_hand_out(idx, mine, other, notional, strike, shards, count, weight):
    scen = mine.shape[2]
    vmem = pl.BlockSpec(memory_space=pltpu.VMEM)
    return pl.pallas_call(
        functools.partial(value_and_hand_out_body, count=count, weight=weight),
        in_specs=[pl.BlockSpec(memory_space=pltpu.SMEM), vmem, vmem, vmem, vmem],
        out_specs=vmem,
        out_shape=jax.ShapeDtypeStruct((shards, count * SLICE, scen), jnp.bfloat16),
        scratch_shapes=[pltpu.VMEM(mine.shape, jnp.float32)],
        compiler_params=params(),
        name="value_and_hand_out",
    )(idx, mine, other, notional, strike)


def only_hand_out_body(idx, blocks, out, held, *, count):
    held[...] = blocks[...].astype(jnp.float32).reshape(held.shape)
    hand_out(idx, held, out, count)


def only_hand_out(idx, blocks, shards, count):
    scen = blocks.shape[2]
    vmem = pl.BlockSpec(memory_space=pltpu.VMEM)
    held = blocks.shape[0] * blocks.shape[1] // SLICE
    return pl.pallas_call(
        functools.partial(only_hand_out_body, count=count),
        in_specs=[pl.BlockSpec(memory_space=pltpu.SMEM), vmem],
        out_specs=vmem,
        out_shape=jax.ShapeDtypeStruct((shards, count * SLICE, scen), jnp.bfloat16),
        scratch_shapes=[pltpu.VMEM((held, SLICE, scen), jnp.float32)],
        compiler_params=params(),
        name="hand_out",
    )(idx, blocks)


def tile_grad_pair(grads, pair):
    rows = grads[:, pl.ds(pl.multiple_of(pair * 2 * SLICE, 2 * SLICE), 2 * SLICE), :]
    rows = rows.astype(jnp.float32)
    width = rows.shape[0] * SLICE
    return [
        rows[:, u * SLICE : (u + 1) * SLICE, :].reshape(width, -1).astype(jnp.bfloat16)
        for u in range(2)
    ]


def first_backward_body(cols, low, high, tiles, out, total, *, half):
    step = pl.program_id(0)

    @pl.when(step == 0)
    def _():
        total[...] = jnp.zeros_like(total)

    def go(grads, pair):
        for u, grad in enumerate(tile_grad_pair(grads, pair)):
            total[cols[2 * step + u]] += jnp.dot(tiles[u], grad, preferred_element_type=jnp.float32)

    @pl.when(step < half // 2)
    def _():
        go(low, step)

    @pl.when(step >= half // 2)
    def _():
        go(high, step - half // 2)

    @pl.when(step == pl.num_programs(0) - 1)
    def _():
        out[...] = total[...].astype(jnp.bfloat16)


def first_backward(cols, low, high, tiles, blocks_dev):
    slots, width, _ = tiles.shape
    scen = low.shape[2]
    whole = pl.BlockSpec(low.shape, lambda g: (0, 0, 0))
    return pl.pallas_call(
        functools.partial(first_backward_body, half=slots // 2),
        grid=(slots // 2,),
        in_specs=[
            pl.BlockSpec(memory_space=pltpu.SMEM),
            whole,
            whole,
            pl.BlockSpec((2, width, width), lambda g: (g, 0, 0)),
        ],
        out_specs=pl.BlockSpec((blocks_dev, width, scen), lambda g: (0, 0, 0)),
        out_shape=jax.ShapeDtypeStruct((blocks_dev, width, scen), jnp.bfloat16),
        scratch_shapes=[pltpu.VMEM((blocks_dev, width, scen), jnp.float32)],
        compiler_params=params(),
        name="first_backward",
    )(cols, low, high, tiles)


def last_backward_body(
    meta, low0, high0, low1, high1, inputs, tiles, sens, adjoint, total, *, half
):
    step = pl.program_id(0)
    section = meta[2 * half]

    @pl.when(step == 0)
    def _():
        total[...] = jnp.zeros_like(total)

    def go(grads, pair):
        for u, grad in enumerate(tile_grad_pair(grads, pair)):
            col = meta[2 * step + u]
            total[col] += jnp.dot(tiles[u], grad, preferred_element_type=jnp.float32)
            sens[u] = lax.dot_general(
                inputs[col], grad, (((1,), (1,)), ((), ())), preferred_element_type=jnp.float32
            ).astype(jnp.bfloat16)

    for wanted, low, high in ((0, low0, high0), (1, low1, high1)):

        @pl.when((section == wanted) & (step < half // 2))
        def _(low=low):
            go(low, step)

        @pl.when((section == wanted) & (step >= half // 2))
        def _(high=high):
            go(high, step - half // 2)

    @pl.when(step == pl.num_programs(0) - 1)
    def _():
        width = total.shape[1]
        for c in range(total.shape[0]):
            adjoint[:, c * width : (c + 1) * width] = total[c].T.astype(jnp.bfloat16)


def last_backward(meta, low0, high0, low1, high1, inputs, tiles):
    slots, width, _ = tiles.shape
    scen = low0.shape[2]
    blocks_dev = inputs.shape[0]
    whole = pl.BlockSpec(low0.shape, lambda g: (0, 0, 0), pipeline_mode=pl.Buffered(1))
    pair = pl.BlockSpec((2, width, width), lambda g: (g, 0, 0))
    return pl.pallas_call(
        functools.partial(last_backward_body, half=slots // 2),
        grid=(slots // 2,),
        in_specs=[
            pl.BlockSpec(memory_space=pltpu.SMEM),
            whole,
            whole,
            whole,
            whole,
            pl.BlockSpec(inputs.shape, lambda g: (0, 0, 0)),
            pair,
        ],
        out_specs=[pair, pl.BlockSpec((scen, blocks_dev * width), lambda g: (0, 0))],
        out_shape=[
            jax.ShapeDtypeStruct(tiles.shape, jnp.bfloat16),
            jax.ShapeDtypeStruct((scen, blocks_dev * width), jnp.bfloat16),
        ],
        scratch_shapes=[pltpu.VMEM((blocks_dev, width, scen), jnp.float32)],
        compiler_params=params(),
        name="last_backward",
    )(meta, low0, high0, low1, high1, inputs, tiles)


def three_terms(values):
    terms = []
    for _ in range(3):
        term = lax.reduce_precision(values, 8, 7)
        terms.append(term)
        values = values - term
    return jnp.stack(terms)


def exchange(block):
    return lax.all_to_all(block, "blk", split_axis=0, concat_axis=0, tiled=True)


def on_device(normals, section_tile_list, tile_output_block, tile_col, notional, strike):
    shards = lax.axis_size("blk")
    core = lax.axis_index("phase")
    tiles = section_tile_list[0]
    slots, width, _ = tiles.shape
    half = slots // 2
    scen, local_width = normals.shape
    blocks_dev = local_width // width
    blocks = shards * blocks_dev
    cols = tile_col[0]
    weight = 1.0 / math.sqrt(scen)

    def of_core(zero, one):
        return jnp.where(core == 0, zero, one)

    def send(block, source):
        return lax.ppermute(block, "phase", [(source, 1 - source)])

    def swap(block):
        return lax.ppermute(block, "phase", [(0, 1), (1, 0)])

    my_rows = tile_output_block[0]
    other_rows = swap(my_rows)
    split_rows = [
        of_core(r.reshape(shards, slots)[:, :half], r.reshape(shards, slots)[:, half:]).reshape(-1)
        for r in (of_core(my_rows, other_rows), of_core(other_rows, my_rows))
    ]

    sent = send(products(cols, normals, tiles, half, half), 0)
    kept = products(cols, normals, tiles, 0, half)
    arrived = exchange(of_core(kept, sent))
    part = add_up(split_rows[0], arrived, blocks)
    shock_slices = (part + swap(part)).astype(jnp.bfloat16)

    scales = jnp.stack([three_terms(notional), three_terms(strike)])
    scales = scales.reshape(6, blocks_dev, shards, SLICE).transpose(2, 0, 1, 3)
    scales = scales.reshape(shards, 1, 6 * blocks_dev * SLICE).astype(jnp.bfloat16)
    scales = jnp.pad(scales, ((0, 0), (0, SLICE - 1), (0, scen - scales.shape[2])))
    shock_rows = shock_slices.reshape(shards, blocks_dev * SLICE, scen)
    arrived = exchange(jnp.concatenate([shock_rows, scales], axis=1))
    shocks = arrived[:, : blocks_dev * SLICE].reshape(shards, blocks_dev, SLICE, scen)
    shocks = shocks.transpose(1, 0, 2, 3).reshape(blocks_dev, width, scen)
    shocks_natural = shocks.transpose(2, 0, 1).reshape(scen, local_width)
    scales = arrived[:, blocks_dev * SLICE, : 6 * blocks_dev * SLICE].astype(jnp.float32)
    scales = scales.reshape(shards, 2, 3, blocks_dev, SLICE)
    scales = (scales[:, :, 0] + scales[:, :, 1]) + scales[:, :, 2]
    scales = scales.transpose(1, 0, 2, 3).reshape(2, blocks, SLICE, 1)

    sent = send(products(cols, shocks_natural, tiles, 0, half), 1)
    kept = products(cols, shocks_natural, tiles, half, half)
    arrived = exchange(of_core(sent, kept))
    part = add_up(split_rows[1], arrived, blocks)
    outgoing = value_and_hand_out(
        split_rows[1], part, swap(part), scales[0], scales[1], shards, half, weight
    )

    high1 = exchange(outgoing)
    low1 = send(high1, 0)
    shock_grad = first_backward(cols, low1, high1, tiles, blocks_dev)

    shock_grad = of_core(send(shock_grad, 1), shock_grad)
    shock_grad = shock_grad.reshape(blocks_dev, shards, SLICE, scen).transpose(1, 0, 2, 3)
    arrived = exchange(shock_grad.reshape(shards, blocks_dev * SLICE, scen))
    low0 = exchange(only_hand_out(split_rows[0], arrived, shards, half))
    high0 = send(low0, 1)

    normals_held = normals.reshape(scen, blocks_dev, width).transpose(1, 2, 0)
    meta = jnp.concatenate([cols, core[None].astype(jnp.int32)])
    sens, adjoint = last_backward(
        meta, low0, high0, low1, high1, of_core(normals_held, shocks), tiles
    )
    return sens[None], adjoint[None]


def solution(mesh):
    return jax.shard_map(
        on_device,
        mesh=mesh,
        in_specs=(
            P(None, "blk"),
            P("phase", "blk", None, None),
            P("phase", None),
            P("phase", "blk"),
            P("blk"),
            P("blk"),
        ),
        out_specs=(P("phase", "blk", None, None), P("phase", None, "blk")),
        check_vma=False,
    )
```

time: 536 us -> 226 us (0.42); the launches traced: 525 us -> 225 us
  waiting for transfers between devices: 184 us -> 46.9 us
  matrix products: 99.5 us -> 0 us
  Pallas kernels: 0 us -> 51.9 us
  blocking collectives: 125 us -> 76.8 us
  local copies, waits for them, and re-layouts: 36.2 us -> 6.23 us
  other arithmetic: 26.9 us -> 4.33 us
  starting transfers between devices: 52 us -> 37.5 us
    all_to_all x4 -> x2, waiting for transfers between devices: 176 us -> 37.8 us  [exchange(): return lax.all_to_all(block, 'blk', split_axis=0, concat_axis=0, tiled=True)]
    dot_general x15 -> x0, matrix products: 99.5 us -> none  [the longest x3 40 us: on_device(): jnp.einsum('rtk,rtn->tkn', pick_columns(inputs), tile_grads, preferred_el...]
    pallas_call x0 -> x10, Pallas kernels: none -> 51.9 us  [the longest x4 19.7 us: products(): pl.pallas_call(functools.partial(products_body, first=first, width=width)...]
    all_to_all x2 -> x4, blocking collectives: 125 us -> 76.8 us  [exchange(): return lax.all_to_all(block, 'blk', split_axis=0, concat_axis=0, tiled=True)]
    gather x15 -> x0, local copies, waits for them, and re-layouts: 33.6 us -> none  [the longest x3 8.69 us: on_device(): tile_grads = jnp.take(returned, owners, axis=1)]
    all_to_all x4 -> x2, starting transfers between devices: 39.3 us -> 16.8 us  [exchange(): return lax.all_to_all(block, 'blk', split_axis=0, concat_axis=0, tiled=True)]
    select_n x19 -> x6, other arithmetic: 23.7 us -> 3.97 us  [of_core(): return jnp.where(core == 0, zero, one)]
    ppermute x4 -> x8, starting transfers between devices: 12.7 us -> 20.7 us  [the longest x5 15.5 us: send(): return lax.ppermute(block, 'phase', [(source, 1 - source)])]
  transfers between devices with their start and end apart: 8 -> 10, of which waited for: 8 -> 7; matrix products, arithmetic and copies ran while one was open for 6% -> 2% of each run, Pallas kernels for 0% -> 4%
where the time goes in v1:
time: 226 us; the launch traced here: 225 us
  blocking collectives  76.8 us (34%)
  Pallas kernels  51.9 us (23%)
  waiting for transfers between devices  46.9 us (21%)
  starting transfers between devices  37.5 us (17%)
  local copies, waits for them, and re-layouts  6.23 us (3%)
  other arithmetic  4.33 us (2%)
    all_to_all x4, blocking collectives, exchange(): return lax.all_to_all(block, 'blk', split_axis=0, concat_axis=0, tiled=True)  76.8 us
    all_to_all x2, waiting for transfers between devices, exchange(): return lax.all_to_all(block, 'blk', split_axis=0, concat_axis=0, tiled=True)  37.8 us
    pallas_call x4, Pallas kernels, products(): pl.pallas_call(functools.partial(products_body, first=first, width=width)...  19.7 us
    all_to_all x2, starting transfers between devices, exchange(): return lax.all_to_all(block, 'blk', split_axis=0, concat_axis=0, tiled=True)  16.8 us
    ppermute x5, starting transfers between devices, send(): return lax.ppermute(block, 'phase', [(source, 1 - source)])  15.5 us
    pallas_call x1, Pallas kernels, last_backward(): pl.pallas_call(functools.partial(last_backward_body, half=slots // 2), gr...  14.2 us
    pallas_call x1, Pallas kernels, first_backward(): pl.pallas_call(functools.partial(first_backward_body, half=slots // 2), g...  9.8 us
    ppermute x5, waiting for transfers between devices, send(): return lax.ppermute(block, 'phase', [(source, 1 - source)])  7.45 us
  transfers between devices with their start and end apart: 10, of which 7 were waited for; matrix products, arithmetic and copies ran while one was open for 2% of the time, Pallas kernels for 4%

profile of v1, /device:TPU:1, one launch (start us, length us, event | category | flops | bytes accessed | tf_op | source)
XLA Modules:
  0.0 224.8 jit_solution(12923471048500530181)
XLA Ops:
  0.6 0.9 copy-done.2
  1.6 0.7 copy-done.4
  2.2 4.9 %products.5 = bf16[64,80,128]{2,1,0:T(8,128)(2,1)S(1)} custom-call(s32[20]{0:T(128)S(1)} %bitcast.40, bf16[128,1024]{1,0:T(8,128)(2,1)S(1)} %copy-done.2, bf16[20,512,512]{2,1,0:T(8,128)(2,1)} %bitcast.46), custom_call_target="tpu_custom_call" | custom-call | tf_op jit(solution)/shard_map/products/pallas_call | solution.py:34
  7.2 1.3 collective-permute-start.1
  8.5 4.9 %products.4 = bf16[64,80,128]{2,1,0:T(8,128)(2,1)S(1)} custom-call(s32[20]{0:T(128)S(1)} %bitcast.41, bf16[128,1024]{1,0:T(8,128)(2,1)S(1)} %copy-done.2, bf16[20,512,512]{2,1,0:T(8,128)(2,1)} %bitcast.47), custom_call_target="tpu_custom_call" | custom-call | tf_op jit(solution)/shard_map/products/pallas_call | solution.py:34
  13.4 2.5 %broadcast_select_fusion.1 = bf16[64,80,128]{2,1,0:T(8,128)(2,1)} fusion(bf16[64,80,128]{2,1,0:T(8,128)(2,1)S(1)} %products.4, bf16[64,80,128]{2,1,0:T(8,128)(2,1)} %collective-permute-done.1, pred[]{:T(512)S(6)} %eq.2), kind=kLoop, calls=%fused_computation.1 | loop fusion | flops 655360 | bytes 3932161 | tf_op jit(solution)/shard_map/jit(_where)/select_n | solution.py:273
  15.9 12.1 %all-to-all-start = ((bf16[64,80,128]{2,1,0:T(8,128)(2,1)}), bf16[64,80,128]{2,1,0:T(8,128)(2,1)S(1)}, u32[]{:S(2)}, u32[]{:S(2)}) async-start(bf16[64,80,128]{2,1,0:T(8,128)(2,1)} %broadcast_select_fusion.1), calls=%async_computation | async-start | bytes 2621440 | tf_op jit(solution)/shard_map/all_to_all | solution.py:257
  28.1 1.2 collective-permute-start
  29.3 0.8 collective-permute-done
  30.1 0.1 reshape.66
  30.3 0.1 reshape.67.idx
  30.5 16.6 %all-to-all-done.data = bf16[64,80,128]{2,1,0:T(8,128)(2,1)S(1)} async-done(((bf16[64,80,128]{2,1,0:T(8,128)(2,1)}), bf16[64,80,128]{2,1,0:T(8,128)(2,1)S(1)}, u32[]{:S(2)}, u32[]{:S(2)}) %all-to-all-start) | async-done | bytes 1310752 | tf_op jit(solution)/shard_map/all_to_all | solution.py:257
  47.1 1.8 add_up.2
  48.9 3.4 %collective-permute-start.2 = (f32[128,8,128]{2,1,0:T(8,128)S(1)}, f32[128,8,128]{2,1,0:T(8,128)S(1)}, u32[]{:S(2)}, u32[]{:S(2)}) collective-permute-start(f32[128,8,128]{2,1,0:T(8,128)S(1)} %add_up.2), channel_id=1, source_target_pairs={{0,64},{64,0},{1,65},{65,1},{2,66},{66,2},{3,67},{67,3},{4,68},{68... | collective-permute-start | bytes 1572872 | tf_op jit(solution)/shard_map/ppermute | solution.py:279
  52.5 0.3 convert_element_type.31
  52.7 0.1 copy.38
  52.8 0.1 copy.52
  53.0 0.9 collective-permute-done.2
  54.0 15.0 %all_to_all.30 = bf16[64,24,128]{2,1,0:T(8,128)(2,1)S(1)} all-to-all(bf16[64,24,128]{2,1,0:T(8,128)(2,1)S(1)} %fusion.1), channel_id=1, replica_groups=mesh['phase'=2,'blk'=64] {'blk'}, dimensions={0} | all-to-all | bytes 786432 | tf_op jit(solution)/shard_map/all_to_all | solution.py:257
  69.0 0.1 copy.41.x
  69.2 4.9 %products.6 = bf16[64,80,128]{2,1,0:T(8,128)(2,1)S(1)} custom-call(s32[20]{0:T(128)S(1)} %bitcast.42, bf16[128,1024]{1,0:T(8,128)(2,1)S(1)} %copy.41.x, bf16[20,512,512]{2,1,0:T(8,128)(2,1)} %bitcast.48), custom_call_target="tpu_custom_call" | custom-call | tf_op jit(solution)/shard_map/products/pallas_call | solution.py:34
  74.1 3.9 %collective-permute-start.3 = (bf16[64,80,128]{2,1,0:T(8,128)(2,1)S(1)}, bf16[64,80,128]{2,1,0:T(8,128)(2,1)S(1)}, u32[]{:S(2)}, u32[]{:S(2)}) collective-permute-start(bf16[64,80,128]{2,1,0:T(8,128)(2,1)S(1)} %products.6), channel_id=1, source_target_pairs={{64,0},{65,1},{66,2},{67,3},{68,4},{69,5},{70,6},{71,7},{72,8},{73... | collective-permute-start | bytes 3932168 | tf_op jit(solution)/shard_map/ppermute | solution.py:276
  78.1 4.9 %products.7 = bf16[64,80,128]{2,1,0:T(8,128)(2,1)S(1)} custom-call(s32[20]{0:T(128)S(1)} %bitcast.43, bf16[128,1024]{1,0:T(8,128)(2,1)S(1)} %copy.41.x, bf16[20,512,512]{2,1,0:T(8,128)(2,1)} %bitcast.49), custom_call_target="tpu_custom_call" | custom-call | tf_op jit(solution)/shard_map/products/pallas_call | solution.py:34
  83.0 1.2 broadcast_select_fusion
  84.2 4.7 %all-to-all-start.2 = ((bf16[64,80,128]{2,1,0:T(8,128)(2,1)}), bf16[64,80,128]{2,1,0:T(8,128)(2,1)S(1)}, u32[]{:S(2)}, u32[]{:S(2)}) async-start(bf16[64,80,128]{2,1,0:T(8,128)(2,1)} %broadcast_select_fusion), calls=%async_computation.2 | async-start | bytes 2621440 | tf_op jit(solution)/shard_map/all_to_all | solution.py:257
  89.1 0.1 reshape.69.idx
  89.3 21.2 %all-to-all-done.2.data = bf16[64,80,128]{2,1,0:T(8,128)(2,1)S(1)} async-done(((bf16[64,80,128]{2,1,0:T(8,128)(2,1)}), bf16[64,80,128]{2,1,0:T(8,128)(2,1)S(1)}, u32[]{:S(2)}, u32[]{:S(2)}) %all-to-all-start.2) | async-done | bytes 1310752 | tf_op jit(solution)/shard_map/all_to_all | solution.py:257
  110.4 1.8 add_up.3.mine
  112.2 0.6 collective-permute-start.4
  112.9 0.1 copy.46
  113.0 0.1 copy.45
  113.2 0.8 copy.47.notional
  114.0 0.8 copy.48.strike
  114.8 3.0 %value_and_hand_out.1 = bf16[64,80,128]{2,1,0:T(8,128)(2,1)S(1)} custom-call(s32[640]{0:T(1024)S(1)} %reshape.69.idx, f32[128,8,128]{2,1,0:T(8,128)S(1)} %add_up.3.mine, f32[128,8,128]{2,1,0:T(8,128)S(1)} %collective-permute-done.4.other, f32[128,8,1]{2,1,0:T(8,128)S(1)} %copy.47.notional, f32[128,8,1]{2,1,0:T(8,128)S(1)} %copy.48.strike), custom_call_target="tpu_custom_call" | custom-call | tf_op jit(solution)/shard_map/value_and_hand_out/pallas_call | solution.py:97
  117.8 24.9 %all_to_all.31.high.high1 = bf16[64,80,128]{2,1,0:T(8,128)(2,1)S(1)} all-to-all(bf16[64,80,128]{2,1,0:T(8,128)(2,1)S(1)} %value_and_hand_out.1), channel_id=1, replica_groups=mesh['phase'=2,'blk'=64] {'blk'}, dimensions={0} | all-to-all | bytes 2621440 | tf_op jit(solution)/shard_map/all_to_all | solution.py:257
  142.7 1.3 collective-permute-start.5
  144.0 4.9 %collective-permute-done.5.low.low1 = bf16[64,80,128]{2,1,0:T(8,128)(2,1)S(1)} collective-permute-done((bf16[64,80,128]{2,1,0:T(8,128)(2,1)S(1)}, bf16[64,80,128]{2,1,0:T(8,128)(2,1)S(1)}, u32[]{:S(2)}, u32[]{:S(2)}) %collective-permute-start.5) | collective-permute-done | bytes 1310752 | tf_op jit(solution)/shard_map/ppermute | solution.py:276
  149.0 9.8 %first_backward.1 = bf16[2,512,128]{2,1,0:T(8,128)(2,1)S(1)} custom-call(s32[20]{0:T(128)S(1)} %bitcast.44, bf16[64,80,128]{2,1,0:T(8,128)(2,1)S(1)} %collective-permute-done.5.low.low1, bf16[64,80,128]{2,1,0:T(8,128)(2,1)S(1)} %all_to_all.31.high.high1, bf16[20,512,512]{2,1,0:T(8,128)(2,1)} %bitcast.50), custom_call_target="tpu_custom_call" | custom-call | tf_op jit(solution)/shard_map/first_backward/pallas_call | solution.py:166
  158.8 2.1 collective-permute-start.6
  160.8 1.1 collective-permute-done.6
  162.0 13.6 %all_to_all.32.blocks = bf16[64,16,128]{2,1,0:T(8,128)(2,1)S(1)} all-to-all(bf16[64,16,128]{2,1,0:T(8,128)(2,1)S(1)} %copy_bitcast_fusion), channel_id=1, replica_groups=mesh['phase'=2,'blk'=64] {'blk'}, dimensions={0} | all-to-all | bytes 524288 | tf_op jit(solution)/shard_map/all_to_all | solution.py:257
  175.6 1.7 hand_out.1
  177.3 23.3 %all_to_all.33.low0 = bf16[64,80,128]{2,1,0:T(8,128)(2,1)S(1)} all-to-all(bf16[64,80,128]{2,1,0:T(8,128)(2,1)S(1)} %hand_out.1), channel_id=1, replica_groups=mesh['phase'=2,'blk'=64] {'blk'}, dimensions={0} | all-to-all | bytes 2621440 | tf_op jit(solution)/shard_map/all_to_all | solution.py:257
  200.7 6.9 %collective-permute-start.7 = (bf16[64,80,128]{2,1,0:T(8,128)(2,1)S(1)}, bf16[64,80,128]{2,1,0:T(8,128)(2,1)}, u32[]{:S(2)}, u32[]{:S(2)}) collective-permute-start(bf16[64,80,128]{2,1,0:T(8,128)(2,1)S(1)} %all_to_all.33.low0), channel_id=1, source_target_pairs={{64,0},{65,1},{66,2},{67,3},{68,4},{69,5},{70,6},{71,7},{72,8},{73... | collective-permute-start | bytes 3932168 | tf_op jit(solution)/shard_map/ppermute | solution.py:276
  207.6 0.2 copy.50
  207.9 1.4 collective-permute-done.7.high0
  209.3 1.3 copy-done.1
  210.6 14.2 %last_backward.1 = (bf16[20,512,512]{2,1,0:T(8,128)(2,1)}, bf16[128,1024]{1,0:T(8,128)(2,1)}) custom-call(s32[21]{0:T(128)S(1)} %pad_add_fusion.meta, bf16[64,80,128]{2,1,0:T(8,128)(2,1)S(1)} %all_to_all.33.low0, bf16[64,80,128]{2,1,0:T(8,128)(2,1)} %collective-permute-done.7.high0, bf16[64,80,128]{2,1,0:T(8,128)(2,1)S(1)} %copy-done.1, ...), custom_call_target="tpu_custom_call" | custom-call | tf_op jit(solution)/shard_map/last_backward/pallas_call | solution.py:224
  (45 shorter events, 0.9 us)
Async XLA Ops:
  0.6 1.0 copy-start.2
  1.6 0.7 copy-start.4
  7.2 6.2 %collective-permute-start.1 = (bf16[64,80,128]{2,1,0:T(8,128)(2,1)S(1)}, bf16[64,80,128]{2,1,0:T(8,128)(2,1)}, u32[]{:S(2)}, u32[]{:S(2)}) collective-permute-start(bf16[64,80,128]{2,1,0:T(8,128)(2,1)S(1)} %products.5), channel_id=1, source_target_pairs={{0,64},{1,65},{2,66},{3,67},{4,68},{5,69},{6,70},{7,71},{8,72},{9,... | collective-permute-start | bytes 3932168 | tf_op jit(solution)/shard_map/ppermute | solution.py:276
  15.9 12.1 %copy-start.6 = (s32[1,1280]{1,0:T(1,128)S(1)}, s32[1,1280]{1,0:T(1,128)}, u32[]{:S(2)}) copy-start(s32[1,1280]{1,0:T(1,128)} %param.8) | copy-start | bytes 15364
  15.9 31.2 %all-to-all-start = ((bf16[64,80,128]{2,1,0:T(8,128)(2,1)}), bf16[64,80,128]{2,1,0:T(8,128)(2,1)S(1)}, u32[]{:S(2)}, u32[]{:S(2)}) async-start(bf16[64,80,128]{2,1,0:T(8,128)(2,1)} %broadcast_select_fusion.1), calls=%async_computation | async-start | bytes 2621440 | tf_op jit(solution)/shard_map/all_to_all | solution.py:257
  28.0 24.3 %copy-start.7 = (f32[1024]{0:T(1024)S(1)}, f32[1024]{0:T(1024)}, u32[]{:S(2)}) copy-start(f32[1024]{0:T(1024)} %param.10) | copy-start | bytes 12292
  28.1 24.3 %copy-start.8 = (f32[1024]{0:T(1024)S(1)}, f32[1024]{0:T(1024)}, u32[]{:S(2)}) copy-start(f32[1024]{0:T(1024)} %param.11) | copy-start | bytes 12292
  28.1 2.0 collective-permute-start
  48.9 5.0 %collective-permute-start.2 = (f32[128,8,128]{2,1,0:T(8,128)S(1)}, f32[128,8,128]{2,1,0:T(8,128)S(1)}, u32[]{:S(2)}, u32[]{:S(2)}) collective-permute-start(f32[128,8,128]{2,1,0:T(8,128)S(1)} %add_up.2), channel_id=1, source_target_pairs={{0,64},{64,0},{1,65},{65,1},{2,66},{66,2},{3,67},{67,3},{4,68},{68... | collective-permute-start | bytes 1572872 | tf_op jit(solution)/shard_map/ppermute | solution.py:279
  54.0 15.2 %copy-start.5 = (s32[1,20]{1,0:T(1,128)S(1)}, s32[1,20]{1,0:T(1,128)}, u32[]{:S(2)}) copy-start(s32[1,20]{1,0:T(1,128)} %param.9) | copy-start | bytes 244
  74.1 8.9 %collective-permute-start.3 = (bf16[64,80,128]{2,1,0:T(8,128)(2,1)S(1)}, bf16[64,80,128]{2,1,0:T(8,128)(2,1)S(1)}, u32[]{:S(2)}, u32[]{:S(2)}) collective-permute-start(bf16[64,80,128]{2,1,0:T(8,128)(2,1)S(1)} %products.6), channel_id=1, source_target_pairs={{64,0},{65,1},{66,2},{67,3},{68,4},{69,5},{70,6},{71,7},{72,8},{73... | collective-permute-start | bytes 3932168 | tf_op jit(solution)/shard_map/ppermute | solution.py:276
  84.2 26.2 %all-to-all-start.2 = ((bf16[64,80,128]{2,1,0:T(8,128)(2,1)}), bf16[64,80,128]{2,1,0:T(8,128)(2,1)S(1)}, u32[]{:S(2)}, u32[]{:S(2)}) async-start(bf16[64,80,128]{2,1,0:T(8,128)(2,1)} %broadcast_select_fusion), calls=%async_computation.2 | async-start | bytes 2621440 | tf_op jit(solution)/shard_map/all_to_all | solution.py:257
  112.2 2.6 %collective-permute-start.4 = (f32[128,8,128]{2,1,0:T(8,128)S(1)}, f32[128,8,128]{2,1,0:T(8,128)S(1)}, u32[]{:S(2)}, u32[]{:S(2)}) collective-permute-start(f32[128,8,128]{2,1,0:T(8,128)S(1)} %add_up.3.mine), channel_id=1, source_target_pairs={{0,64},{64,0},{1,65},{65,1},{2,66},{66,2},{3,67},{67,3},{4,68},{68... | collective-permute-start | bytes 1572872 | tf_op jit(solution)/shard_map/ppermute | solution.py:279
  142.7 6.2 %collective-permute-start.5 = (bf16[64,80,128]{2,1,0:T(8,128)(2,1)S(1)}, bf16[64,80,128]{2,1,0:T(8,128)(2,1)S(1)}, u32[]{:S(2)}, u32[]{:S(2)}) collective-permute-start(bf16[64,80,128]{2,1,0:T(8,128)(2,1)S(1)} %all_to_all.31.high.high1), channel_id=1, source_target_pairs={{0,64},{1,65},{2,66},{3,67},{4,68},{5,69},{6,70},{7,71},{8,72},{9,... | collective-permute-start | bytes 3932168 | tf_op jit(solution)/shard_map/ppermute | solution.py:276
  149.0 9.8 %copy-start = (bf16[64,80,128]{2,1,0:T(8,128)(2,1)}, bf16[64,80,128]{2,1,0:T(8,128)(2,1)S(1)}, u32[]{:S(2)}) copy-start(bf16[64,80,128]{2,1,0:T(8,128)(2,1)S(1)} %collective-permute-done.5.low.low1) | copy-start | bytes 3932164
  158.8 3.2 %collective-permute-start.6 = (bf16[2,512,128]{2,1,0:T(8,128)(2,1)S(1)}, bf16[2,512,128]{2,1,0:T(8,128)(2,1)S(1)}, u32[]{:S(2)}, u32[]{:S(2)}) collective-permute-start(bf16[2,512,128]{2,1,0:T(8,128)(2,1)S(1)} %first_backward.1), channel_id=1, source_target_pairs={{64,0},{65,1},{66,2},{67,3},{68,4},{69,5},{70,6},{71,7},{72,8},{73... | collective-permute-start | bytes 786440 | tf_op jit(solution)/shard_map/ppermute | solution.py:276
  177.3 30.2 %copy-start.3 = (bf16[128,1024]{1,0:T(8,128)(2,1)S(1)}, bf16[128,1024]{1,0:T(8,128)(2,1)}, u32[]{:S(2)}) copy-start(bf16[128,1024]{1,0:T(8,128)(2,1)} %x.5) | copy-start | bytes 786436
  200.7 8.6 %collective-permute-start.7 = (bf16[64,80,128]{2,1,0:T(8,128)(2,1)S(1)}, bf16[64,80,128]{2,1,0:T(8,128)(2,1)}, u32[]{:S(2)}, u32[]{:S(2)}) collective-permute-start(bf16[64,80,128]{2,1,0:T(8,128)(2,1)S(1)} %all_to_all.33.low0), channel_id=1, source_target_pairs={{64,0},{65,1},{66,2},{67,3},{68,4},{69,5},{70,6},{71,7},{72,8},{73... | collective-permute-start | bytes 3932168 | tf_op jit(solution)/shard_map/ppermute | solution.py:276
  209.3 1.3 copy-start.1

commit v2 on v1

v2 whole, which is shorter than its diff:
```python
import functools
import math

import jax
import jax.numpy as jnp
from jax import lax
from jax.experimental import pallas as pl
from jax.experimental.pallas import tpu as pltpu
from jax.sharding import PartitionSpec as P

SLICE = 8
VMEM_LIMIT = 16 * 1024 * 1024
STREAM_LIMIT = 48 * 1024 * 1024


def params(limit=VMEM_LIMIT):
    return pltpu.CompilerParams(vmem_limit_bytes=limit)


def tile_copies(source, first, held, sems):
    def copy(k):
        return pltpu.make_async_copy(
            source.at[pl.ds(first + 2 * k, 2)], held.at[pl.ds(2 * k, 2)], sems.at[k]
        )

    return copy


def tile_scratch(count, width):
    return [pltpu.VMEM((count, width, width), jnp.bfloat16), pltpu.SemaphoreType.DMA((count // 2,))]


def product_pair(cols, at, x, tiles, out, pair):
    width = tiles.shape[1]
    parts = []
    for u in range(2):
        col = cols[at + 2 * pair + u]
        picked = x[:, pl.ds(pl.multiple_of(col * width, width), width)]
        product = jnp.dot(picked, tiles[2 * pair + u], preferred_element_type=jnp.float32)
        parts.append(product.T.reshape(width // SLICE, SLICE, x.shape[0]))
    both = jnp.concatenate(parts, axis=1).astype(jnp.bfloat16)
    out[:, pl.ds(pl.multiple_of(2 * SLICE * pair, 2 * SLICE), 2 * SLICE), :] = both


def first_products_body(cols, x, tiles, out, held, sems, *, first):
    pairs = held.shape[0] // 2
    copy = tile_copies(tiles, first, held, sems)
    for k in range(pairs):
        copy(k).start()

    @pl.loop(0, pairs)
    def _(k):
        copy(k).wait()
        product_pair(cols, first, x, held, out, k)


def first_products(cols, x, tiles, first, count):
    width = tiles.shape[1]
    scen = x.shape[0]
    vmem = pl.BlockSpec(memory_space=pltpu.VMEM)
    return pl.pallas_call(
        functools.partial(first_products_body, first=first),
        in_specs=[
            pl.BlockSpec(memory_space=pltpu.SMEM),
            vmem,
            pl.BlockSpec(memory_space=pl.ANY),
        ],
        out_specs=vmem,
        out_shape=jax.ShapeDtypeStruct((width // SLICE, count * SLICE, scen), jnp.bfloat16),
        scratch_shapes=tile_scratch(count, width),
        compiler_params=params(STREAM_LIMIT),
        name="first_products",
    )(cols, x, tiles)


def start_split_tiles(core, received, tiles, held, sems):
    count = held.shape[0]

    @pl.when(core == 0)
    def _():
        for k in range(count // 2):
            tile_copies(received, 0, held, sems)(k).start()

    @pl.when(core == 1)
    def _():
        for k in range(count // 2):
            tile_copies(tiles, count, held, sems)(k).start()

    return tile_copies(received, 0, held, sems)


def split_products_body(meta, x, received, tiles, out, held, sems):
    copy = start_split_tiles(meta[0], received, tiles, held, sems)

    @pl.loop(0, held.shape[0] // 2)
    def _(k):
        copy(k).wait()
        product_pair(meta, 1, x, held, out, k)


def split_products(meta, x, received, tiles):
    count, width = received.shape[0] // 2, received.shape[1]
    scen = x.shape[0]
    vmem = pl.BlockSpec(memory_space=pltpu.VMEM)
    hbm = pl.BlockSpec(memory_space=pl.ANY)
    return pl.pallas_call(
        split_products_body,
        in_specs=[pl.BlockSpec(memory_space=pltpu.SMEM), vmem, hbm, hbm],
        out_specs=vmem,
        out_shape=jax.ShapeDtypeStruct((width // SLICE, count * SLICE, scen), jnp.bfloat16),
        scratch_shapes=tile_scratch(count, width),
        compiler_params=params(STREAM_LIMIT),
        name="split_products",
    )(meta, x, received, tiles)


def add_up_body(idx, data, out, *, count):
    out[...] = jnp.zeros_like(out)

    @pl.loop(0, data.shape[0])
    def _(i):
        values = data[i].astype(jnp.float32)
        places = [idx[i * count + t] for t in range(count)]
        sums = [
            out[places[t]] + values[t * SLICE : (t + 1) * SLICE] for t in range(count)
        ]
        for t in range(count):
            out[places[t]] = sums[t]


def add_up(idx, data, blocks):
    count = data.shape[1] // SLICE
    return pl.pallas_call(
        functools.partial(add_up_body, count=count),
        in_specs=[pl.BlockSpec(memory_space=pltpu.SMEM), pl.BlockSpec(memory_space=pltpu.VMEM)],
        out_specs=pl.BlockSpec(memory_space=pltpu.VMEM),
        out_shape=jax.ShapeDtypeStruct((blocks, SLICE, data.shape[2]), jnp.float32),
        compiler_params=params(),
        name="add_up",
    )(idx, data)


def hand_out(idx, held, out, count):
    @pl.loop(0, out.shape[0])
    def _(i):
        for t in range(0, count, 2):
            pair = [held[idx[i * count + t]], held[idx[i * count + t + 1]]]
            rows = jnp.concatenate(pair, axis=0).astype(jnp.bfloat16)
            out[i, t * SLICE : (t + 2) * SLICE, :] = rows


def value_and_hand_out_body(idx, mine, other, notional, strike, out, held, *, count, weight):
    @pl.loop(0, held.shape[0], step=8)
    def _(b):
        for k in range(8):
            moneyness = mine[b + k] + other[b + k]
            held[b + k] = notional[b + k] * jax.nn.sigmoid(moneyness - strike[b + k]) * weight

    hand_out(idx, held, out, count)


def value_and_hand_out(idx, mine, other, notional, strike, shards, count, weight):
    scen = mine.shape[2]
    vmem = pl.BlockSpec(memory_space=pltpu.VMEM)
    return pl.pallas_call(
        functools.partial(value_and_hand_out_body, count=count, weight=weight),
        in_specs=[pl.BlockSpec(memory_space=pltpu.SMEM), vmem, vmem, vmem, vmem],
        out_specs=vmem,
        out_shape=jax.ShapeDtypeStruct((shards, count * SLICE, scen), jnp.bfloat16),
        scratch_shapes=[pltpu.VMEM(mine.shape, jnp.float32)],
        compiler_params=params(),
        name="value_and_hand_out",
    )(idx, mine, other, notional, strike)


def only_hand_out_body(idx, blocks, out, held, *, count):
    held[...] = blocks[...].astype(jnp.float32).reshape(held.shape)
    hand_out(idx, held, out, count)


def only_hand_out(idx, blocks, shards, count):
    scen = blocks.shape[2]
    vmem = pl.BlockSpec(memory_space=pltpu.VMEM)
    held = blocks.shape[0] * blocks.shape[1] // SLICE
    return pl.pallas_call(
        functools.partial(only_hand_out_body, count=count),
        in_specs=[pl.BlockSpec(memory_space=pltpu.SMEM), vmem],
        out_specs=vmem,
        out_shape=jax.ShapeDtypeStruct((shards, count * SLICE, scen), jnp.bfloat16),
        scratch_shapes=[pltpu.VMEM((held, SLICE, scen), jnp.float32)],
        compiler_params=params(),
        name="hand_out",
    )(idx, blocks)


def tile_grad_pair(grads, pair):
    rows = grads[:, pl.ds(pl.multiple_of(pair * 2 * SLICE, 2 * SLICE), 2 * SLICE), :]
    rows = rows.astype(jnp.float32)
    width = rows.shape[0] * SLICE
    return [
        rows[:, u * SLICE : (u + 1) * SLICE, :].reshape(width, -1).astype(jnp.bfloat16)
        for u in range(2)
    ]


def split_backward_body(meta, grads, received, tiles, total, held, sems):
    copy = start_split_tiles(meta[0], received, tiles, held, sems)
    total[...] = jnp.zeros_like(total)

    @pl.loop(0, held.shape[0] // 2)
    def _(k):
        copy(k).wait()
        for u, grad in enumerate(tile_grad_pair(grads, k)):
            product = jnp.dot(held[2 * k + u], grad, preferred_element_type=jnp.float32)
            total[meta[1 + 2 * k + u]] += product


def split_backward(meta, grads, received, tiles, blocks_dev):
    count, width = received.shape[0] // 2, received.shape[1]
    vmem = pl.BlockSpec(memory_space=pltpu.VMEM)
    hbm = pl.BlockSpec(memory_space=pl.ANY)
    return pl.pallas_call(
        split_backward_body,
        in_specs=[pl.BlockSpec(memory_space=pltpu.SMEM), vmem, hbm, hbm],
        out_specs=vmem,
        out_shape=jax.ShapeDtypeStruct((blocks_dev, width, grads.shape[2]), jnp.float32),
        scratch_shapes=tile_scratch(count, width),
        compiler_params=params(STREAM_LIMIT),
        name="split_backward",
    )(meta, grads, received, tiles)


def last_backward_body(meta, grads0, grads1, inputs, tiles, *rest, first):
    earlier = rest[:2] if first else ()
    sens, result, grads, total, stage, out_sems, held, sems = rest[len(earlier) :]
    pairs = held.shape[0] // 2
    take = tile_copies(tiles, first, held, sems)
    for k in range(pairs):
        take(k).start()

    @pl.when(meta[0] == 0)
    def _():
        grads[...] = grads0[...]

    @pl.when(meta[0] == 1)
    def _():
        grads[...] = grads1[...]

    total[...] = earlier[0][...] if earlier else jnp.zeros_like(total)

    def put(k):
        slot = lax.rem(k, 2)
        return pltpu.make_async_copy(
            stage.at[slot], sens.at[pl.ds(first + 2 * k, 2)], out_sems.at[slot]
        )

    @pl.loop(0, pairs)
    def _(k):
        @pl.when(k >= 2)
        def _():
            put(k - 2).wait()

        take(k).wait()
        slot = lax.rem(k, 2)
        for u, grad in enumerate(tile_grad_pair(grads, k)):
            col = meta[1 + first + 2 * k + u]
            total[col] += jnp.dot(held[2 * k + u], grad, preferred_element_type=jnp.float32)
            stage[slot, u] = lax.dot_general(
                inputs[col], grad, (((1,), (1,)), ((), ())), preferred_element_type=jnp.float32
            ).astype(jnp.bfloat16)
        put(k).start()

    if earlier:
        width = total.shape[1]
        for c in range(total.shape[0]):
            result[:, c * width : (c + 1) * width] = total[c].T.astype(jnp.bfloat16)
    else:
        result[...] = total[...]
    for k in range(max(pairs - 2, 0), pairs):
        put(k).wait()


def last_backward(meta, grads0, grads1, inputs, tiles, first, count, earlier=()):
    slots, width, _ = tiles.shape
    blocks_dev, _, scen = inputs.shape
    vmem = pl.BlockSpec(memory_space=pltpu.VMEM)
    hbm = pl.BlockSpec(memory_space=pl.ANY)
    result = (
        jax.ShapeDtypeStruct((scen, blocks_dev * width), jnp.bfloat16)
        if earlier
        else jax.ShapeDtypeStruct(inputs.shape, jnp.float32)
    )
    return pl.pallas_call(
        functools.partial(last_backward_body, first=first),
        in_specs=[pl.BlockSpec(memory_space=pltpu.SMEM), vmem, vmem, vmem, hbm]
        + [vmem, hbm][: len(earlier)],
        out_specs=[hbm, vmem],
        out_shape=[jax.ShapeDtypeStruct((slots, width, width), jnp.bfloat16), result],
        scratch_shapes=[
            pltpu.VMEM(grads0.shape, jnp.bfloat16),
            pltpu.VMEM(inputs.shape, jnp.float32),
            pltpu.VMEM((2, 2, width, width), jnp.bfloat16),
            pltpu.SemaphoreType.DMA((2,)),
        ]
        + tile_scratch(count, width),
        input_output_aliases={6: 0} if earlier else {},
        compiler_params=params(STREAM_LIMIT),
        name="last_backward",
    )(meta, grads0, grads1, inputs, tiles, *earlier)


def three_terms(values):
    terms = []
    for _ in range(3):
        term = lax.reduce_precision(values, 8, 7)
        terms.append(term)
        values = values - term
    return jnp.stack(terms)


def exchange(block):
    return lax.all_to_all(block, "blk", split_axis=0, concat_axis=0, tiled=True)


def on_device(normals, section_tile_list, tile_output_block, tile_col, notional, strike):
    shards = lax.axis_size("blk")
    core = lax.axis_index("phase")
    tiles = section_tile_list[0]
    slots, width, _ = tiles.shape
    half = slots // 2
    scen, local_width = normals.shape
    blocks_dev = local_width // width
    blocks = shards * blocks_dev
    cols = tile_col[0]
    weight = 1.0 / math.sqrt(scen)

    def of_core(zero, one):
        return jnp.where(core == 0, zero, one)

    def send(block, source):
        return lax.ppermute(block, "phase", [(source, 1 - source)])

    def swap(block):
        return lax.ppermute(block, "phase", [(0, 1), (1, 0)])

    my_places = jnp.concatenate([tile_output_block[0], cols])
    other_places = swap(my_places)
    places = [of_core(my_places, other_places), of_core(other_places, my_places)]
    split_rows = []
    for place in places:
        rows = place[: shards * slots].reshape(shards, slots)
        split_rows.append(of_core(rows[:, :half], rows[:, half:]).reshape(-1))
    my_number = core[None].astype(jnp.int32)
    split_meta = jnp.concatenate([my_number, of_core(places[1][-slots:-half], cols[half:])])
    meta = jnp.concatenate([my_number, cols])

    sent = first_products(cols, normals, tiles, half, half)
    kept = first_products(cols, normals, tiles, 0, half)
    outgoing, tiles_now = lax.optimization_barrier((of_core(kept, send(sent, 0)), tiles))
    received = send(tiles_now, 1)
    arrived = exchange(outgoing)
    part = add_up(split_rows[0], arrived, blocks)
    shock_slices = (part + swap(part)).astype(jnp.bfloat16)

    scales = jnp.stack([three_terms(notional), three_terms(strike)])
    scales = scales.reshape(6, blocks_dev, shards, SLICE).transpose(2, 0, 1, 3)
    scales = scales.reshape(shards, 1, 6 * blocks_dev * SLICE).astype(jnp.bfloat16)
    scales = jnp.pad(scales, ((0, 0), (0, SLICE - 1), (0, scen - scales.shape[2])))
    shock_rows = shock_slices.reshape(shards, blocks_dev * SLICE, scen)
    arrived = exchange(jnp.concatenate([shock_rows, scales], axis=1))
    shocks = arrived[:, : blocks_dev * SLICE].reshape(shards, blocks_dev, SLICE, scen)
    shocks = shocks.transpose(1, 0, 2, 3).reshape(blocks_dev, width, scen)
    shocks_natural = shocks.transpose(2, 0, 1).reshape(scen, local_width)
    scales = arrived[:, blocks_dev * SLICE, : 6 * blocks_dev * SLICE].astype(jnp.float32)
    scales = scales.reshape(shards, 2, 3, blocks_dev, SLICE)
    scales = (scales[:, :, 0] + scales[:, :, 1]) + scales[:, :, 2]
    scales = scales.transpose(1, 0, 2, 3).reshape(2, blocks, SLICE, 1)

    arrived = exchange(split_products(split_meta, shocks_natural, received, tiles))
    part = add_up(split_rows[1], arrived, blocks)
    outgoing = value_and_hand_out(
        split_rows[1], part, swap(part), scales[0], scales[1], shards, half, weight
    )

    high1 = exchange(outgoing)
    part = split_backward(split_meta, high1, received, tiles, blocks_dev)
    shock_grad = (part + swap(part)).astype(jnp.bfloat16)
    low1 = send(high1, 0)

    shock_grad = shock_grad.reshape(blocks_dev, shards, SLICE, scen).transpose(1, 0, 2, 3)
    arrived = exchange(shock_grad.reshape(shards, blocks_dev * SLICE, scen))
    low0 = exchange(only_hand_out(split_rows[0], arrived, shards, half))
    high0 = send(low0, 1)

    normals_held = normals.reshape(scen, blocks_dev, width).transpose(1, 2, 0)
    inputs = of_core(normals_held, shocks)
    sens, part = last_backward(meta, low0, low1, inputs, tiles, 0, half)
    sens, adjoint = last_backward(meta, high0, high1, inputs, tiles, half, half, (part, sens))
    return sens[None], adjoint[None]


def solution(mesh):
    return jax.shard_map(
        on_device,
        mesh=mesh,
        in_specs=(
            P(None, "blk"),
            P("phase", "blk", None, None),
            P("phase", None),
            P("phase", "blk"),
            P("blk"),
            P("blk"),
        ),
        out_specs=(P("phase", "blk", None, None), P("phase", None, "blk")),
        check_vma=False,
    )
```

time: 226 us -> 206 us (0.912)
  blocking collectives: 76.8 us -> 37.6 us
  waiting for transfers between devices: 46.9 us -> 67.2 us
  starting transfers between devices: 37.5 us -> 48.9 us
  Pallas kernels: 51.9 us -> 41.7 us
    all_to_all x4 -> x2, blocking collectives: 76.8 us -> 37.6 us  [exchange(): return lax.all_to_all(block, 'blk', split_axis=0, concat_axis=0, tiled=True)]
    all_to_all x2 -> x4, waiting for transfers between devices: 37.8 us -> 63 us  [exchange(): return lax.all_to_all(block, 'blk', split_axis=0, concat_axis=0, tiled=True)]
    pallas_call x6, Pallas kernels: 43.6 us -> 32.4 us  [the longest x2 16 us: last_backward(): pl.pallas_call(functools.partial(last_backward_body, first=first), in_spe...]
    all_to_all x2 -> x4, starting transfers between devices: 16.8 us -> 26.3 us  [exchange(): return lax.all_to_all(block, 'blk', split_axis=0, concat_axis=0, tiled=True)]
    ppermute x5 -> x4, waiting for transfers between devices: 7.45 us -> 0.3 us  [send(): return lax.ppermute(block, 'phase', [(source, 1 - source)])]
    ppermute x5 -> x4, starting transfers between devices: 15.5 us -> 16.5 us  [send(): return lax.ppermute(block, 'phase', [(source, 1 - source)])]
    ppermute x3 -> x4, starting transfers between devices: 5.28 us -> 6.2 us  [swap(): return lax.ppermute(block, 'phase', [(0, 1), (1, 0)])]
  transfers between devices with their start and end apart: 10 -> 12, of which waited for: 7 -> 8; matrix products, arithmetic and copies ran while one was open for 2% -> 2% of each run, Pallas kernels for 4% -> 6%
where the time goes in v2:
time: 206 us
  waiting for transfers between devices  67.2 us (33%)
  starting transfers between devices  48.9 us (24%)
  Pallas kernels  41.7 us (20%)
  blocking collectives  37.6 us (18%)
  local copies, waits for them, and re-layouts  4.91 us (2%)
  other arithmetic  4.11 us (2%)
    all_to_all x4, waiting for transfers between devices, exchange(): return lax.all_to_all(block, 'blk', split_axis=0, concat_axis=0, tiled=True)  63 us
    all_to_all x2, blocking collectives, exchange(): return lax.all_to_all(block, 'blk', split_axis=0, concat_axis=0, tiled=True)  37.6 us
    all_to_all x4, starting transfers between devices, exchange(): return lax.all_to_all(block, 'blk', split_axis=0, concat_axis=0, tiled=True)  26.3 us
    ppermute x4, starting transfers between devices, send(): return lax.ppermute(block, 'phase', [(source, 1 - source)])  16.5 us
    pallas_call x2, Pallas kernels, last_backward(): pl.pallas_call(functools.partial(last_backward_body, first=first), in_spe...  16 us
    pallas_call x2, Pallas kernels, first_products(): pl.pallas_call(functools.partial(first_products_body, first=first), in_sp...  7.5 us
    ppermute x4, starting transfers between devices, swap(): return lax.ppermute(block, 'phase', [(0, 1), (1, 0)])  6.2 us
    pallas_call x1, Pallas kernels, split_products(): pl.pallas_call(split_products_body, in_specs=[pl.BlockSpec(memory_space=p...  4.84 us
  transfers between devices with their start and end apart: 12, of which 8 were waited for; matrix products, arithmetic and copies ran while one was open for 2% of the time, Pallas kernels for 6%

profile of v2, /device:TPU:1, one launch (start us, length us, event | category | flops | bytes accessed | tf_op | source)
XLA Modules:
  0.0 205.5 jit_solution(11140789478031263362)
XLA Ops:
  0.6 0.9 copy-done
  1.6 0.7 copy-done.2
  2.2 3.7 %first_products.3 = bf16[64,80,128]{2,1,0:T(8,128)(2,1)S(1)} custom-call(s32[20]{0:T(128)S(1)} %bitcast.43, bf16[128,1024]{1,0:T(8,128)(2,1)S(1)} %copy-done, bf16[20,512,512]{2,1,0:T(8,128)(2,1)} %bitcast.49), custom_call_target="tpu_custom_call" | custom-call | tf_op jit(solution)/shard_map/first_products/pallas_call | solution.py:61
  6.0 1.3 collective-permute-start.1
  7.3 3.7 %first_products.2 = bf16[64,80,128]{2,1,0:T(8,128)(2,1)S(1)} custom-call(s32[20]{0:T(128)S(1)} %bitcast.44, bf16[128,1024]{1,0:T(8,128)(2,1)S(1)} %copy-done, bf16[20,512,512]{2,1,0:T(8,128)(2,1)} %bitcast.50), custom_call_target="tpu_custom_call" | custom-call | tf_op jit(solution)/shard_map/first_products/pallas_call | solution.py:61
  11.1 0.3 collective-permute-done.1
  11.4 2.6 %broadcast_select_fusion = bf16[64,80,128]{2,1,0:T(8,128)(2,1)} fusion(bf16[64,80,128]{2,1,0:T(8,128)(2,1)S(1)} %first_products.2, bf16[64,80,128]{2,1,0:T(8,128)(2,1)} %collective-permute-done.1, pred[]{:T(512)S(6)} %eq.2), kind=kLoop, calls=%fused_computation | loop fusion | flops 655360 | bytes 3932161 | tf_op jit(solution)/shard_map/jit(_where)/select_n | solution.py:338
  13.9 7.0 %collective-permute-start.3 = (bf16[20,512,512]{2,1,0:T(8,128)(2,1)}, bf16[20,512,512]{2,1,0:T(8,128)(2,1)}, u32[]{:S(2)}, u32[]{:S(2)}) collective-permute-start(bf16[20,512,512]{2,1,0:T(8,128)(2,1)} %bitcast.51), channel_id=1, source_target_pairs={{64,0},{65,1},{66,2},{67,3},{68,4},{69,5},{70,6},{71,7},{72,8},{73... | collective-permute-start | bytes 31457288 | tf_op jit(solution)/shard_map/ppermute | solution.py:341
  20.9 11.7 %all-to-all-start = ((bf16[64,80,128]{2,1,0:T(8,128)(2,1)}), bf16[64,80,128]{2,1,0:T(8,128)(2,1)S(1)}, u32[]{:S(2)}, u32[]{:S(2)}) async-start(bf16[64,80,128]{2,1,0:T(8,128)(2,1)} %broadcast_select_fusion), calls=%async_computation | async-start | bytes 2621440 | tf_op jit(solution)/shard_map/all_to_all | solution.py:322
  32.7 0.1 collective-permute-start
  32.7 1.2 collective-permute-done
  33.9 0.1 slice.71
  34.1 0.1 reshape.77.idx
  34.2 16.2 %all-to-all-done.data = bf16[64,80,128]{2,1,0:T(8,128)(2,1)S(1)} async-done(((bf16[64,80,128]{2,1,0:T(8,128)(2,1)}), bf16[64,80,128]{2,1,0:T(8,128)(2,1)S(1)}, u32[]{:S(2)}, u32[]{:S(2)}) %all-to-all-start) | async-done | bytes 1310752 | tf_op jit(solution)/shard_map/all_to_all | solution.py:322
  50.4 1.8 add_up.2
  52.5 0.3 convert_element_type.34
  52.7 0.1 copy.36
  52.8 0.1 copy.49
  53.0 1.2 collective-permute-done.2
  54.2 0.8 fusion.1
  55.0 4.6 %all-to-all-start.1 = ((bf16[64,24,128]{2,1,0:T(8,128)(2,1)}), bf16[64,24,128]{2,1,0:T(8,128)(2,1)S(1)}, u32[]{:S(2)}, u32[]{:S(2)}) async-start(bf16[64,24,128]{2,1,0:T(8,128)(2,1)} %fusion.1), calls=%async_computation.1 | async-start | bytes 786432 | tf_op jit(solution)/shard_map/all_to_all | solution.py:322
  59.8 11.0 %all-to-all-done.1 = bf16[64,24,128]{2,1,0:T(8,128)(2,1)S(1)} async-done(((bf16[64,24,128]{2,1,0:T(8,128)(2,1)}), bf16[64,24,128]{2,1,0:T(8,128)(2,1)S(1)}, u32[]{:S(2)}, u32[]{:S(2)}) %all-to-all-start.1) | async-done | bytes 393248 | tf_op jit(solution)/shard_map/all_to_all | solution.py:322
  70.9 0.1 copy.39.x
  71.0 4.8 %split_products.1 = bf16[64,80,128]{2,1,0:T(8,128)(2,1)} custom-call(s32[11]{0:T(128)S(1)} %pad_add_fusion.2.meta, bf16[128,1024]{1,0:T(8,128)(2,1)S(1)} %copy.39.x, bf16[20,512,512]{2,1,0:T(8,128)(2,1)} %collective-permute-done.3.received, bf16[20,512,512]{2,1,0:T(8,128)(2,1)} %bitcast.52), custom_call_target="tpu_custom_call" | custom-call | tf_op jit(solution)/shard_map/split_products/pallas_call | solution.py:106
  75.9 5.0 %all-to-all-start.2 = ((bf16[64,80,128]{2,1,0:T(8,128)(2,1)}), bf16[64,80,128]{2,1,0:T(8,128)(2,1)S(1)}, u32[]{:S(2)}, u32[]{:S(2)}) async-start(bf16[64,80,128]{2,1,0:T(8,128)(2,1)} %split_products.1), calls=%async_computation.2 | async-start | bytes 2621440 | tf_op jit(solution)/shard_map/all_to_all | solution.py:322
  80.8 0.1 slice.78
  81.0 0.1 reshape.78.idx
  81.2 18.6 %all-to-all-done.2.data = bf16[64,80,128]{2,1,0:T(8,128)(2,1)S(1)} async-done(((bf16[64,80,128]{2,1,0:T(8,128)(2,1)}), bf16[64,80,128]{2,1,0:T(8,128)(2,1)S(1)}, u32[]{:S(2)}, u32[]{:S(2)}) %all-to-all-start.2) | async-done | bytes 1310752 | tf_op jit(solution)/shard_map/all_to_all | solution.py:322
  99.8 1.8 add_up.3.mine
  101.6 3.5 %collective-permute-start.4 = (f32[128,8,128]{2,1,0:T(8,128)S(1)}, f32[128,8,128]{2,1,0:T(8,128)S(1)}, u32[]{:S(2)}, u32[]{:S(2)}) collective-permute-start(f32[128,8,128]{2,1,0:T(8,128)S(1)} %add_up.3.mine), channel_id=1, source_target_pairs={{0,64},{64,0},{1,65},{65,1},{2,66},{66,2},{3,67},{67,3},{4,68},{68... | collective-permute-start | bytes 1572872 | tf_op jit(solution)/shard_map/ppermute | solution.py:344
  105.2 0.1 copy.43
  105.3 0.1 copy.42
  105.4 0.8 copy.44.notional
  106.3 0.8 copy.45.strike
  107.1 3.0 %value_and_hand_out.1 = bf16[64,80,128]{2,1,0:T(8,128)(2,1)S(1)} custom-call(s32[640]{0:T(1024)S(1)} %reshape.78.idx, f32[128,8,128]{2,1,0:T(8,128)S(1)} %add_up.3.mine, f32[128,8,128]{2,1,0:T(8,128)S(1)} %collective-permute-done.4.other, f32[128,8,1]{2,1,0:T(8,128)S(1)} %copy.44.notional, f32[128,8,1]{2,1,0:T(8,128)S(1)} %copy.45.strike), custom_call_target="tpu_custom_call" | custom-call | tf_op jit(solution)/shard_map/value_and_hand_out/pallas_call | solution.py:165
  110.1 24.2 %all_to_all.30.grads.grads1 = bf16[64,80,128]{2,1,0:T(8,128)(2,1)S(1)} all-to-all(bf16[64,80,128]{2,1,0:T(8,128)(2,1)S(1)} %value_and_hand_out.1), channel_id=1, replica_groups=mesh['phase'=2,'blk'=64] {'blk'}, dimensions={0} | all-to-all | bytes 2621440 | tf_op jit(solution)/shard_map/all_to_all | solution.py:322
  134.3 4.0 %split_backward.1 = f32[2,512,128]{2,1,0:T(8,128)S(1)} custom-call(s32[11]{0:T(128)S(1)} %pad_add_fusion.2.meta, bf16[64,80,128]{2,1,0:T(8,128)(2,1)S(1)} %all_to_all.30.grads.grads1, bf16[20,512,512]{2,1,0:T(8,128)(2,1)} %collective-permute-done.3.received, bf16[20,512,512]{2,1,0:T(8,128)(2,1)} %bitcast.53), custom_call_target="tpu_custom_call" | custom-call | tf_op jit(solution)/shard_map/split_backward/pallas_call | solution.py:222
  138.3 2.5 %collective-permute-start.5 = (f32[2,512,128]{2,1,0:T(8,128)S(1)}, f32[2,512,128]{2,1,0:T(8,128)S(1)}, u32[]{:S(2)}, u32[]{:S(2)}) collective-permute-start(f32[2,512,128]{2,1,0:T(8,128)S(1)} %split_backward.1), channel_id=1, source_target_pairs={{0,64},{64,0},{1,65},{65,1},{2,66},{66,2},{3,67},{67,3},{4,68},{68... | collective-permute-start | bytes 1572872 | tf_op jit(solution)/shard_map/ppermute | solution.py:344
  140.8 1.5 collective-permute-done.5
  142.4 13.5 %all_to_all.31.blocks = bf16[64,16,128]{2,1,0:T(8,128)(2,1)S(1)} all-to-all(bf16[64,16,128]{2,1,0:T(8,128)(2,1)S(1)} %copy_bitcast_fusion), channel_id=1, replica_groups=mesh['phase'=2,'blk'=64] {'blk'}, dimensions={0} | all-to-all | bytes 524288 | tf_op jit(solution)/shard_map/all_to_all | solution.py:322
  155.9 2.8 %hand_out.1 = bf16[64,80,128]{2,1,0:T(8,128)(2,1)} custom-call(s32[640]{0:T(1024)S(1)} %reshape.77.idx, bf16[64,16,128]{2,1,0:T(8,128)(2,1)S(1)} %all_to_all.31.blocks), custom_call_target="tpu_custom_call" | custom-call | tf_op jit(solution)/shard_map/hand_out/pallas_call | solution.py:185
  158.7 5.0 %all-to-all-start.5 = ((bf16[64,80,128]{2,1,0:T(8,128)(2,1)}), bf16[64,80,128]{2,1,0:T(8,128)(2,1)S(1)}, u32[]{:S(2)}, u32[]{:S(2)}) async-start(bf16[64,80,128]{2,1,0:T(8,128)(2,1)} %hand_out.1), calls=%async_computation.5 | async-start | bytes 2621440 | tf_op jit(solution)/shard_map/all_to_all | solution.py:322
  163.7 1.3 collective-permute-start.7
  165.0 17.2 %all-to-all-done.5.grads0 = bf16[64,80,128]{2,1,0:T(8,128)(2,1)S(1)} async-done(((bf16[64,80,128]{2,1,0:T(8,128)(2,1)}), bf16[64,80,128]{2,1,0:T(8,128)(2,1)S(1)}, u32[]{:S(2)}, u32[]{:S(2)}) %all-to-all-start.5) | async-done | bytes 1310752 | tf_op jit(solution)/shard_map/all_to_all | solution.py:322
  182.2 6.9 %collective-permute-start.6 = (bf16[64,80,128]{2,1,0:T(8,128)(2,1)S(1)}, bf16[64,80,128]{2,1,0:T(8,128)(2,1)}, u32[]{:S(2)}, u32[]{:S(2)}) collective-permute-start(bf16[64,80,128]{2,1,0:T(8,128)(2,1)S(1)} %all-to-all-done.5.grads0), channel_id=1, source_target_pairs={{64,0},{65,1},{66,2},{67,3},{68,4},{69,5},{70,6},{71,7},{72,8},{73... | collective-permute-start | bytes 3932168 | tf_op jit(solution)/shard_map/ppermute | solution.py:341
  189.1 0.2 copy.47
  189.5 7.7 %last_backward.2 = (bf16[20,512,512]{2,1,0:T(8,128)(2,1)}, f32[2,512,128]{2,1,0:T(8,128)S(1)}) custom-call(s32[21]{0:T(128)S(1)} %pad_add_fusion.1.meta, bf16[64,80,128]{2,1,0:T(8,128)(2,1)S(1)} %all-to-all-done.5.grads0, bf16[64,80,128]{2,1,0:T(8,128)(2,1)} %collective-permute-done.7.grads1, bf16[2,512,128]{2,1,0:T(8,128)(2,1)S(1)} %bitcast_select_fusion.inputs, ...), custom_call_target="tpu_custom_call" | custom-call | tf_op jit(solution)/shard_map/last_backward/pallas_call | solution.py:293
  197.2 8.4 %last_backward.3 = (bf16[20,512,512]{2,1,0:T(8,128)(2,1)}, bf16[128,1024]{1,0:T(8,128)(2,1)}) custom-call(s32[21]{0:T(128)S(1)} %pad_add_fusion.1.meta, bf16[64,80,128]{2,1,0:T(8,128)(2,1)} %collective-permute-done.6.grads0, bf16[64,80,128]{2,1,0:T(8,128)(2,1)S(1)} %all_to_all.30.grads.grads1, ...), custom_call_target="tpu_custom_call", output_to_operand_aliasing={{0}: (6, {})} | custom-call | tf_op jit(solution)/shard_map/last_backward/pallas_call | solution.py:293
  (46 shorter events, 1.0 us)
Async XLA Ops:
  0.6 1.0 copy-start
  1.6 0.7 copy-start.2
  6.0 5.4 %collective-permute-start.1 = (bf16[64,80,128]{2,1,0:T(8,128)(2,1)S(1)}, bf16[64,80,128]{2,1,0:T(8,128)(2,1)}, u32[]{:S(2)}, u32[]{:S(2)}) collective-permute-start(bf16[64,80,128]{2,1,0:T(8,128)(2,1)S(1)} %first_products.3), channel_id=1, source_target_pairs={{0,64},{1,65},{2,66},{3,67},{4,68},{5,69},{6,70},{7,71},{8,72},{9,... | collective-permute-start | bytes 3932168 | tf_op jit(solution)/shard_map/ppermute | solution.py:341
  13.9 18.6 %copy-start.4 = (s32[1,1280]{1,0:T(1,128)S(1)}, s32[1,1280]{1,0:T(1,128)}, u32[]{:S(2)}) copy-start(s32[1,1280]{1,0:T(1,128)} %param.8) | copy-start | bytes 15364
  13.9 18.7 %copy-start.3 = (s32[1,20]{1,0:T(1,128)S(1)}, s32[1,20]{1,0:T(1,128)}, u32[]{:S(2)}) copy-start(s32[1,20]{1,0:T(1,128)} %param.9) | copy-start | bytes 244
  13.9 57.1 %collective-permute-start.3 = (bf16[20,512,512]{2,1,0:T(8,128)(2,1)}, bf16[20,512,512]{2,1,0:T(8,128)(2,1)}, u32[]{:S(2)}, u32[]{:S(2)}) collective-permute-start(bf16[20,512,512]{2,1,0:T(8,128)(2,1)} %bitcast.51), channel_id=1, source_target_pairs={{64,0},{65,1},{66,2},{67,3},{68,4},{69,5},{70,6},{71,7},{72,8},{73... | collective-permute-start | bytes 31457288 | tf_op jit(solution)/shard_map/ppermute | solution.py:341
  20.9 29.5 %all-to-all-start = ((bf16[64,80,128]{2,1,0:T(8,128)(2,1)}), bf16[64,80,128]{2,1,0:T(8,128)(2,1)S(1)}, u32[]{:S(2)}, u32[]{:S(2)}) async-start(bf16[64,80,128]{2,1,0:T(8,128)(2,1)} %broadcast_select_fusion), calls=%async_computation | async-start | bytes 2621440 | tf_op jit(solution)/shard_map/all_to_all | solution.py:322
  32.6 19.7 %copy-start.5 = (f32[1024]{0:T(1024)S(1)}, f32[1024]{0:T(1024)}, u32[]{:S(2)}) copy-start(f32[1024]{0:T(1024)} %param.10) | copy-start | bytes 12292
  32.6 19.7 %copy-start.6 = (f32[1024]{0:T(1024)S(1)}, f32[1024]{0:T(1024)}, u32[]{:S(2)}) copy-start(f32[1024]{0:T(1024)} %param.11) | copy-start | bytes 12292
  32.7 1.3 collective-permute-start
  52.2 2.0 collective-permute-start.2
  55.0 15.8 %all-to-all-start.1 = ((bf16[64,24,128]{2,1,0:T(8,128)(2,1)}), bf16[64,24,128]{2,1,0:T(8,128)(2,1)S(1)}, u32[]{:S(2)}, u32[]{:S(2)}) async-start(bf16[64,24,128]{2,1,0:T(8,128)(2,1)} %fusion.1), calls=%async_computation.1 | async-start | bytes 786432 | tf_op jit(solution)/shard_map/all_to_all | solution.py:322
  75.9 23.9 %all-to-all-start.2 = ((bf16[64,80,128]{2,1,0:T(8,128)(2,1)}), bf16[64,80,128]{2,1,0:T(8,128)(2,1)S(1)}, u32[]{:S(2)}, u32[]{:S(2)}) async-start(bf16[64,80,128]{2,1,0:T(8,128)(2,1)} %split_products.1), calls=%async_computation.2 | async-start | bytes 2621440 | tf_op jit(solution)/shard_map/all_to_all | solution.py:322
  101.6 5.5 %collective-permute-start.4 = (f32[128,8,128]{2,1,0:T(8,128)S(1)}, f32[128,8,128]{2,1,0:T(8,128)S(1)}, u32[]{:S(2)}, u32[]{:S(2)}) collective-permute-start(f32[128,8,128]{2,1,0:T(8,128)S(1)} %add_up.3.mine), channel_id=1, source_target_pairs={{0,64},{64,0},{1,65},{65,1},{2,66},{66,2},{3,67},{67,3},{4,68},{68... | collective-permute-start | bytes 1572872 | tf_op jit(solution)/shard_map/ppermute | solution.py:344
  138.3 4.0 %collective-permute-start.5 = (f32[2,512,128]{2,1,0:T(8,128)S(1)}, f32[2,512,128]{2,1,0:T(8,128)S(1)}, u32[]{:S(2)}, u32[]{:S(2)}) collective-permute-start(f32[2,512,128]{2,1,0:T(8,128)S(1)} %split_backward.1), channel_id=1, source_target_pairs={{0,64},{64,0},{1,65},{65,1},{2,66},{66,2},{3,67},{67,3},{4,68},{68... | collective-permute-start | bytes 1572872 | tf_op jit(solution)/shard_map/ppermute | solution.py:344
  158.7 30.5 %copy-start.1 = (bf16[128,1024]{1,0:T(8,128)(2,1)S(1)}, bf16[128,1024]{1,0:T(8,128)(2,1)}, u32[]{:S(2)}) copy-start(bf16[128,1024]{1,0:T(8,128)(2,1)} %x.5) | copy-start | bytes 786436
  158.7 23.5 %all-to-all-start.5 = ((bf16[64,80,128]{2,1,0:T(8,128)(2,1)}), bf16[64,80,128]{2,1,0:T(8,128)(2,1)S(1)}, u32[]{:S(2)}, u32[]{:S(2)}) async-start(bf16[64,80,128]{2,1,0:T(8,128)(2,1)} %hand_out.1), calls=%async_computation.5 | async-start | bytes 2621440 | tf_op jit(solution)/shard_map/all_to_all | solution.py:322
  163.7 25.7 %collective-permute-start.7 = (bf16[64,80,128]{2,1,0:T(8,128)(2,1)S(1)}, bf16[64,80,128]{2,1,0:T(8,128)(2,1)}, u32[]{:S(2)}, u32[]{:S(2)}) collective-permute-start(bf16[64,80,128]{2,1,0:T(8,128)(2,1)S(1)} %all_to_all.30.grads.grads1), channel_id=1, source_target_pairs={{0,64},{1,65},{2,66},{3,67},{4,68},{5,69},{6,70},{7,71},{8,72},{9,... | collective-permute-start | bytes 3932168 | tf_op jit(solution)/shard_map/ppermute | solution.py:341
  182.2 14.9 %collective-permute-start.6 = (bf16[64,80,128]{2,1,0:T(8,128)(2,1)S(1)}, bf16[64,80,128]{2,1,0:T(8,128)(2,1)}, u32[]{:S(2)}, u32[]{:S(2)}) collective-permute-start(bf16[64,80,128]{2,1,0:T(8,128)(2,1)S(1)} %all-to-all-done.5.grads0), channel_id=1, source_target_pairs={{64,0},{65,1},{66,2},{67,3},{68,4},{69,5},{70,6},{71,7},{72,8},{73... | collective-permute-start | bytes 3932168 | tf_op jit(solution)/shard_map/ppermute | solution.py:341

commit v3 on v2

--- a/solution.py
+++ b/solution.py
@@ -11,6 +11,7 @@
 SLICE = 8
 VMEM_LIMIT = 16 * 1024 * 1024
 STREAM_LIMIT = 48 * 1024 * 1024
+PASSING_LIMIT = 45 * 1024 * 1024
 
 
 def params(limit=VMEM_LIMIT):
@@ -39,35 +40,68 @@
         product = jnp.dot(picked, tiles[2 * pair + u], preferred_element_type=jnp.float32)
         parts.append(product.T.reshape(width // SLICE, SLICE, x.shape[0]))
     both = jnp.concatenate(parts, axis=1).astype(jnp.bfloat16)
-    out[:, pl.ds(pl.multiple_of(2 * SLICE * pair, 2 * SLICE), 2 * SLICE), :] = both
-
-
-def first_products_body(cols, x, tiles, out, held, sems, *, first):
+    out[:, 2 * SLICE * pair : 2 * SLICE * (pair + 1), :] = both
+
+
+def first_products_body(
+    cols_in, x_in, tiles, out, *rest, first
+):
+    *low, cols, x, small_sems, held, sems, low_sems = rest
     pairs = held.shape[0] // 2
     copy = tile_copies(tiles, first, held, sems)
+    cols_copy = pltpu.make_async_copy(cols_in, cols, small_sems.at[0])
+    x_copy = pltpu.make_async_copy(x_in, x, small_sems.at[1])
+    cols_copy.start()
+    x_copy.start()
     for k in range(pairs):
         copy(k).start()
-
-    @pl.loop(0, pairs)
-    def _(k):
-        copy(k).wait()
-        product_pair(cols, first, x, held, out, k)
-
-
-def first_products(cols, x, tiles, first, count):
+    cols_copy.wait()
+    x_copy.wait()
+
+    def multiply():
+        for k in range(pairs):
+            copy(k).wait()
+            product_pair(cols.at[0], first, x, held, out, k)
+
+    if not low:
+        multiply()
+        return
+    core = lax.axis_index("phase")
+    pl.when(core == 0)(multiply)
+
+    @pl.when(core == 1)
+    def _():
+        def put(k):
+            return pltpu.make_async_copy(
+                held.at[pl.ds(2 * k, 2)], low[0].at[pl.ds(2 * k, 2)], low_sems.at[k]
+            )
+
+        for k in range(pairs):
+            copy(k).wait()
+            put(k).start()
+        for k in range(pairs):
+            put(k).wait()
+
+
+def first_products(cols, x, tiles, first, count, keep):
     width = tiles.shape[1]
     scen = x.shape[0]
     vmem = pl.BlockSpec(memory_space=pltpu.VMEM)
+    hbm = pl.BlockSpec(memory_space=pl.ANY)
+    out = jax.ShapeDtypeStruct((width // SLICE, count * SLICE, scen), jnp.bfloat16)
+    low = jax.ShapeDtypeStruct((count, width, width), jnp.bfloat16)
     return pl.pallas_call(
         functools.partial(first_products_body, first=first),
-        in_specs=[
-            pl.BlockSpec(memory_space=pltpu.SMEM),
-            vmem,
-            pl.BlockSpec(memory_space=pl.ANY),
-        ],
-        out_specs=vmem,
-        out_shape=jax.ShapeDtypeStruct((width // SLICE, count * SLICE, scen), jnp.bfloat16),
-        scratch_shapes=tile_scratch(count, width),
+        in_specs=[hbm, hbm, hbm],
+        out_specs=[vmem, hbm] if keep else vmem,
+        out_shape=[out, low] if keep else out,
+        scratch_shapes=[
+            pltpu.SMEM(cols.shape, jnp.int32),
+            pltpu.VMEM(x.shape, jnp.bfloat16),
+            pltpu.SemaphoreType.DMA((2,)),
+        ]
+        + tile_scratch(count, width)
+        + [pltpu.SemaphoreType.DMA((count // 2,))],
         compiler_params=params(STREAM_LIMIT),
         name="first_products",
     )(cols, x, tiles)
@@ -89,43 +123,55 @@
     return tile_copies(received, 0, held, sems)
 
 
-def split_products_body(meta, x, received, tiles, out, held, sems):
+def split_products_body(meta, x, received, tiles, out, held, sems, stage, out_sems):
+    pairs = held.shape[0] // 2
     copy = start_split_tiles(meta[0], received, tiles, held, sems)
 
-    @pl.loop(0, held.shape[0] // 2)
-    def _(k):
+    def put(k):
+        rows = slice(2 * SLICE * k, 2 * SLICE * (k + 1))
+        return pltpu.make_async_copy(stage.at[:, rows], out.at[:, rows], out_sems.at[k])
+
+    for k in range(pairs):
         copy(k).wait()
-        product_pair(meta, 1, x, held, out, k)
+        product_pair(meta, 1, x, held, stage, k)
+        put(k).start()
+    for k in range(pairs):
+        put(k).wait()
 
 
 def split_products(meta, x, received, tiles):
-    count, width = received.shape[0] // 2, received.shape[1]
-    scen = x.shape[0]
+    count, width = received.shape[0], received.shape[1]
+    out_shape = (width // SLICE, count * SLICE, x.shape[0])
     vmem = pl.BlockSpec(memory_space=pltpu.VMEM)
     hbm = pl.BlockSpec(memory_space=pl.ANY)
     return pl.pallas_call(
         split_products_body,
         in_specs=[pl.BlockSpec(memory_space=pltpu.SMEM), vmem, hbm, hbm],
-        out_specs=vmem,
-        out_shape=jax.ShapeDtypeStruct((width // SLICE, count * SLICE, scen), jnp.bfloat16),
-        scratch_shapes=tile_scratch(count, width),
+        out_specs=hbm,
+        out_shape=jax.ShapeDtypeStruct(out_shape, jnp.bfloat16),
+        scratch_shapes=tile_scratch(count, width)
+        + [pltpu.VMEM(out_shape, jnp.bfloat16), pltpu.SemaphoreType.DMA((count // 2,))],
         compiler_params=params(STREAM_LIMIT),
         name="split_products",
     )(meta, x, received, tiles)
 
 
-def add_up_body(idx, data, out, *, count):
+def add_up_body(idx, data, out, second, *, count):
     out[...] = jnp.zeros_like(out)
-
-    @pl.loop(0, data.shape[0])
+    second[...] = jnp.zeros_like(second)
+
+    @pl.loop(0, data.shape[0], step=2)
     def _(i):
-        values = data[i].astype(jnp.float32)
-        places = [idx[i * count + t] for t in range(count)]
-        sums = [
-            out[places[t]] + values[t * SLICE : (t + 1) * SLICE] for t in range(count)
-        ]
-        for t in range(count):
-            out[places[t]] = sums[t]
+        for holder, total in ((i, out), (i + 1, second)):
+            values = data[holder].astype(jnp.float32)
+            places = [idx[holder * count + t] for t in range(count)]
+            sums = [
+                total[places[t]] + values[t * SLICE : (t + 1) * SLICE] for t in range(count)
+            ]
+            for t in range(count):
+                total[places[t]] = sums[t]
+
+    out[...] += second[...]
 
 
 def add_up(idx, data, blocks):
@@ -135,24 +181,26 @@
         in_specs=[pl.BlockSpec(memory_space=pltpu.SMEM), pl.BlockSpec(memory_space=pltpu.VMEM)],
         out_specs=pl.BlockSpec(memory_space=pltpu.VMEM),
         out_shape=jax.ShapeDtypeStruct((blocks, SLICE, data.shape[2]), jnp.float32),
+        scratch_shapes=[pltpu.VMEM((blocks, SLICE, data.shape[2]), jnp.float32)],
         compiler_params=params(),
         name="add_up",
     )(idx, data)
 
 
 def hand_out(idx, held, out, count):
-    @pl.loop(0, out.shape[0])
+    @pl.loop(0, out.shape[0], step=4)
     def _(i):
-        for t in range(0, count, 2):
-            pair = [held[idx[i * count + t]], held[idx[i * count + t + 1]]]
-            rows = jnp.concatenate(pair, axis=0).astype(jnp.bfloat16)
-            out[i, t * SLICE : (t + 2) * SLICE, :] = rows
+        for holder in (i, i + 1, i + 2, i + 3):
+            for t in range(0, count, 2):
+                pair = [held[idx[holder * count + t]], held[idx[holder * count + t + 1]]]
+                rows = jnp.concatenate(pair, axis=0).astype(jnp.bfloat16)
+                out[holder, t * SLICE : (t + 2) * SLICE, :] = rows
 
 
 def value_and_hand_out_body(idx, mine, other, notional, strike, out, held, *, count, weight):
-    @pl.loop(0, held.shape[0], step=8)
+    @pl.loop(0, held.shape[0], step=32)
     def _(b):
-        for k in range(8):
+        for k in range(32):
             moneyness = mine[b + k] + other[b + k]
             held[b + k] = notional[b + k] * jax.nn.sigmoid(moneyness - strike[b + k]) * weight
 
@@ -194,8 +242,7 @@
 
 
 def tile_grad_pair(grads, pair):
-    rows = grads[:, pl.ds(pl.multiple_of(pair * 2 * SLICE, 2 * SLICE), 2 * SLICE), :]
-    rows = rows.astype(jnp.float32)
+    rows = grads[:, 2 * SLICE * pair : 2 * SLICE * (pair + 1), :].astype(jnp.float32)
     width = rows.shape[0] * SLICE
     return [
         rows[:, u * SLICE : (u + 1) * SLICE, :].reshape(width, -1).astype(jnp.bfloat16)
@@ -207,8 +254,7 @@
     copy = start_split_tiles(meta[0], received, tiles, held, sems)
     total[...] = jnp.zeros_like(total)
 
-    @pl.loop(0, held.shape[0] // 2)
-    def _(k):
+    for k in range(held.shape[0] // 2):
         copy(k).wait()
         for u, grad in enumerate(tile_grad_pair(grads, k)):
             product = jnp.dot(held[2 * k + u], grad, preferred_element_type=jnp.float32)
@@ -216,7 +262,7 @@
 
 
 def split_backward(meta, grads, received, tiles, blocks_dev):
-    count, width = received.shape[0] // 2, received.shape[1]
+    count, width = received.shape[0], received.shape[1]
     vmem = pl.BlockSpec(memory_space=pltpu.VMEM)
     hbm = pl.BlockSpec(memory_space=pl.ANY)
     return pl.pallas_call(
@@ -231,82 +277,112 @@
 
 
 def last_backward_body(meta, grads0, grads1, inputs, tiles, *rest, first):
-    earlier = rest[:2] if first else ()
-    sens, result, grads, total, stage, out_sems, held, sems = rest[len(earlier) :]
-    pairs = held.shape[0] // 2
-    take = tile_copies(tiles, first, held, sems)
-    for k in range(pairs):
-        take(k).start()
+    if first:
+        earlier, _, sens, adjoint_out, grads, grads_sems, stage, out_sems, *more = rest
+        total, adjoint, adjoint_sem = more
+        held = tiles
+    else:
+        sens, total, following, grads, grads_sems, stage, out_sems, held, sems, next_sems = rest
+
+    pairs = stage.shape[0]
+
+    def grads_copy(source, k):
+        rows = slice(2 * SLICE * k, 2 * SLICE * (k + 1))
+        return pltpu.make_async_copy(source.at[:, rows], grads.at[:, rows], grads_sems.at[k])
 
     @pl.when(meta[0] == 0)
     def _():
-        grads[...] = grads0[...]
+        for k in range(pairs):
+            grads_copy(grads0, k).start()
 
     @pl.when(meta[0] == 1)
     def _():
-        grads[...] = grads1[...]
-
-    total[...] = earlier[0][...] if earlier else jnp.zeros_like(total)
+        for k in range(pairs):
+            grads_copy(grads1, k).start()
+
+    if not first:
+        take = tile_copies(tiles, 0, held, sems)
+        take_next = tile_copies(tiles, held.shape[0], following, next_sems)
+        for k in range(held.shape[0] // 2):
+            take(k).start()
+        for k in range(held.shape[0] // 2):
+            take_next(k).start()
+
+    total[...] = earlier[...] if first else jnp.zeros_like(total)
 
     def put(k):
-        slot = lax.rem(k, 2)
         return pltpu.make_async_copy(
-            stage.at[slot], sens.at[pl.ds(first + 2 * k, 2)], out_sems.at[slot]
+            stage.at[k // 2, k % 2], sens.at[first + k], out_sems.at[k]
         )
 
-    @pl.loop(0, pairs)
-    def _(k):
-        @pl.when(k >= 2)
-        def _():
-            put(k - 2).wait()
-
-        take(k).wait()
-        slot = lax.rem(k, 2)
+    for k in range(pairs):
+        if not first:
+            take(k).wait()
+        grads_copy(grads0, k).wait()
         for u, grad in enumerate(tile_grad_pair(grads, k)):
             col = meta[1 + first + 2 * k + u]
             total[col] += jnp.dot(held[2 * k + u], grad, preferred_element_type=jnp.float32)
-            stage[slot, u] = lax.dot_general(
+            stage[k, u] = lax.dot_general(
                 inputs[col], grad, (((1,), (1,)), ((), ())), preferred_element_type=jnp.float32
             ).astype(jnp.bfloat16)
-        put(k).start()
-
-    if earlier:
+            put(2 * k + u).start()
+
+    if first:
         width = total.shape[1]
         for c in range(total.shape[0]):
-            result[:, c * width : (c + 1) * width] = total[c].T.astype(jnp.bfloat16)
+            adjoint[:, c * width : (c + 1) * width] = total[c].T.astype(jnp.bfloat16)
+        adjoint_copy = pltpu.make_async_copy(adjoint, adjoint_out, adjoint_sem)
+        adjoint_copy.start()
+        adjoint_copy.wait()
     else:
-        result[...] = total[...]
-    for k in range(max(pairs - 2, 0), pairs):
+        for k in range(pairs):
+            take_next(k).wait()
+    for k in range(2 * pairs):
         put(k).wait()
 
 
-def last_backward(meta, grads0, grads1, inputs, tiles, first, count, earlier=()):
+def last_backward_calls(meta, grads, inputs, tiles):
     slots, width, _ = tiles.shape
+    half = slots // 2
     blocks_dev, _, scen = inputs.shape
+    smem = pl.BlockSpec(memory_space=pltpu.SMEM)
     vmem = pl.BlockSpec(memory_space=pltpu.VMEM)
     hbm = pl.BlockSpec(memory_space=pl.ANY)
-    result = (
-        jax.ShapeDtypeStruct((scen, blocks_dev * width), jnp.bfloat16)
-        if earlier
-        else jax.ShapeDtypeStruct(inputs.shape, jnp.float32)
-    )
-    return pl.pallas_call(
-        functools.partial(last_backward_body, first=first),
-        in_specs=[pl.BlockSpec(memory_space=pltpu.SMEM), vmem, vmem, vmem, hbm]
-        + [vmem, hbm][: len(earlier)],
-        out_specs=[hbm, vmem],
-        out_shape=[jax.ShapeDtypeStruct((slots, width, width), jnp.bfloat16), result],
+    sens_shape = jax.ShapeDtypeStruct((slots, width, width), jnp.bfloat16)
+    total_shape = jax.ShapeDtypeStruct(inputs.shape, jnp.float32)
+    half_shape = jax.ShapeDtypeStruct((half, width, width), jnp.bfloat16)
+    sems = pltpu.SemaphoreType.DMA((half // 2,))
+    scratch = [
+        pltpu.VMEM(grads[0][0].shape, jnp.bfloat16),
+        sems,
+        pltpu.VMEM((half // 2, 2, width, width), jnp.bfloat16),
+        pltpu.SemaphoreType.DMA((half,)),
+    ]
+    adjoint_shape = (scen, blocks_dev * width)
+    sens, total, high_tiles = pl.pallas_call(
+        functools.partial(last_backward_body, first=0),
+        in_specs=[smem, hbm, hbm, vmem, hbm],
+        out_specs=[hbm, vmem, vmem],
+        out_shape=[sens_shape, total_shape, half_shape],
+        scratch_shapes=[*scratch, *tile_scratch(half, width), sems],
+        compiler_params=params(PASSING_LIMIT),
+        name="last_backward_low",
+    )(meta, *grads[0], inputs, tiles)
+    return pl.pallas_call(
+        functools.partial(last_backward_body, first=half),
+        in_specs=[smem, hbm, hbm, vmem, vmem, vmem, hbm],
+        out_specs=[hbm, hbm],
+        out_shape=[sens_shape, jax.ShapeDtypeStruct(adjoint_shape, jnp.bfloat16)],
         scratch_shapes=[
-            pltpu.VMEM(grads0.shape, jnp.bfloat16),
+            *scratch,
             pltpu.VMEM(inputs.shape, jnp.float32),
-            pltpu.VMEM((2, 2, width, width), jnp.bfloat16),
-            pltpu.SemaphoreType.DMA((2,)),
-        ]
-        + tile_scratch(count, width),
-        input_output_aliases={6: 0} if earlier else {},
-        compiler_params=params(STREAM_LIMIT),
-        name="last_backward",
-    )(meta, grads0, grads1, inputs, tiles, *earlier)
+            pltpu.VMEM(adjoint_shape, jnp.bfloat16),
+            pltpu.SemaphoreType.DMA,
+        ],
+        input_output_aliases={6: 0},
+        compiler_params=params(),
+        name="last_backward_high",
+    )(meta, *grads[1], inputs, high_tiles, total, sens)
 
 
 def three_terms(values):
@@ -354,13 +430,13 @@
     split_meta = jnp.concatenate([my_number, of_core(places[1][-slots:-half], cols[half:])])
     meta = jnp.concatenate([my_number, cols])
 
-    sent = first_products(cols, normals, tiles, half, half)
-    kept = first_products(cols, normals, tiles, 0, half)
-    outgoing, tiles_now = lax.optimization_barrier((of_core(kept, send(sent, 0)), tiles))
-    received = send(tiles_now, 1)
-    arrived = exchange(outgoing)
+    sent = first_products(tile_col, normals, tiles, half, half, False)
+    kept, low_tiles = first_products(tile_col, normals, tiles, 0, half, True)
+    arrived = exchange(of_core(kept, send(sent, 0)))
     part = add_up(split_rows[0], arrived, blocks)
-    shock_slices = (part + swap(part)).astype(jnp.bfloat16)
+    other_part, low_tiles = lax.optimization_barrier((swap(part), low_tiles))
+    received = send(low_tiles, 1)
+    shock_slices = (part + other_part).astype(jnp.bfloat16)
 
     scales = jnp.stack([three_terms(notional), three_terms(strike)])
     scales = scales.reshape(6, blocks_dev, shards, SLICE).transpose(2, 0, 1, 3)
@@ -394,8 +470,9 @@
 
     normals_held = normals.reshape(scen, blocks_dev, width).transpose(1, 2, 0)
     inputs = of_core(normals_held, shocks)
-    sens, part = last_backward(meta, low0, low1, inputs, tiles, 0, half)
-    sens, adjoint = last_backward(meta, high0, high1, inputs, tiles, half, half, (part, sens))
+    sens, adjoint = last_backward_calls(
+        meta, ((low0, low1), (high0, high1)), inputs, tiles
+    )
     return sens[None], adjoint[None]
 
 

time: 206 us -> 202 us (0.981)
  Pallas kernels: 41.7 us -> 36.6 us
  starting transfers between devices: 48.9 us -> 44.7 us
  waiting for transfers between devices: 67.2 us -> 71.2 us
    all_to_all x4, waiting for transfers between devices: 63 us -> 67 us  [exchange(): return lax.all_to_all(block, 'blk', split_axis=0, concat_axis=0, tiled=True)]
    pallas_call x2, Pallas kernels: 16 us -> 12.7 us  [the longest x1 7.45 us: last_backward_calls(): pl.pallas_call(functools.partial(last_backward_body, first=0), in_specs=[...]
    ppermute x4, starting transfers between devices: 16.5 us -> 14.1 us  [send(): return lax.ppermute(block, 'phase', [(source, 1 - source)])]
    ppermute x4, starting transfers between devices: 6.2 us -> 4.05 us  [swap(): return lax.ppermute(block, 'phase', [(0, 1), (1, 0)])]
  transfers between devices with their start and end apart: 12 -> 12, of which waited for: 8 -> 7; matrix products, arithmetic and copies ran while one was open for 2% -> 2% of each run, Pallas kernels for 6% -> 6%
where the time goes in v3:
time: 202 us; the launch traced here: 201 us
  waiting for transfers between devices  71.2 us (35%)
  starting transfers between devices  44.7 us (22%)
  blocking collectives  38.4 us (19%)
  Pallas kernels  36.6 us (18%)
  local copies, waits for them, and re-layouts  4.91 us (2%)
  other arithmetic  4.11 us (2%)
    all_to_all x4, waiting for transfers between devices, exchange(): return lax.all_to_all(block, 'blk', split_axis=0, concat_axis=0, tiled=True)  67 us
    all_to_all x2, blocking collectives, exchange(): return lax.all_to_all(block, 'blk', split_axis=0, concat_axis=0, tiled=True)  38.4 us
    all_to_all x4, starting transfers between devices, exchange(): return lax.all_to_all(block, 'blk', split_axis=0, concat_axis=0, tiled=True)  26.6 us
    ppermute x4, starting transfers between devices, send(): return lax.ppermute(block, 'phase', [(source, 1 - source)])  14.1 us
    pallas_call x2, Pallas kernels, first_products(): pl.pallas_call(functools.partial(first_products_body, first=first), in_sp...  7.7 us
    pallas_call x1, Pallas kernels, last_backward_calls(): pl.pallas_call(functools.partial(last_backward_body, first=0), in_specs=[...  7.45 us
    pallas_call x1, Pallas kernels, last_backward_calls(): pl.pallas_call(functools.partial(last_backward_body, first=half), in_spec...  5.28 us
    pallas_call x1, Pallas kernels, split_products(): pl.pallas_call(split_products_body, in_specs=[pl.BlockSpec(memory_space=p...  4.5 us
  transfers between devices with their start and end apart: 12, of which 7 were waited for; matrix products, arithmetic and copies ran while one was open for 2% of the time, Pallas kernels for 6%

profile of v3, /device:TPU:1, one launch (start us, length us, event | category | flops | bytes accessed | tf_op | source)
XLA Modules:
  0.0 201.2 jit_solution(14458883675079703148)
XLA Ops:
  0.6 0.9 copy-done
  1.6 0.7 copy-done.2
  2.2 3.3 %first_products.3 = bf16[64,80,128]{2,1,0:T(8,128)(2,1)S(1)} custom-call(s32[1,20]{1,0:T(1,128)S(1)} %copy-done.2, bf16[128,1024]{1,0:T(8,128)(2,1)S(1)} %copy-done, bf16[20,512,512]{2,1,0:T(8,128)(2,1)} %bitcast.47), custom_call_target="tpu_custom_call" | custom-call | tf_op jit(solution)/shard_map/first_products/pallas_call | solution.py:93
  5.5 1.3 collective-permute-start.1
  6.8 4.4 %first_products.2 = (bf16[64,80,128]{2,1,0:T(8,128)(2,1)S(1)}, bf16[10,512,512]{2,1,0:T(8,128)(2,1)}) custom-call(s32[1,20]{1,0:T(1,128)S(1)} %copy-done.2, bf16[128,1024]{1,0:T(8,128)(2,1)S(1)} %copy-done, bf16[20,512,512]{2,1,0:T(8,128)(2,1)} %bitcast.48), custom_call_target="tpu_custom_call" | custom-call | tf_op jit(solution)/shard_map/first_products/pallas_call | solution.py:93
  11.3 2.6 %broadcast_select_fusion = bf16[64,80,128]{2,1,0:T(8,128)(2,1)} fusion(bf16[64,80,128]{2,1,0:T(8,128)(2,1)S(1)} %get-tuple-element.11, bf16[64,80,128]{2,1,0:T(8,128)(2,1)} %collective-permute-done.1, pred[]{:T(512)S(6)} %eq.2), kind=kLoop, calls=%fused_computation | loop fusion | flops 655360 | bytes 3932161 | tf_op jit(solution)/shard_map/jit(_where)/select_n | solution.py:414
  13.9 12.1 %all-to-all-start = ((bf16[64,80,128]{2,1,0:T(8,128)(2,1)}), bf16[64,80,128]{2,1,0:T(8,128)(2,1)S(1)}, u32[]{:S(2)}, u32[]{:S(2)}) async-start(bf16[64,80,128]{2,1,0:T(8,128)(2,1)} %broadcast_select_fusion), calls=%async_computation | async-start | bytes 2621440 | tf_op jit(solution)/shard_map/all_to_all | solution.py:398
  26.1 0.1 collective-permute-start
  26.2 1.1 collective-permute-done
  27.3 0.1 slice.71
  27.5 0.1 reshape.77.idx
  27.6 19.2 %all-to-all-done.data = bf16[64,80,128]{2,1,0:T(8,128)(2,1)S(1)} async-done(((bf16[64,80,128]{2,1,0:T(8,128)(2,1)}), bf16[64,80,128]{2,1,0:T(8,128)(2,1)S(1)}, u32[]{:S(2)}, u32[]{:S(2)}) %all-to-all-start) | async-done | bytes 1310752 | tf_op jit(solution)/shard_map/all_to_all | solution.py:398
  46.9 1.7 add_up.2
  48.6 1.3 collective-permute-start.2
  49.9 1.5 collective-permute-done.2
  51.4 4.6 %collective-permute-start.3 = (bf16[10,512,512]{2,1,0:T(8,128)(2,1)}, bf16[10,512,512]{2,1,0:T(8,128)(2,1)}, u32[]{:S(2)}, u32[]{:S(2)}) collective-permute-start(bf16[10,512,512]{2,1,0:T(8,128)(2,1)} %get-tuple-element.14), channel_id=1, source_target_pairs={{64,0},{65,1},{66,2},{67,3},{68,4},{69,5},{70,6},{71,7},{72,8},{73... | collective-permute-start | bytes 15728648 | tf_op jit(solution)/shard_map/ppermute | solution.py:417
  56.2 0.3 convert_element_type.34
  56.5 0.1 copy.36
  56.6 0.1 copy.49
  56.8 0.8 fusion.1
  57.6 4.8 %all-to-all-start.1 = ((bf16[64,24,128]{2,1,0:T(8,128)(2,1)}), bf16[64,24,128]{2,1,0:T(8,128)(2,1)S(1)}, u32[]{:S(2)}, u32[]{:S(2)}) async-start(bf16[64,24,128]{2,1,0:T(8,128)(2,1)} %fusion.1), calls=%async_computation.1 | async-start | bytes 786432 | tf_op jit(solution)/shard_map/all_to_all | solution.py:398
  62.5 9.9 %all-to-all-done.1 = bf16[64,24,128]{2,1,0:T(8,128)(2,1)S(1)} async-done(((bf16[64,24,128]{2,1,0:T(8,128)(2,1)}), bf16[64,24,128]{2,1,0:T(8,128)(2,1)S(1)}, u32[]{:S(2)}, u32[]{:S(2)}) %all-to-all-start.1) | async-done | bytes 393248 | tf_op jit(solution)/shard_map/all_to_all | solution.py:398
  72.5 0.1 copy.39.x
  72.7 4.5 %split_products.1 = bf16[64,80,128]{2,1,0:T(8,128)(2,1)} custom-call(s32[11]{0:T(128)S(1)} %pad_add_fusion.2.meta, bf16[128,1024]{1,0:T(8,128)(2,1)S(1)} %copy.39.x, bf16[10,512,512]{2,1,0:T(8,128)(2,1)} %collective-permute-done.3.received, bf16[20,512,512]{2,1,0:T(8,128)(2,1)} %bitcast.49), custom_call_target="tpu_custom_call" | custom-call | tf_op jit(solution)/shard_map/split_products/pallas_call | solution.py:147
  77.2 4.7 %all-to-all-start.2 = ((bf16[64,80,128]{2,1,0:T(8,128)(2,1)}), bf16[64,80,128]{2,1,0:T(8,128)(2,1)S(1)}, u32[]{:S(2)}, u32[]{:S(2)}) async-start(bf16[64,80,128]{2,1,0:T(8,128)(2,1)} %split_products.1), calls=%async_computation.2 | async-start | bytes 2621440 | tf_op jit(solution)/shard_map/all_to_all | solution.py:398
  81.9 0.1 slice.78
  82.0 0.1 reshape.78.idx
  82.2 20.6 %all-to-all-done.2.data = bf16[64,80,128]{2,1,0:T(8,128)(2,1)S(1)} async-done(((bf16[64,80,128]{2,1,0:T(8,128)(2,1)}), bf16[64,80,128]{2,1,0:T(8,128)(2,1)S(1)}, u32[]{:S(2)}, u32[]{:S(2)}) %all-to-all-start.2) | async-done | bytes 1310752 | tf_op jit(solution)/shard_map/all_to_all | solution.py:398
  102.9 1.6 add_up.3.mine
  104.5 0.1 collective-permute-start.4
  104.7 0.1 copy.43
  104.8 0.1 copy.42
  104.9 0.8 copy.44.notional
  105.8 0.8 copy.45.strike
  106.6 1.9 value_and_hand_out.1
  108.5 24.9 %all_to_all.30.grads.grads1 = bf16[64,80,128]{2,1,0:T(8,128)(2,1)S(1)} all-to-all(bf16[64,80,128]{2,1,0:T(8,128)(2,1)S(1)} %value_and_hand_out.1), channel_id=1, replica_groups=mesh['phase'=2,'blk'=64] {'blk'}, dimensions={0} | all-to-all | bytes 2621440 | tf_op jit(solution)/shard_map/all_to_all | solution.py:398
  133.4 4.0 %split_backward.1 = f32[2,512,128]{2,1,0:T(8,128)S(1)} custom-call(s32[11]{0:T(128)S(1)} %pad_add_fusion.2.meta, bf16[64,80,128]{2,1,0:T(8,128)(2,1)S(1)} %all_to_all.30.grads.grads1, bf16[10,512,512]{2,1,0:T(8,128)(2,1)} %collective-permute-done.3.received, bf16[20,512,512]{2,1,0:T(8,128)(2,1)} %bitcast.50), custom_call_target="tpu_custom_call" | custom-call | tf_op jit(solution)/shard_map/split_backward/pallas_call | solution.py:268
  137.4 2.5 %collective-permute-start.5 = (f32[2,512,128]{2,1,0:T(8,128)S(1)}, f32[2,512,128]{2,1,0:T(8,128)S(1)}, u32[]{:S(2)}, u32[]{:S(2)}) collective-permute-start(f32[2,512,128]{2,1,0:T(8,128)S(1)} %split_backward.1), channel_id=1, source_target_pairs={{0,64},{64,0},{1,65},{65,1},{2,66},{66,2},{3,67},{67,3},{4,68},{68... | collective-permute-start | bytes 1572872 | tf_op jit(solution)/shard_map/ppermute | solution.py:420
  139.9 1.5 collective-permute-done.5
  141.5 13.5 %all_to_all.31.blocks = bf16[64,16,128]{2,1,0:T(8,128)(2,1)S(1)} all-to-all(bf16[64,16,128]{2,1,0:T(8,128)(2,1)S(1)} %copy_bitcast_fusion), channel_id=1, replica_groups=mesh['phase'=2,'blk'=64] {'blk'}, dimensions={0} | all-to-all | bytes 524288 | tf_op jit(solution)/shard_map/all_to_all | solution.py:398
  155.0 2.4 %hand_out.1 = bf16[64,80,128]{2,1,0:T(8,128)(2,1)} custom-call(s32[640]{0:T(1024)S(1)} %reshape.77.idx, bf16[64,16,128]{2,1,0:T(8,128)(2,1)S(1)} %all_to_all.31.blocks), custom_call_target="tpu_custom_call" | custom-call | tf_op jit(solution)/shard_map/hand_out/pallas_call | solution.py:233
  157.4 5.0 %all-to-all-start.5 = ((bf16[64,80,128]{2,1,0:T(8,128)(2,1)}), bf16[64,80,128]{2,1,0:T(8,128)(2,1)S(1)}, u32[]{:S(2)}, u32[]{:S(2)}) async-start(bf16[64,80,128]{2,1,0:T(8,128)(2,1)} %hand_out.1), calls=%async_computation.5 | async-start | bytes 2621440 | tf_op jit(solution)/shard_map/all_to_all | solution.py:398
  162.5 1.3 collective-permute-start.7
  163.8 17.2 %all-to-all-done.5.grads0 = bf16[64,80,128]{2,1,0:T(8,128)(2,1)S(1)} async-done(((bf16[64,80,128]{2,1,0:T(8,128)(2,1)}), bf16[64,80,128]{2,1,0:T(8,128)(2,1)S(1)}, u32[]{:S(2)}, u32[]{:S(2)}) %all-to-all-start.5) | async-done | bytes 1310752 | tf_op jit(solution)/shard_map/all_to_all | solution.py:398
  181.0 6.9 %collective-permute-start.6 = (bf16[64,80,128]{2,1,0:T(8,128)(2,1)S(1)}, bf16[64,80,128]{2,1,0:T(8,128)(2,1)}, u32[]{:S(2)}, u32[]{:S(2)}) collective-permute-start(bf16[64,80,128]{2,1,0:T(8,128)(2,1)S(1)} %all-to-all-done.5.grads0), channel_id=1, source_target_pairs={{64,0},{65,1},{66,2},{67,3},{68,4},{69,5},{70,6},{71,7},{72,8},{73... | collective-permute-start | bytes 3932168 | tf_op jit(solution)/shard_map/ppermute | solution.py:417
  187.9 0.2 copy.47
  188.3 7.5 %last_backward_low.1 = (bf16[20,512,512]{2,1,0:T(8,128)(2,1)}, f32[2,512,128]{2,1,0:T(8,128)S(1)}, bf16[10,512,512]{2,1,0:T(8,128)(2,1)S(1)}) custom-call(s32[21]{0:T(128)S(1)} %pad_add_fusion.1.meta, bf16[64,80,128]{2,1,0:T(8,128)(2,1)S(1)} %all-to-all-done.5.grads0, bf16[64,80,128]{2,1,0:T(8,128)(2,1)} %collective-permute-done.7.grads1, ...), custom_call_target="tpu_custom_call" | custom-call | tf_op jit(solution)/shard_map/last_backward_low/pallas_call | solution.py:362
  195.7 5.3 %last_backward_high.1 = (bf16[20,512,512]{2,1,0:T(8,128)(2,1)}, bf16[128,1024]{1,0:T(8,128)(2,1)}) custom-call(s32[21]{0:T(128)S(1)} %pad_add_fusion.1.meta, bf16[64,80,128]{2,1,0:T(8,128)(2,1)} %collective-permute-done.6.grads0, bf16[64,80,128]{2,1,0:T(8,128)(2,1)S(1)} %all_to_all.30.grads.grads1, ...), custom_call_target="tpu_custom_call", output_to_operand_aliasing={{0}: (6, {})} | custom-call | tf_op jit(solution)/shard_map/last_backward_high/pallas_call | solution.py:371
  (46 shorter events, 0.9 us)
Async XLA Ops:
  0.6 1.0 copy-start
  1.6 0.7 copy-start.2
  5.5 5.7 %collective-permute-start.1 = (bf16[64,80,128]{2,1,0:T(8,128)(2,1)S(1)}, bf16[64,80,128]{2,1,0:T(8,128)(2,1)}, u32[]{:S(2)}, u32[]{:S(2)}) collective-permute-start(bf16[64,80,128]{2,1,0:T(8,128)(2,1)S(1)} %first_products.3), channel_id=1, source_target_pairs={{0,64},{1,65},{2,66},{3,67},{4,68},{5,69},{6,70},{7,71},{8,72},{9,... | collective-permute-start | bytes 3932168 | tf_op jit(solution)/shard_map/ppermute | solution.py:417
  13.9 12.1 %copy-start.4 = (s32[1,1280]{1,0:T(1,128)S(1)}, s32[1,1280]{1,0:T(1,128)}, u32[]{:S(2)}) copy-start(s32[1,1280]{1,0:T(1,128)} %param.8) | copy-start | bytes 15364
  13.9 12.2 %copy-start.3 = (s32[1,20]{1,0:T(1,128)S(1)}, s32[1,20]{1,0:T(1,128)}, u32[]{:S(2)}) copy-start(s32[1,20]{1,0:T(1,128)} %cols_in.3) | copy-start | bytes 244
  13.9 33.0 %all-to-all-start = ((bf16[64,80,128]{2,1,0:T(8,128)(2,1)}), bf16[64,80,128]{2,1,0:T(8,128)(2,1)S(1)}, u32[]{:S(2)}, u32[]{:S(2)}) async-start(bf16[64,80,128]{2,1,0:T(8,128)(2,1)} %broadcast_select_fusion), calls=%async_computation | async-start | bytes 2621440 | tf_op jit(solution)/shard_map/all_to_all | solution.py:398
  26.0 30.1 %copy-start.5 = (f32[1024]{0:T(1024)S(1)}, f32[1024]{0:T(1024)}, u32[]{:S(2)}) copy-start(f32[1024]{0:T(1024)} %param.10) | copy-start | bytes 12292
  26.0 30.1 %copy-start.6 = (f32[1024]{0:T(1024)S(1)}, f32[1024]{0:T(1024)}, u32[]{:S(2)}) copy-start(f32[1024]{0:T(1024)} %param.11) | copy-start | bytes 12292
  26.1 1.3 collective-permute-start
  48.6 2.9 %collective-permute-start.2 = (f32[128,8,128]{2,1,0:T(8,128)S(1)}, f32[128,8,128]{2,1,0:T(8,128)S(1)}, u32[]{:S(2)}, u32[]{:S(2)}) collective-permute-start(f32[128,8,128]{2,1,0:T(8,128)S(1)} %add_up.2), channel_id=1, source_target_pairs={{0,64},{64,0},{1,65},{65,1},{2,66},{66,2},{3,67},{67,3},{4,68},{68... | collective-permute-start | bytes 1572872 | tf_op jit(solution)/shard_map/ppermute | solution.py:420
  51.4 21.2 %collective-permute-start.3 = (bf16[10,512,512]{2,1,0:T(8,128)(2,1)}, bf16[10,512,512]{2,1,0:T(8,128)(2,1)}, u32[]{:S(2)}, u32[]{:S(2)}) collective-permute-start(bf16[10,512,512]{2,1,0:T(8,128)(2,1)} %get-tuple-element.14), channel_id=1, source_target_pairs={{64,0},{65,1},{66,2},{67,3},{68,4},{69,5},{70,6},{71,7},{72,8},{73... | collective-permute-start | bytes 15728648 | tf_op jit(solution)/shard_map/ppermute | solution.py:417
  57.6 14.8 %all-to-all-start.1 = ((bf16[64,24,128]{2,1,0:T(8,128)(2,1)}), bf16[64,24,128]{2,1,0:T(8,128)(2,1)S(1)}, u32[]{:S(2)}, u32[]{:S(2)}) async-start(bf16[64,24,128]{2,1,0:T(8,128)(2,1)} %fusion.1), calls=%async_computation.1 | async-start | bytes 786432 | tf_op jit(solution)/shard_map/all_to_all | solution.py:398
  77.2 25.7 %all-to-all-start.2 = ((bf16[64,80,128]{2,1,0:T(8,128)(2,1)}), bf16[64,80,128]{2,1,0:T(8,128)(2,1)S(1)}, u32[]{:S(2)}, u32[]{:S(2)}) async-start(bf16[64,80,128]{2,1,0:T(8,128)(2,1)} %split_products.1), calls=%async_computation.2 | async-start | bytes 2621440 | tf_op jit(solution)/shard_map/all_to_all | solution.py:398
  104.5 2.1 %collective-permute-start.4 = (f32[128,8,128]{2,1,0:T(8,128)S(1)}, f32[128,8,128]{2,1,0:T(8,128)S(1)}, u32[]{:S(2)}, u32[]{:S(2)}) collective-permute-start(f32[128,8,128]{2,1,0:T(8,128)S(1)} %add_up.3.mine), channel_id=1, source_target_pairs={{0,64},{64,0},{1,65},{65,1},{2,66},{66,2},{3,67},{67,3},{4,68},{68... | collective-permute-start | bytes 1572872 | tf_op jit(solution)/shard_map/ppermute | solution.py:420
  137.4 4.0 %collective-permute-start.5 = (f32[2,512,128]{2,1,0:T(8,128)S(1)}, f32[2,512,128]{2,1,0:T(8,128)S(1)}, u32[]{:S(2)}, u32[]{:S(2)}) collective-permute-start(f32[2,512,128]{2,1,0:T(8,128)S(1)} %split_backward.1), channel_id=1, source_target_pairs={{0,64},{64,0},{1,65},{65,1},{2,66},{66,2},{3,67},{67,3},{4,68},{68... | collective-permute-start | bytes 1572872 | tf_op jit(solution)/shard_map/ppermute | solution.py:420
  157.4 30.5 %copy-start.1 = (bf16[128,1024]{1,0:T(8,128)(2,1)S(1)}, bf16[128,1024]{1,0:T(8,128)(2,1)}, u32[]{:S(2)}) copy-start(bf16[128,1024]{1,0:T(8,128)(2,1)} %x_in.3) | copy-start | bytes 786436
  157.4 23.5 %all-to-all-start.5 = ((bf16[64,80,128]{2,1,0:T(8,128)(2,1)}), bf16[64,80,128]{2,1,0:T(8,128)(2,1)S(1)}, u32[]{:S(2)}, u32[]{:S(2)}) async-start(bf16[64,80,128]{2,1,0:T(8,128)(2,1)} %hand_out.1), calls=%async_computation.5 | async-start | bytes 2621440 | tf_op jit(solution)/shard_map/all_to_all | solution.py:398
  162.5 25.7 %collective-permute-start.7 = (bf16[64,80,128]{2,1,0:T(8,128)(2,1)S(1)}, bf16[64,80,128]{2,1,0:T(8,128)(2,1)}, u32[]{:S(2)}, u32[]{:S(2)}) collective-permute-start(bf16[64,80,128]{2,1,0:T(8,128)(2,1)S(1)} %all_to_all.30.grads.grads1), channel_id=1, source_target_pairs={{0,64},{1,65},{2,66},{3,67},{4,68},{5,69},{6,70},{7,71},{8,72},{9,... | collective-permute-start | bytes 3932168 | tf_op jit(solution)/shard_map/ppermute | solution.py:417
  181.0 14.7 %collective-permute-start.6 = (bf16[64,80,128]{2,1,0:T(8,128)(2,1)S(1)}, bf16[64,80,128]{2,1,0:T(8,128)(2,1)}, u32[]{:S(2)}, u32[]{:S(2)}) collective-permute-start(bf16[64,80,128]{2,1,0:T(8,128)(2,1)S(1)} %all-to-all-done.5.grads0), channel_id=1, source_target_pairs={{64,0},{65,1},{66,2},{67,3},{68,4},{69,5},{70,6},{71,7},{72,8},{73... | collective-permute-start | bytes 3932168 | tf_op jit(solution)/shard_map/ppermute | solution.py:417

commit v4 on v3

--- a/solution.py
+++ b/solution.py
@@ -41,6 +41,11 @@
         parts.append(product.T.reshape(width // SLICE, SLICE, x.shape[0]))
     both = jnp.concatenate(parts, axis=1).astype(jnp.bfloat16)
     out[:, 2 * SLICE * pair : 2 * SLICE * (pair + 1), :] = both
+
+
+def put_rows(stage, out, sems, k):
+    rows = slice(2 * SLICE * k, 2 * SLICE * (k + 1))
+    return pltpu.make_async_copy(stage.at[:, rows], out.at[:, rows], sems.at[k])
 
 
 def first_products_body(
@@ -127,16 +132,12 @@
     pairs = held.shape[0] // 2
     copy = start_split_tiles(meta[0], received, tiles, held, sems)
 
-    def put(k):
-        rows = slice(2 * SLICE * k, 2 * SLICE * (k + 1))
-        return pltpu.make_async_copy(stage.at[:, rows], out.at[:, rows], out_sems.at[k])
-
     for k in range(pairs):
         copy(k).wait()
         product_pair(meta, 1, x, held, stage, k)
-        put(k).start()
+        put_rows(stage, out, out_sems, k).start()
     for k in range(pairs):
-        put(k).wait()
+        put_rows(stage, out, out_sems, k).wait()
 
 
 def split_products(meta, x, received, tiles):
@@ -197,7 +198,20 @@
                 out[holder, t * SLICE : (t + 2) * SLICE, :] = rows
 
 
-def value_and_hand_out_body(idx, mine, other, notional, strike, out, held, *, count, weight):
+def value_and_hand_out_body(
+    idx, mine, other, notional, strike, received, tiles, out, taken, held, sem, *, count, weight
+):
+    core = lax.axis_index("phase")
+    half = taken.shape[0]
+
+    @pl.when(core == 0)
+    def _():
+        pltpu.make_async_copy(received, taken, sem).start()
+
+    @pl.when(core == 1)
+    def _():
+        pltpu.make_async_copy(tiles.at[pl.ds(half, half)], taken, sem).start()
+
     @pl.loop(0, held.shape[0], step=32)
     def _(b):
         for k in range(32):
@@ -205,20 +219,27 @@
             held[b + k] = notional[b + k] * jax.nn.sigmoid(moneyness - strike[b + k]) * weight
 
     hand_out(idx, held, out, count)
-
-
-def value_and_hand_out(idx, mine, other, notional, strike, shards, count, weight):
+    pltpu.make_async_copy(received, taken, sem).wait()
+
+
+def value_and_hand_out(
+    idx, mine, other, notional, strike, received, tiles, shards, count, weight
+):
     scen = mine.shape[2]
     vmem = pl.BlockSpec(memory_space=pltpu.VMEM)
+    hbm = pl.BlockSpec(memory_space=pl.ANY)
     return pl.pallas_call(
         functools.partial(value_and_hand_out_body, count=count, weight=weight),
-        in_specs=[pl.BlockSpec(memory_space=pltpu.SMEM), vmem, vmem, vmem, vmem],
-        out_specs=vmem,
-        out_shape=jax.ShapeDtypeStruct((shards, count * SLICE, scen), jnp.bfloat16),
-        scratch_shapes=[pltpu.VMEM(mine.shape, jnp.float32)],
-        compiler_params=params(),
+        in_specs=[pl.BlockSpec(memory_space=pltpu.SMEM), vmem, vmem, vmem, vmem, hbm, hbm],
+        out_specs=[vmem, vmem],
+        out_shape=[
+            jax.ShapeDtypeStruct((shards, count * SLICE, scen), jnp.bfloat16),
+            jax.ShapeDtypeStruct(received.shape, jnp.bfloat16),
+        ],
+        scratch_shapes=[pltpu.VMEM(mine.shape, jnp.float32), pltpu.SemaphoreType.DMA],
+        compiler_params=params(PASSING_LIMIT),
         name="value_and_hand_out",
-    )(idx, mine, other, notional, strike)
+    )(idx, mine, other, notional, strike, received, tiles)
 
 
 def only_hand_out_body(idx, blocks, out, held, *, count):
@@ -250,39 +271,35 @@
     ]
 
 
-def split_backward_body(meta, grads, received, tiles, total, held, sems):
-    copy = start_split_tiles(meta[0], received, tiles, held, sems)
+def first_backward_body(meta, grads, tiles, total):
     total[...] = jnp.zeros_like(total)
-
-    for k in range(held.shape[0] // 2):
-        copy(k).wait()
+    for k in range(tiles.shape[0] // 2):
         for u, grad in enumerate(tile_grad_pair(grads, k)):
-            product = jnp.dot(held[2 * k + u], grad, preferred_element_type=jnp.float32)
+            product = jnp.dot(tiles[2 * k + u], grad, preferred_element_type=jnp.float32)
             total[meta[1 + 2 * k + u]] += product
 
 
-def split_backward(meta, grads, received, tiles, blocks_dev):
-    count, width = received.shape[0], received.shape[1]
+def first_backward(meta, grads, tiles, blocks_dev):
     vmem = pl.BlockSpec(memory_space=pltpu.VMEM)
-    hbm = pl.BlockSpec(memory_space=pl.ANY)
-    return pl.pallas_call(
-        split_backward_body,
-        in_specs=[pl.BlockSpec(memory_space=pltpu.SMEM), vmem, hbm, hbm],
+    return pl.pallas_call(
+        first_backward_body,
+        in_specs=[pl.BlockSpec(memory_space=pltpu.SMEM), vmem, vmem],
         out_specs=vmem,
-        out_shape=jax.ShapeDtypeStruct((blocks_dev, width, grads.shape[2]), jnp.float32),
-        scratch_shapes=tile_scratch(count, width),
-        compiler_params=params(STREAM_LIMIT),
-        name="split_backward",
-    )(meta, grads, received, tiles)
+        out_shape=jax.ShapeDtypeStruct(
+            (blocks_dev, tiles.shape[1], grads.shape[2]), jnp.float32
+        ),
+        compiler_params=params(),
+        name="first_backward",
+    )(meta, grads, tiles)
 
 
 def last_backward_body(meta, grads0, grads1, inputs, tiles, *rest, first):
     if first:
-        earlier, _, sens, adjoint_out, grads, grads_sems, stage, out_sems, *more = rest
-        total, adjoint, adjoint_sem = more
-        held = tiles
+        earlier, _, sens, adjoint_out, *scratch, total, adjoint, adjoint_sem = rest
     else:
-        sens, total, following, grads, grads_sems, stage, out_sems, held, sems, next_sems = rest
+        sens, total, *scratch = rest
+    grads, grads_sems, stage, out_sems, held, sems = scratch
+    take = tile_copies(tiles, first, held, sems)
 
     pairs = stage.shape[0]
 
@@ -300,14 +317,8 @@
         for k in range(pairs):
             grads_copy(grads1, k).start()
 
-    if not first:
-        take = tile_copies(tiles, 0, held, sems)
-        take_next = tile_copies(tiles, held.shape[0], following, next_sems)
-        for k in range(held.shape[0] // 2):
-            take(k).start()
-        for k in range(held.shape[0] // 2):
-            take_next(k).start()
-
+    for k in range(pairs):
+        take(k).start()
     total[...] = earlier[...] if first else jnp.zeros_like(total)
 
     def put(k):
@@ -316,8 +327,7 @@
         )
 
     for k in range(pairs):
-        if not first:
-            take(k).wait()
+        take(k).wait()
         grads_copy(grads0, k).wait()
         for u, grad in enumerate(tile_grad_pair(grads, k)):
             col = meta[1 + first + 2 * k + u]
@@ -334,9 +344,6 @@
         adjoint_copy = pltpu.make_async_copy(adjoint, adjoint_out, adjoint_sem)
         adjoint_copy.start()
         adjoint_copy.wait()
-    else:
-        for k in range(pairs):
-            take_next(k).wait()
     for k in range(2 * pairs):
         put(k).wait()
 
@@ -350,27 +357,27 @@
     hbm = pl.BlockSpec(memory_space=pl.ANY)
     sens_shape = jax.ShapeDtypeStruct((slots, width, width), jnp.bfloat16)
     total_shape = jax.ShapeDtypeStruct(inputs.shape, jnp.float32)
-    half_shape = jax.ShapeDtypeStruct((half, width, width), jnp.bfloat16)
     sems = pltpu.SemaphoreType.DMA((half // 2,))
     scratch = [
         pltpu.VMEM(grads[0][0].shape, jnp.bfloat16),
         sems,
         pltpu.VMEM((half // 2, 2, width, width), jnp.bfloat16),
         pltpu.SemaphoreType.DMA((half,)),
+        *tile_scratch(half, width),
     ]
     adjoint_shape = (scen, blocks_dev * width)
-    sens, total, high_tiles = pl.pallas_call(
+    sens, total = pl.pallas_call(
         functools.partial(last_backward_body, first=0),
         in_specs=[smem, hbm, hbm, vmem, hbm],
-        out_specs=[hbm, vmem, vmem],
-        out_shape=[sens_shape, total_shape, half_shape],
-        scratch_shapes=[*scratch, *tile_scratch(half, width), sems],
-        compiler_params=params(PASSING_LIMIT),
+        out_specs=[hbm, vmem],
+        out_shape=[sens_shape, total_shape],
+        scratch_shapes=scratch,
+        compiler_params=params(STREAM_LIMIT),
         name="last_backward_low",
     )(meta, *grads[0], inputs, tiles)
     return pl.pallas_call(
         functools.partial(last_backward_body, first=half),
-        in_specs=[smem, hbm, hbm, vmem, vmem, vmem, hbm],
+        in_specs=[smem, hbm, hbm, vmem, hbm, vmem, hbm],
         out_specs=[hbm, hbm],
         out_shape=[sens_shape, jax.ShapeDtypeStruct(adjoint_shape, jnp.bfloat16)],
         scratch_shapes=[
@@ -380,9 +387,9 @@
             pltpu.SemaphoreType.DMA,
         ],
         input_output_aliases={6: 0},
-        compiler_params=params(),
+        compiler_params=params(STREAM_LIMIT),
         name="last_backward_high",
-    )(meta, *grads[1], inputs, high_tiles, total, sens)
+    )(meta, *grads[1], inputs, tiles, total, sens)
 
 
 def three_terms(values):
@@ -392,6 +399,13 @@
         terms.append(term)
         values = values - term
     return jnp.stack(terms)
+
+
+def scales_to_send(notional, strike, shards, blocks_dev, scen):
+    scales = jnp.stack([three_terms(notional), three_terms(strike)])
+    scales = scales.reshape(6, blocks_dev, shards, SLICE).transpose(2, 0, 1, 3)
+    scales = scales.reshape(shards, 1, 6 * blocks_dev * SLICE).astype(jnp.bfloat16)
+    return jnp.pad(scales, ((0, 0), (0, SLICE - 1), (0, scen - scales.shape[2])))
 
 
 def exchange(block):
@@ -433,15 +447,13 @@
     sent = first_products(tile_col, normals, tiles, half, half, False)
     kept, low_tiles = first_products(tile_col, normals, tiles, 0, half, True)
     arrived = exchange(of_core(kept, send(sent, 0)))
+    scales = scales_to_send(notional, strike, shards, blocks_dev, scen)
+    split_rows[0], scales = lax.optimization_barrier((split_rows[0], scales))
     part = add_up(split_rows[0], arrived, blocks)
     other_part, low_tiles = lax.optimization_barrier((swap(part), low_tiles))
     received = send(low_tiles, 1)
     shock_slices = (part + other_part).astype(jnp.bfloat16)
 
-    scales = jnp.stack([three_terms(notional), three_terms(strike)])
-    scales = scales.reshape(6, blocks_dev, shards, SLICE).transpose(2, 0, 1, 3)
-    scales = scales.reshape(shards, 1, 6 * blocks_dev * SLICE).astype(jnp.bfloat16)
-    scales = jnp.pad(scales, ((0, 0), (0, SLICE - 1), (0, scen - scales.shape[2])))
     shock_rows = shock_slices.reshape(shards, blocks_dev * SLICE, scen)
     arrived = exchange(jnp.concatenate([shock_rows, scales], axis=1))
     shocks = arrived[:, : blocks_dev * SLICE].reshape(shards, blocks_dev, SLICE, scen)
@@ -453,23 +465,32 @@
     scales = scales.transpose(1, 0, 2, 3).reshape(2, blocks, SLICE, 1)
 
     arrived = exchange(split_products(split_meta, shocks_natural, received, tiles))
+    split_rows[1], scales = lax.optimization_barrier((split_rows[1], scales))
     part = add_up(split_rows[1], arrived, blocks)
-    outgoing = value_and_hand_out(
-        split_rows[1], part, swap(part), scales[0], scales[1], shards, half, weight
+    outgoing, split_tiles = value_and_hand_out(
+        split_rows[1],
+        part,
+        swap(part),
+        scales[0],
+        scales[1],
+        received,
+        tiles,
+        shards,
+        half,
+        weight,
     )
 
     high1 = exchange(outgoing)
-    part = split_backward(split_meta, high1, received, tiles, blocks_dev)
+    part = first_backward(split_meta, high1, split_tiles, blocks_dev)
     shock_grad = (part + swap(part)).astype(jnp.bfloat16)
     low1 = send(high1, 0)
 
     shock_grad = shock_grad.reshape(blocks_dev, shards, SLICE, scen).transpose(1, 0, 2, 3)
     arrived = exchange(shock_grad.reshape(shards, blocks_dev * SLICE, scen))
+    normals_held = normals.reshape(scen, blocks_dev, width).transpose(1, 2, 0)
+    inputs = of_core(normals_held, shocks)
     low0 = exchange(only_hand_out(split_rows[0], arrived, shards, half))
     high0 = send(low0, 1)
-
-    normals_held = normals.reshape(scen, blocks_dev, width).transpose(1, 2, 0)
-    inputs = of_core(normals_held, shocks)
     sens, adjoint = last_backward_calls(
         meta, ((low0, low1), (high0, high1)), inputs, tiles
     )

time: 202 us -> 201 us (level)
  transfers between devices with their start and end apart: 12 -> 12, of which waited for: 7 -> 8; matrix products, arithmetic and copies ran while one was open for 2% -> 2% of each run, Pallas kernels for 6% -> 6%
where the time goes in v4:
time: 201 us; the launch traced here: 200 us
  waiting for transfers between devices  70.6 us (35%)
  starting transfers between devices  45 us (22%)
  blocking collectives  37.8 us (19%)
  Pallas kernels  36.3 us (18%)
  local copies, waits for them, and re-layouts  4.92 us (2%)
  other arithmetic  4.02 us (2%)
    all_to_all x4, waiting for transfers between devices, exchange(): return lax.all_to_all(block, 'blk', split_axis=0, concat_axis=0, tiled=True)  66.8 us
    all_to_all x2, blocking collectives, exchange(): return lax.all_to_all(block, 'blk', split_axis=0, concat_axis=0, tiled=True)  37.8 us
    all_to_all x4, starting transfers between devices, exchange(): return lax.all_to_all(block, 'blk', split_axis=0, concat_axis=0, tiled=True)  26.6 us
    ppermute x4, starting transfers between devices, send(): return lax.ppermute(block, 'phase', [(source, 1 - source)])  14.1 us
    pallas_call x2, Pallas kernels, first_products(): pl.pallas_call(functools.partial(first_products_body, first=first), in_sp...  7.68 us
    pallas_call x1, Pallas kernels, last_backward_calls(): pl.pallas_call(functools.partial(last_backward_body, first=0), in_specs=[...  6.68 us
    pallas_call x1, Pallas kernels, last_backward_calls(): pl.pallas_call(functools.partial(last_backward_body, first=half), in_spec...  6.52 us
    pallas_call x1, Pallas kernels, split_products(): pl.pallas_call(split_products_body, in_specs=[pl.BlockSpec(memory_space=p...  4.5 us
  transfers between devices with their start and end apart: 12, of which 8 were waited for; matrix products, arithmetic and copies ran while one was open for 2% of the time, Pallas kernels for 6%

profile of v4, /device:TPU:1, one launch (start us, length us, event | category | flops | bytes accessed | tf_op | source)
XLA Modules:
  0.0 199.8 jit_solution(8025056332303785291)
XLA Ops:
  0.6 0.9 copy-done
  1.6 0.7 copy-done.2
  2.2 3.3 %first_products.3 = bf16[64,80,128]{2,1,0:T(8,128)(2,1)S(1)} custom-call(s32[1,20]{1,0:T(1,128)S(1)} %copy-done.2, bf16[128,1024]{1,0:T(8,128)(2,1)S(1)} %copy-done, bf16[20,512,512]{2,1,0:T(8,128)(2,1)} %bitcast.51), custom_call_target="tpu_custom_call" | custom-call | tf_op jit(solution)/shard_map/first_products/pallas_call | solution.py:98
  5.5 1.3 collective-permute-start.1
  6.8 4.4 %first_products.2 = (bf16[64,80,128]{2,1,0:T(8,128)(2,1)S(1)}, bf16[10,512,512]{2,1,0:T(8,128)(2,1)}) custom-call(s32[1,20]{1,0:T(1,128)S(1)} %copy-done.2, bf16[128,1024]{1,0:T(8,128)(2,1)S(1)} %copy-done, bf16[20,512,512]{2,1,0:T(8,128)(2,1)} %bitcast.52), custom_call_target="tpu_custom_call" | custom-call | tf_op jit(solution)/shard_map/first_products/pallas_call | solution.py:98
  11.3 2.5 %broadcast_select_fusion = bf16[64,80,128]{2,1,0:T(8,128)(2,1)} fusion(bf16[64,80,128]{2,1,0:T(8,128)(2,1)S(1)} %get-tuple-element.17, bf16[64,80,128]{2,1,0:T(8,128)(2,1)} %collective-permute-done.1, pred[]{:T(512)S(6)} %eq.2), kind=kLoop, calls=%fused_computation | loop fusion | flops 655360 | bytes 3932161 | tf_op jit(solution)/shard_map/jit(_where)/select_n | solution.py:428
  13.8 12.1 %all-to-all-start = ((bf16[64,80,128]{2,1,0:T(8,128)(2,1)}), bf16[64,80,128]{2,1,0:T(8,128)(2,1)S(1)}, u32[]{:S(2)}, u32[]{:S(2)}) async-start(bf16[64,80,128]{2,1,0:T(8,128)(2,1)} %broadcast_select_fusion), calls=%async_computation | async-start | bytes 2621440 | tf_op jit(solution)/shard_map/all_to_all | solution.py:412
  26.0 0.1 collective-permute-start
  26.3 0.3 convert_element_type.33
  26.5 0.1 copy.44
  26.7 0.5 collective-permute-done
  27.2 0.1 slice.69
  27.4 0.1 reshape.75.idx
  27.6 19.3 %all-to-all-done.data = bf16[64,80,128]{2,1,0:T(8,128)(2,1)S(1)} async-done(((bf16[64,80,128]{2,1,0:T(8,128)(2,1)}), bf16[64,80,128]{2,1,0:T(8,128)(2,1)S(1)}, u32[]{:S(2)}, u32[]{:S(2)}) %all-to-all-start) | async-done | bytes 1310752 | tf_op jit(solution)/shard_map/all_to_all | solution.py:412
  46.8 1.6 add_up.2
  48.5 1.3 collective-permute-start.2
  49.8 1.5 collective-permute-done.2
  51.4 4.6 %collective-permute-start.3 = (bf16[10,512,512]{2,1,0:T(8,128)(2,1)}, bf16[10,512,512]{2,1,0:T(8,128)(2,1)}, u32[]{:S(2)}, u32[]{:S(2)}) collective-permute-start(bf16[10,512,512]{2,1,0:T(8,128)(2,1)} %get-tuple-element.22), channel_id=1, source_target_pairs={{64,0},{65,1},{66,2},{67,3},{68,4},{69,5},{70,6},{71,7},{72,8},{73... | collective-permute-start | bytes 15728648 | tf_op jit(solution)/shard_map/ppermute | solution.py:431
  56.0 0.2 copy.45
  56.2 0.8 pad_maximum_fusion
  57.0 4.8 %all-to-all-start.1 = ((bf16[64,24,128]{2,1,0:T(8,128)(2,1)}), bf16[64,24,128]{2,1,0:T(8,128)(2,1)S(1)}, u32[]{:S(2)}, u32[]{:S(2)}) async-start(bf16[64,24,128]{2,1,0:T(8,128)(2,1)} %pad_maximum_fusion), calls=%async_computation.1 | async-start | bytes 786432 | tf_op jit(solution)/shard_map/all_to_all | solution.py:412
  61.9 9.9 %all-to-all-done.1 = bf16[64,24,128]{2,1,0:T(8,128)(2,1)S(1)} async-done(((bf16[64,24,128]{2,1,0:T(8,128)(2,1)}), bf16[64,24,128]{2,1,0:T(8,128)(2,1)S(1)}, u32[]{:S(2)}, u32[]{:S(2)}) %all-to-all-start.1) | async-done | bytes 393248 | tf_op jit(solution)/shard_map/all_to_all | solution.py:412
  71.9 0.1 copy.49.x
  72.1 4.5 %split_products.1 = bf16[64,80,128]{2,1,0:T(8,128)(2,1)} custom-call(s32[11]{0:T(128)S(1)} %pad_add_fusion.2.meta, bf16[128,1024]{1,0:T(8,128)(2,1)S(1)} %copy.49.x, bf16[10,512,512]{2,1,0:T(8,128)(2,1)} %collective-permute-done.3.received, bf16[20,512,512]{2,1,0:T(8,128)(2,1)} %bitcast.53), custom_call_target="tpu_custom_call" | custom-call | tf_op jit(solution)/shard_map/split_products/pallas_call | solution.py:148
  76.6 4.7 %all-to-all-start.2 = ((bf16[64,80,128]{2,1,0:T(8,128)(2,1)}), bf16[64,80,128]{2,1,0:T(8,128)(2,1)S(1)}, u32[]{:S(2)}, u32[]{:S(2)}) async-start(bf16[64,80,128]{2,1,0:T(8,128)(2,1)} %split_products.1), calls=%async_computation.2 | async-start | bytes 2621440 | tf_op jit(solution)/shard_map/all_to_all | solution.py:412
  81.2 0.1 slice.76
  81.4 0.1 reshape.76.idx
  81.6 0.1 copy.60
  81.7 0.1 copy.47
  81.8 20.4 %all-to-all-done.2.data = bf16[64,80,128]{2,1,0:T(8,128)(2,1)S(1)} async-done(((bf16[64,80,128]{2,1,0:T(8,128)(2,1)}), bf16[64,80,128]{2,1,0:T(8,128)(2,1)S(1)}, u32[]{:S(2)}, u32[]{:S(2)}) %all-to-all-start.2) | async-done | bytes 1310752 | tf_op jit(solution)/shard_map/all_to_all | solution.py:412
  102.3 1.6 add_up.3.mine
  104.0 0.8 copy.53.strike
  104.8 0.8 copy.52.notional
  105.6 0.2 collective-permute-done.4.other
  105.9 3.1 %value_and_hand_out.1 = (bf16[64,80,128]{2,1,0:T(8,128)(2,1)S(1)}, bf16[10,512,512]{2,1,0:T(8,128)(2,1)S(1)}) custom-call(s32[640]{0:T(1024)S(1)} %reshape.76.idx, f32[128,8,128]{2,1,0:T(8,128)S(1)} %add_up.3.mine, f32[128,8,128]{2,1,0:T(8,128)S(1)} %collective-permute-done.4.other, f32[128,8,1]{2,1,0:T(8,128)S(1)} %copy.52.notional, ...), custom_call_target="tpu_custom_call" | custom-call | tf_op jit(solution)/shard_map/value_and_hand_out/pallas_call | solution.py:231
  109.0 24.3 %all_to_all.30.grads.grads1 = bf16[64,80,128]{2,1,0:T(8,128)(2,1)S(1)} all-to-all(bf16[64,80,128]{2,1,0:T(8,128)(2,1)S(1)} %get-tuple-element.24), channel_id=1, replica_groups=mesh['phase'=2,'blk'=64] {'blk'}, dimensions={0} | all-to-all | bytes 2621440 | tf_op jit(solution)/shard_map/all_to_all | solution.py:412
  133.3 2.1 %first_backward.1 = f32[2,512,128]{2,1,0:T(8,128)S(1)} custom-call(s32[11]{0:T(128)S(1)} %pad_add_fusion.2.meta, bf16[64,80,128]{2,1,0:T(8,128)(2,1)S(1)} %all_to_all.30.grads.grads1, bf16[10,512,512]{2,1,0:T(8,128)(2,1)S(1)} %get-tuple-element.25.tiles), custom_call_target="tpu_custom_call" | custom-call | tf_op jit(solution)/shard_map/first_backward/pallas_call | solution.py:284
  135.4 2.7 %collective-permute-start.5 = (f32[2,512,128]{2,1,0:T(8,128)S(1)}, f32[2,512,128]{2,1,0:T(8,128)S(1)}, u32[]{:S(2)}, u32[]{:S(2)}) collective-permute-start(f32[2,512,128]{2,1,0:T(8,128)S(1)} %first_backward.1), channel_id=1, source_target_pairs={{0,64},{64,0},{1,65},{65,1},{2,66},{66,2},{3,67},{67,3},{4,68},{68... | collective-permute-start | bytes 1572872 | tf_op jit(solution)/shard_map/ppermute | solution.py:434
  138.1 1.5 collective-permute-done.5
  139.7 13.5 %all_to_all.31.blocks = bf16[64,16,128]{2,1,0:T(8,128)(2,1)S(1)} all-to-all(bf16[64,16,128]{2,1,0:T(8,128)(2,1)S(1)} %copy_bitcast_fusion), channel_id=1, replica_groups=mesh['phase'=2,'blk'=64] {'blk'}, dimensions={0} | all-to-all | bytes 524288 | tf_op jit(solution)/shard_map/all_to_all | solution.py:412
  153.2 2.4 %hand_out.1 = bf16[64,80,128]{2,1,0:T(8,128)(2,1)} custom-call(s32[640]{0:T(1024)S(1)} %reshape.75.idx, bf16[64,16,128]{2,1,0:T(8,128)(2,1)S(1)} %all_to_all.31.blocks), custom_call_target="tpu_custom_call" | custom-call | tf_op jit(solution)/shard_map/hand_out/pallas_call | solution.py:254
  155.6 5.0 %all-to-all-start.5 = ((bf16[64,80,128]{2,1,0:T(8,128)(2,1)}), bf16[64,80,128]{2,1,0:T(8,128)(2,1)S(1)}, u32[]{:S(2)}, u32[]{:S(2)}) async-start(bf16[64,80,128]{2,1,0:T(8,128)(2,1)} %hand_out.1), calls=%async_computation.5 | async-start | bytes 2621440 | tf_op jit(solution)/shard_map/all_to_all | solution.py:412
  160.7 1.3 collective-permute-start.7
  162.0 17.2 %all-to-all-done.5.grads0 = bf16[64,80,128]{2,1,0:T(8,128)(2,1)S(1)} async-done(((bf16[64,80,128]{2,1,0:T(8,128)(2,1)}), bf16[64,80,128]{2,1,0:T(8,128)(2,1)S(1)}, u32[]{:S(2)}, u32[]{:S(2)}) %all-to-all-start.5) | async-done | bytes 1310752 | tf_op jit(solution)/shard_map/all_to_all | solution.py:412
  179.2 6.9 %collective-permute-start.6 = (bf16[64,80,128]{2,1,0:T(8,128)(2,1)S(1)}, bf16[64,80,128]{2,1,0:T(8,128)(2,1)}, u32[]{:S(2)}, u32[]{:S(2)}) collective-permute-start(bf16[64,80,128]{2,1,0:T(8,128)(2,1)S(1)} %all-to-all-done.5.grads0), channel_id=1, source_target_pairs={{64,0},{65,1},{66,2},{67,3},{68,4},{69,5},{70,6},{71,7},{72,8},{73... | collective-permute-start | bytes 3932168 | tf_op jit(solution)/shard_map/ppermute | solution.py:431
  186.1 0.2 copy.55
  186.4 6.7 %last_backward_low.1 = (bf16[20,512,512]{2,1,0:T(8,128)(2,1)}, f32[2,512,128]{2,1,0:T(8,128)S(1)}) custom-call(s32[21]{0:T(128)S(1)} %pad_add_fusion.1.meta, bf16[64,80,128]{2,1,0:T(8,128)(2,1)S(1)} %all-to-all-done.5.grads0, bf16[64,80,128]{2,1,0:T(8,128)(2,1)} %collective-permute-done.7.grads1, bf16[2,512,128]{2,1,0:T(8,128)(2,1)S(1)} %bitcast_select_fusion.inputs, ...), custom_call_target="tpu_custom_call" | custom-call | tf_op jit(solution)/shard_map/last_backward_low/pallas_call | solution.py:369
  193.1 6.5 %last_backward_high.1 = (bf16[20,512,512]{2,1,0:T(8,128)(2,1)}, bf16[128,1024]{1,0:T(8,128)(2,1)}) custom-call(s32[21]{0:T(128)S(1)} %pad_add_fusion.1.meta, bf16[64,80,128]{2,1,0:T(8,128)(2,1)} %collective-permute-done.6.grads0, bf16[64,80,128]{2,1,0:T(8,128)(2,1)S(1)} %all_to_all.30.grads.grads1, ...), custom_call_target="tpu_custom_call", output_to_operand_aliasing={{0}: (6, {})} | custom-call | tf_op jit(solution)/shard_map/last_backward_high/pallas_call | solution.py:378
  (46 shorter events, 1.0 us)
Async XLA Ops:
  0.6 1.0 copy-start
  1.6 0.7 copy-start.2
  5.5 5.7 %collective-permute-start.1 = (bf16[64,80,128]{2,1,0:T(8,128)(2,1)S(1)}, bf16[64,80,128]{2,1,0:T(8,128)(2,1)}, u32[]{:S(2)}, u32[]{:S(2)}) collective-permute-start(bf16[64,80,128]{2,1,0:T(8,128)(2,1)S(1)} %first_products.3), channel_id=1, source_target_pairs={{0,64},{1,65},{2,66},{3,67},{4,68},{5,69},{6,70},{7,71},{8,72},{9,... | collective-permute-start | bytes 3932168 | tf_op jit(solution)/shard_map/ppermute | solution.py:431
  13.8 12.1 %copy-start.4 = (s32[1,1280]{1,0:T(1,128)S(1)}, s32[1,1280]{1,0:T(1,128)}, u32[]{:S(2)}) copy-start(s32[1,1280]{1,0:T(1,128)} %param.8) | copy-start | bytes 15364
  13.8 12.2 %copy-start.3 = (s32[1,20]{1,0:T(1,128)S(1)}, s32[1,20]{1,0:T(1,128)}, u32[]{:S(2)}) copy-start(s32[1,20]{1,0:T(1,128)} %cols_in.3) | copy-start | bytes 244
  13.8 12.3 %copy-start.5 = (f32[1024]{0:T(1024)S(1)}, f32[1024]{0:T(1024)}, u32[]{:S(2)}) copy-start(f32[1024]{0:T(1024)} %param.10) | copy-start | bytes 12292
  13.8 12.3 %copy-start.6 = (f32[1024]{0:T(1024)S(1)}, f32[1024]{0:T(1024)}, u32[]{:S(2)}) copy-start(f32[1024]{0:T(1024)} %param.11) | copy-start | bytes 12292
  13.8 33.0 %all-to-all-start = ((bf16[64,80,128]{2,1,0:T(8,128)(2,1)}), bf16[64,80,128]{2,1,0:T(8,128)(2,1)S(1)}, u32[]{:S(2)}, u32[]{:S(2)}) async-start(bf16[64,80,128]{2,1,0:T(8,128)(2,1)} %broadcast_select_fusion), calls=%async_computation | async-start | bytes 2621440 | tf_op jit(solution)/shard_map/all_to_all | solution.py:412
  26.0 1.3 collective-permute-start
  48.5 2.9 %collective-permute-start.2 = (f32[128,8,128]{2,1,0:T(8,128)S(1)}, f32[128,8,128]{2,1,0:T(8,128)S(1)}, u32[]{:S(2)}, u32[]{:S(2)}) collective-permute-start(f32[128,8,128]{2,1,0:T(8,128)S(1)} %add_up.2), channel_id=1, source_target_pairs={{0,64},{64,0},{1,65},{65,1},{2,66},{66,2},{3,67},{67,3},{4,68},{68... | collective-permute-start | bytes 1572872 | tf_op jit(solution)/shard_map/ppermute | solution.py:434
  51.4 20.7 %collective-permute-start.3 = (bf16[10,512,512]{2,1,0:T(8,128)(2,1)}, bf16[10,512,512]{2,1,0:T(8,128)(2,1)}, u32[]{:S(2)}, u32[]{:S(2)}) collective-permute-start(bf16[10,512,512]{2,1,0:T(8,128)(2,1)} %get-tuple-element.22), channel_id=1, source_target_pairs={{64,0},{65,1},{66,2},{67,3},{68,4},{69,5},{70,6},{71,7},{72,8},{73... | collective-permute-start | bytes 15728648 | tf_op jit(solution)/shard_map/ppermute | solution.py:431
  57.0 14.8 %all-to-all-start.1 = ((bf16[64,24,128]{2,1,0:T(8,128)(2,1)}), bf16[64,24,128]{2,1,0:T(8,128)(2,1)S(1)}, u32[]{:S(2)}, u32[]{:S(2)}) async-start(bf16[64,24,128]{2,1,0:T(8,128)(2,1)} %pad_maximum_fusion), calls=%async_computation.1 | async-start | bytes 786432 | tf_op jit(solution)/shard_map/all_to_all | solution.py:412
  76.6 25.7 %all-to-all-start.2 = ((bf16[64,80,128]{2,1,0:T(8,128)(2,1)}), bf16[64,80,128]{2,1,0:T(8,128)(2,1)S(1)}, u32[]{:S(2)}, u32[]{:S(2)}) async-start(bf16[64,80,128]{2,1,0:T(8,128)(2,1)} %split_products.1), calls=%async_computation.2 | async-start | bytes 2621440 | tf_op jit(solution)/shard_map/all_to_all | solution.py:412
  103.9 2.0 collective-permute-start.4
  135.4 4.3 %collective-permute-start.5 = (f32[2,512,128]{2,1,0:T(8,128)S(1)}, f32[2,512,128]{2,1,0:T(8,128)S(1)}, u32[]{:S(2)}, u32[]{:S(2)}) collective-permute-start(f32[2,512,128]{2,1,0:T(8,128)S(1)} %first_backward.1), channel_id=1, source_target_pairs={{0,64},{64,0},{1,65},{65,1},{2,66},{66,2},{3,67},{67,3},{4,68},{68... | collective-permute-start | bytes 1572872 | tf_op jit(solution)/shard_map/ppermute | solution.py:434
  155.6 30.5 %copy-start.1 = (bf16[128,1024]{1,0:T(8,128)(2,1)S(1)}, bf16[128,1024]{1,0:T(8,128)(2,1)}, u32[]{:S(2)}) copy-start(bf16[128,1024]{1,0:T(8,128)(2,1)} %x_in.3) | copy-start | bytes 786436
  155.6 23.5 %all-to-all-start.5 = ((bf16[64,80,128]{2,1,0:T(8,128)(2,1)}), bf16[64,80,128]{2,1,0:T(8,128)(2,1)S(1)}, u32[]{:S(2)}, u32[]{:S(2)}) async-start(bf16[64,80,128]{2,1,0:T(8,128)(2,1)} %hand_out.1), calls=%async_computation.5 | async-start | bytes 2621440 | tf_op jit(solution)/shard_map/all_to_all | solution.py:412
  160.7 25.7 %collective-permute-start.7 = (bf16[64,80,128]{2,1,0:T(8,128)(2,1)S(1)}, bf16[64,80,128]{2,1,0:T(8,128)(2,1)}, u32[]{:S(2)}, u32[]{:S(2)}) collective-permute-start(bf16[64,80,128]{2,1,0:T(8,128)(2,1)S(1)} %all_to_all.30.grads.grads1), channel_id=1, source_target_pairs={{0,64},{1,65},{2,66},{3,67},{4,68},{5,69},{6,70},{7,71},{8,72},{9,... | collective-permute-start | bytes 3932168 | tf_op jit(solution)/shard_map/ppermute | solution.py:431
  179.2 14.0 %collective-permute-start.6 = (bf16[64,80,128]{2,1,0:T(8,128)(2,1)S(1)}, bf16[64,80,128]{2,1,0:T(8,128)(2,1)}, u32[]{:S(2)}, u32[]{:S(2)}) collective-permute-start(bf16[64,80,128]{2,1,0:T(8,128)(2,1)S(1)} %all-to-all-done.5.grads0), channel_id=1, source_target_pairs={{64,0},{65,1},{66,2},{67,3},{68,4},{69,5},{70,6},{71,7},{72,8},{73... | collective-permute-start | bytes 3932168 | tf_op jit(solution)/shard_map/ppermute | solution.py:431

commit v5 on v4

--- a/solution.py
+++ b/solution.py
@@ -48,58 +48,57 @@
     return pltpu.make_async_copy(stage.at[:, rows], out.at[:, rows], sems.at[k])
 
 
-def first_products_body(
-    cols_in, x_in, tiles, out, *rest, first
-):
-    *low, cols, x, small_sems, held, sems, low_sems = rest
+def first_products_body(cols_in, x_in, tiles, *rest, first, moved):
+    out, low, cols, x, small_sems, held, sems, low_sems = rest[-8:]
     pairs = held.shape[0] // 2
-    copy = tile_copies(tiles, first, held, sems)
-    cols_copy = pltpu.make_async_copy(cols_in, cols, small_sems.at[0])
-    x_copy = pltpu.make_async_copy(x_in, x, small_sems.at[1])
-    cols_copy.start()
-    x_copy.start()
-    for k in range(pairs):
-        copy(k).start()
-    cols_copy.wait()
-    x_copy.wait()
-
-    def multiply():
+    core = lax.axis_index("phase")
+
+    @pl.when(core == 0)
+    def _():
+        copy = tile_copies(tiles, first, held, sems)
+        cols_copy = pltpu.make_async_copy(cols_in, cols, small_sems.at[0])
+        x_copy = pltpu.make_async_copy(x_in, x, small_sems.at[1])
+        cols_copy.start()
+        x_copy.start()
+        for k in range(pairs):
+            copy(k).start()
+        cols_copy.wait()
+        x_copy.wait()
         for k in range(pairs):
             copy(k).wait()
             product_pair(cols.at[0], first, x, held, out, k)
 
-    if not low:
-        multiply()
-        return
-    core = lax.axis_index("phase")
-    pl.when(core == 0)(multiply)
-
     @pl.when(core == 1)
     def _():
+        copy = tile_copies(tiles, 0, held, sems)
+
         def put(k):
             return pltpu.make_async_copy(
-                held.at[pl.ds(2 * k, 2)], low[0].at[pl.ds(2 * k, 2)], low_sems.at[k]
+                held.at[pl.ds(2 * k, 2)], low.at[pl.ds(2 * k, 2)], low_sems.at[k]
             )
 
-        for k in range(pairs):
+        for k in moved:
+            copy(k).start()
+        for k in moved:
             copy(k).wait()
             put(k).start()
-        for k in range(pairs):
+        for k in moved:
             put(k).wait()
 
 
-def first_products(cols, x, tiles, first, count, keep):
+def first_products(cols, x, tiles, first, count, moved, low=()):
     width = tiles.shape[1]
     scen = x.shape[0]
     vmem = pl.BlockSpec(memory_space=pltpu.VMEM)
     hbm = pl.BlockSpec(memory_space=pl.ANY)
-    out = jax.ShapeDtypeStruct((width // SLICE, count * SLICE, scen), jnp.bfloat16)
-    low = jax.ShapeDtypeStruct((count, width, width), jnp.bfloat16)
-    return pl.pallas_call(
-        functools.partial(first_products_body, first=first),
-        in_specs=[hbm, hbm, hbm],
-        out_specs=[vmem, hbm] if keep else vmem,
-        out_shape=[out, low] if keep else out,
+    return pl.pallas_call(
+        functools.partial(first_products_body, first=first, moved=moved),
+        in_specs=[hbm] * (3 + len(low)),
+        out_specs=[vmem, hbm],
+        out_shape=[
+            jax.ShapeDtypeStruct((width // SLICE, count * SLICE, scen), jnp.bfloat16),
+            jax.ShapeDtypeStruct((count, width, width), jnp.bfloat16),
+        ],
         scratch_shapes=[
             pltpu.SMEM(cols.shape, jnp.int32),
             pltpu.VMEM(x.shape, jnp.bfloat16),
@@ -107,9 +106,10 @@
         ]
         + tile_scratch(count, width)
         + [pltpu.SemaphoreType.DMA((count // 2,))],
+        input_output_aliases={3: 1} if low else {},
         compiler_params=params(STREAM_LIMIT),
         name="first_products",
-    )(cols, x, tiles)
+    )(cols, x, tiles, *low)
 
 
 def start_split_tiles(core, received, tiles, held, sems):
@@ -444,11 +444,16 @@
     split_meta = jnp.concatenate([my_number, of_core(places[1][-slots:-half], cols[half:])])
     meta = jnp.concatenate([my_number, cols])
 
-    sent = first_products(tile_col, normals, tiles, half, half, False)
-    kept, low_tiles = first_products(tile_col, normals, tiles, 0, half, True)
+    split = half // 4 + 1
+    sent, low_tiles = first_products(tile_col, normals, tiles, half, half, range(split))
+    kept, low_tiles = first_products(
+        tile_col, normals, tiles, 0, half, range(split, half // 2), (low_tiles,)
+    )
     arrived = exchange(of_core(kept, send(sent, 0)))
     scales = scales_to_send(notional, strike, shards, blocks_dev, scen)
-    split_rows[0], scales = lax.optimization_barrier((split_rows[0], scales))
+    split_rows[0], scales, split_meta, meta = lax.optimization_barrier(
+        (split_rows[0], scales, split_meta, meta)
+    )
     part = add_up(split_rows[0], arrived, blocks)
     other_part, low_tiles = lax.optimization_barrier((swap(part), low_tiles))
     received = send(low_tiles, 1)

time: 201 us -> 197 us (0.980)
  blocking collectives: 37.8 us -> 51.9 us
  waiting for transfers between devices: 70.6 us -> 59.2 us
  other arithmetic: 4.02 us -> 1.93 us
    all_to_all x2 -> x3, blocking collectives: 37.8 us -> 51.9 us  [exchange(): return lax.all_to_all(block, 'blk', split_axis=0, concat_axis=0, tiled=True)]
    all_to_all x4 -> x3, waiting for transfers between devices: 66.8 us -> 55.9 us  [exchange(): return lax.all_to_all(block, 'blk', split_axis=0, concat_axis=0, tiled=True)]
    all_to_all x4 -> x3, starting transfers between devices: 26.6 us -> 21 us  [exchange(): return lax.all_to_all(block, 'blk', split_axis=0, concat_axis=0, tiled=True)]
    ppermute x4, starting transfers between devices: 4.28 us -> 7.87 us  [swap(): return lax.ppermute(block, 'phase', [(0, 1), (1, 0)])]
  transfers between devices with their start and end apart: 12 -> 11, of which waited for: 8 -> 6; matrix products, arithmetic and copies ran while one was open for 2% -> 3% of each run, Pallas kernels for 6% -> 5%
where the time goes in v5:
time: 197 us; the launch traced here: 196 us
  waiting for transfers between devices  59.2 us (30%)
  blocking collectives  51.9 us (26%)
  starting transfers between devices  43 us (22%)
  Pallas kernels  34.3 us (17%)
  local copies, waits for them, and re-layouts  4.9 us (2%)
    all_to_all x3, waiting for transfers between devices, exchange(): return lax.all_to_all(block, 'blk', split_axis=0, concat_axis=0, tiled=True)  55.9 us
    all_to_all x3, blocking collectives, exchange(): return lax.all_to_all(block, 'blk', split_axis=0, concat_axis=0, tiled=True)  51.9 us
    all_to_all x3, starting transfers between devices, exchange(): return lax.all_to_all(block, 'blk', split_axis=0, concat_axis=0, tiled=True)  21 us
    ppermute x4, starting transfers between devices, send(): return lax.ppermute(block, 'phase', [(source, 1 - source)])  14.1 us
    ppermute x4, starting transfers between devices, swap(): return lax.ppermute(block, 'phase', [(0, 1), (1, 0)])  7.87 us
    pallas_call x1, Pallas kernels, last_backward_calls(): pl.pallas_call(functools.partial(last_backward_body, first=0), in_specs=[...  6.67 us
    pallas_call x1, Pallas kernels, last_backward_calls(): pl.pallas_call(functools.partial(last_backward_body, first=half), in_spec...  6.51 us
    pallas_call x2, Pallas kernels, first_products(): pl.pallas_call(functools.partial(first_products_body, first=first, moved=...  5.73 us
  transfers between devices with their start and end apart: 11, of which 6 were waited for; matrix products, arithmetic and copies ran while one was open for 3% of the time, Pallas kernels for 5%

profile of v5, /device:TPU:1, one launch (start us, length us, event | category | flops | bytes accessed | tf_op | source)
XLA Modules:
  0.0 196.4 jit_solution(17409284406421684300)
XLA Ops:
  0.6 0.9 copy-done
  1.6 0.7 copy-done.2
  2.3 3.1 %first_products.2 = (bf16[64,80,128]{2,1,0:T(8,128)(2,1)S(1)}, bf16[10,512,512]{2,1,0:T(8,128)(2,1)}) custom-call(s32[1,20]{1,0:T(1,128)S(1)} %copy-done.2, bf16[128,1024]{1,0:T(8,128)(2,1)S(1)} %copy-done, bf16[20,512,512]{2,1,0:T(8,128)(2,1)} %bitcast.51), custom_call_target="tpu_custom_call" | custom-call | tf_op jit(solution)/shard_map/first_products/pallas_call | solution.py:94
  5.3 1.3 collective-permute-start.1
  6.7 1.9 collective-permute-start
  8.7 2.7 %first_products.3 = (bf16[64,80,128]{2,1,0:T(8,128)(2,1)S(1)}, bf16[10,512,512]{2,1,0:T(8,128)(2,1)}) custom-call(s32[1,20]{1,0:T(1,128)S(1)} %copy-done.3, bf16[128,1024]{1,0:T(8,128)(2,1)S(1)} %copy-done.1, bf16[20,512,512]{2,1,0:T(8,128)(2,1)} %bitcast.52, bf16[10,512,512]{2,1,0:T(8,128)(2,1)} %get-tuple-element.23.rest_0_), custom_call_target="tpu_custom_call", output_to_operand_aliasing={{1}: (3, {})} | custom-call | tf_op jit(solution)/shard_map/first_products/pallas_call | solution.py:94
  11.4 1.3 broadcast_select_fusion
  12.6 11.4 %all-to-all-start = ((bf16[64,80,128]{2,1,0:T(8,128)(2,1)}), bf16[64,80,128]{2,1,0:T(8,128)(2,1)S(1)}, u32[]{:S(2)}, u32[]{:S(2)}) async-start(bf16[64,80,128]{2,1,0:T(8,128)(2,1)} %broadcast_select_fusion), calls=%async_computation | async-start | bytes 2621440 | tf_op jit(solution)/shard_map/all_to_all | solution.py:412
  24.1 0.3 convert_element_type.33
  24.4 0.1 copy.45
  24.6 0.1 slice.69
  24.7 0.1 slice.76
  24.8 0.1 slice_select_fusion
  24.9 0.1 reshape.75.idx
  25.1 0.1 pad_add_fusion.1.meta
  25.2 18.1 %all-to-all-done.data = bf16[64,80,128]{2,1,0:T(8,128)(2,1)S(1)} async-done(((bf16[64,80,128]{2,1,0:T(8,128)(2,1)}), bf16[64,80,128]{2,1,0:T(8,128)(2,1)S(1)}, u32[]{:S(2)}, u32[]{:S(2)}) %all-to-all-start) | async-done | bytes 1310752 | tf_op jit(solution)/shard_map/all_to_all | solution.py:412
  43.3 1.6 add_up.2
  45.0 3.2 %collective-permute-start.2 = (f32[128,8,128]{2,1,0:T(8,128)S(1)}, f32[128,8,128]{2,1,0:T(8,128)S(1)}, u32[]{:S(2)}, u32[]{:S(2)}) collective-permute-start(f32[128,8,128]{2,1,0:T(8,128)S(1)} %add_up.2), channel_id=1, source_target_pairs={{0,64},{64,0},{1,65},{65,1},{2,66},{66,2},{3,67},{67,3},{4,68},{68... | collective-permute-start | bytes 1572872 | tf_op jit(solution)/shard_map/ppermute | solution.py:434
  48.1 1.5 collective-permute-done.2
  49.7 4.6 %collective-permute-start.3 = (bf16[10,512,512]{2,1,0:T(8,128)(2,1)}, bf16[10,512,512]{2,1,0:T(8,128)(2,1)}, u32[]{:S(2)}, u32[]{:S(2)}) collective-permute-start(bf16[10,512,512]{2,1,0:T(8,128)(2,1)} %get-tuple-element.30), channel_id=1, source_target_pairs={{64,0},{65,1},{66,2},{67,3},{68,4},{69,5},{70,6},{71,7},{72,8},{73... | collective-permute-start | bytes 15728648 | tf_op jit(solution)/shard_map/ppermute | solution.py:431
  54.3 0.2 copy.46
  54.6 14.1 %all_to_all.30 = bf16[64,24,128]{2,1,0:T(8,128)(2,1)S(1)} all-to-all(bf16[64,24,128]{2,1,0:T(8,128)(2,1)S(1)} %pad_maximum_fusion), channel_id=1, replica_groups=mesh['phase'=2,'blk'=64] {'blk'}, dimensions={0} | all-to-all | bytes 786432 | tf_op jit(solution)/shard_map/all_to_all | solution.py:412
  68.7 0.1 copy.50.x
  68.9 4.5 %split_products.1 = bf16[64,80,128]{2,1,0:T(8,128)(2,1)} custom-call(s32[11]{0:T(128)S(1)} %pad_add_fusion.1.meta, bf16[128,1024]{1,0:T(8,128)(2,1)S(1)} %copy.50.x, bf16[10,512,512]{2,1,0:T(8,128)(2,1)} %collective-permute-done.3.received, bf16[20,512,512]{2,1,0:T(8,128)(2,1)} %bitcast.53), custom_call_target="tpu_custom_call" | custom-call | tf_op jit(solution)/shard_map/split_products/pallas_call | solution.py:148
  73.4 4.7 %all-to-all-start.2 = ((bf16[64,80,128]{2,1,0:T(8,128)(2,1)}), bf16[64,80,128]{2,1,0:T(8,128)(2,1)S(1)}, u32[]{:S(2)}, u32[]{:S(2)}) async-start(bf16[64,80,128]{2,1,0:T(8,128)(2,1)} %split_products.1), calls=%async_computation.2 | async-start | bytes 2621440 | tf_op jit(solution)/shard_map/all_to_all | solution.py:412
  78.1 0.1 reshape.76.idx
  78.2 0.1 copy.61
  78.4 0.1 copy.48
  78.5 20.6 %all-to-all-done.2.data = bf16[64,80,128]{2,1,0:T(8,128)(2,1)S(1)} async-done(((bf16[64,80,128]{2,1,0:T(8,128)(2,1)}), bf16[64,80,128]{2,1,0:T(8,128)(2,1)S(1)}, u32[]{:S(2)}, u32[]{:S(2)}) %all-to-all-start.2) | async-done | bytes 1310752 | tf_op jit(solution)/shard_map/all_to_all | solution.py:412
  99.1 1.6 add_up.3.mine
  100.7 0.1 collective-permute-start.4
  100.8 0.8 copy.54.strike
  101.7 0.8 copy.53.notional
  102.5 0.2 collective-permute-done.4.other
  102.7 3.1 %value_and_hand_out.1 = (bf16[64,80,128]{2,1,0:T(8,128)(2,1)S(1)}, bf16[10,512,512]{2,1,0:T(8,128)(2,1)S(1)}) custom-call(s32[640]{0:T(1024)S(1)} %reshape.76.idx, f32[128,8,128]{2,1,0:T(8,128)S(1)} %add_up.3.mine, f32[128,8,128]{2,1,0:T(8,128)S(1)} %collective-permute-done.4.other, f32[128,8,1]{2,1,0:T(8,128)S(1)} %copy.53.notional, ...), custom_call_target="tpu_custom_call" | custom-call | tf_op jit(solution)/shard_map/value_and_hand_out/pallas_call | solution.py:231
  105.8 24.3 %all_to_all.31.grads.grads1 = bf16[64,80,128]{2,1,0:T(8,128)(2,1)S(1)} all-to-all(bf16[64,80,128]{2,1,0:T(8,128)(2,1)S(1)} %get-tuple-element.32), channel_id=1, replica_groups=mesh['phase'=2,'blk'=64] {'blk'}, dimensions={0} | all-to-all | bytes 2621440 | tf_op jit(solution)/shard_map/all_to_all | solution.py:412
  130.1 2.1 %first_backward.1 = f32[2,512,128]{2,1,0:T(8,128)S(1)} custom-call(s32[11]{0:T(128)S(1)} %pad_add_fusion.1.meta, bf16[64,80,128]{2,1,0:T(8,128)(2,1)S(1)} %all_to_all.31.grads.grads1, bf16[10,512,512]{2,1,0:T(8,128)(2,1)S(1)} %get-tuple-element.33.tiles), custom_call_target="tpu_custom_call" | custom-call | tf_op jit(solution)/shard_map/first_backward/pallas_call | solution.py:284
  132.2 2.7 %collective-permute-start.5 = (f32[2,512,128]{2,1,0:T(8,128)S(1)}, f32[2,512,128]{2,1,0:T(8,128)S(1)}, u32[]{:S(2)}, u32[]{:S(2)}) collective-permute-start(f32[2,512,128]{2,1,0:T(8,128)S(1)} %first_backward.1), channel_id=1, source_target_pairs={{0,64},{64,0},{1,65},{65,1},{2,66},{66,2},{3,67},{67,3},{4,68},{68... | collective-permute-start | bytes 1572872 | tf_op jit(solution)/shard_map/ppermute | solution.py:434
  135.0 1.5 collective-permute-done.5
  136.6 13.5 %all_to_all.32.blocks = bf16[64,16,128]{2,1,0:T(8,128)(2,1)S(1)} all-to-all(bf16[64,16,128]{2,1,0:T(8,128)(2,1)S(1)} %copy_bitcast_fusion), channel_id=1, replica_groups=mesh['phase'=2,'blk'=64] {'blk'}, dimensions={0} | all-to-all | bytes 524288 | tf_op jit(solution)/shard_map/all_to_all | solution.py:412
  150.0 2.4 %hand_out.1 = bf16[64,80,128]{2,1,0:T(8,128)(2,1)} custom-call(s32[640]{0:T(1024)S(1)} %reshape.75.idx, bf16[64,16,128]{2,1,0:T(8,128)(2,1)S(1)} %all_to_all.32.blocks), custom_call_target="tpu_custom_call" | custom-call | tf_op jit(solution)/shard_map/hand_out/pallas_call | solution.py:254
  152.5 4.9 %all-to-all-start.5 = ((bf16[64,80,128]{2,1,0:T(8,128)(2,1)}), bf16[64,80,128]{2,1,0:T(8,128)(2,1)S(1)}, u32[]{:S(2)}, u32[]{:S(2)}) async-start(bf16[64,80,128]{2,1,0:T(8,128)(2,1)} %hand_out.1), calls=%async_computation.5 | async-start | bytes 2621440 | tf_op jit(solution)/shard_map/all_to_all | solution.py:412
  157.4 1.3 collective-permute-start.7
  158.7 17.2 %all-to-all-done.5.grads0 = bf16[64,80,128]{2,1,0:T(8,128)(2,1)S(1)} async-done(((bf16[64,80,128]{2,1,0:T(8,128)(2,1)}), bf16[64,80,128]{2,1,0:T(8,128)(2,1)S(1)}, u32[]{:S(2)}, u32[]{:S(2)}) %all-to-all-start.5) | async-done | bytes 1310752 | tf_op jit(solution)/shard_map/all_to_all | solution.py:412
  175.9 6.9 %collective-permute-start.6 = (bf16[64,80,128]{2,1,0:T(8,128)(2,1)S(1)}, bf16[64,80,128]{2,1,0:T(8,128)(2,1)}, u32[]{:S(2)}, u32[]{:S(2)}) collective-permute-start(bf16[64,80,128]{2,1,0:T(8,128)(2,1)S(1)} %all-to-all-done.5.grads0), channel_id=1, source_target_pairs={{64,0},{65,1},{66,2},{67,3},{68,4},{69,5},{70,6},{71,7},{72,8},{73... | collective-permute-start | bytes 3932168 | tf_op jit(solution)/shard_map/ppermute | solution.py:431
  182.8 0.2 copy.56
  183.1 6.7 %last_backward_low.1 = (bf16[20,512,512]{2,1,0:T(8,128)(2,1)}, f32[2,512,128]{2,1,0:T(8,128)S(1)}) custom-call(s32[21]{0:T(128)S(1)} %pad_add_fusion.2.meta, bf16[64,80,128]{2,1,0:T(8,128)(2,1)S(1)} %all-to-all-done.5.grads0, bf16[64,80,128]{2,1,0:T(8,128)(2,1)} %collective-permute-done.7.grads1, bf16[2,512,128]{2,1,0:T(8,128)(2,1)S(1)} %bitcast_select_fusion.inputs, ...), custom_call_target="tpu_custom_call" | custom-call | tf_op jit(solution)/shard_map/last_backward_low/pallas_call | solution.py:369
  189.8 6.5 %last_backward_high.1 = (bf16[20,512,512]{2,1,0:T(8,128)(2,1)}, bf16[128,1024]{1,0:T(8,128)(2,1)}) custom-call(s32[21]{0:T(128)S(1)} %pad_add_fusion.2.meta, bf16[64,80,128]{2,1,0:T(8,128)(2,1)} %collective-permute-done.6.grads0, bf16[64,80,128]{2,1,0:T(8,128)(2,1)S(1)} %all_to_all.31.grads.grads1, ...), custom_call_target="tpu_custom_call", output_to_operand_aliasing={{0}: (6, {})} | custom-call | tf_op jit(solution)/shard_map/last_backward_high/pallas_call | solution.py:378
  (44 shorter events, 0.7 us)
Async XLA Ops:
  0.6 1.0 copy-start
  1.6 0.7 copy-start.2
  2.2 4.4 %copy-start.4 = (s32[1,1280]{1,0:T(1,128)S(1)}, s32[1,1280]{1,0:T(1,128)}, u32[]{:S(2)}) copy-start(s32[1,1280]{1,0:T(1,128)} %param.8) | copy-start | bytes 15364
  2.2 4.4 %copy-start.3 = (s32[1,20]{1,0:T(1,128)S(1)}, s32[1,20]{1,0:T(1,128)}, u32[]{:S(2)}) copy-start(s32[1,20]{1,0:T(1,128)} %cols_in.3) | copy-start | bytes 244
  2.2 6.3 %copy-start.5 = (f32[1024]{0:T(1024)S(1)}, f32[1024]{0:T(1024)}, u32[]{:S(2)}) copy-start(f32[1024]{0:T(1024)} %param.10) | copy-start | bytes 12292
  2.2 6.4 %copy-start.6 = (f32[1024]{0:T(1024)S(1)}, f32[1024]{0:T(1024)}, u32[]{:S(2)}) copy-start(f32[1024]{0:T(1024)} %param.11) | copy-start | bytes 12292
  2.2 6.4 %copy-start.1 = (bf16[128,1024]{1,0:T(8,128)(2,1)S(1)}, bf16[128,1024]{1,0:T(8,128)(2,1)}, u32[]{:S(2)}) copy-start(bf16[128,1024]{1,0:T(8,128)(2,1)} %x_in.3) | copy-start | bytes 786436
  5.3 6.0 %collective-permute-start.1 = (bf16[64,80,128]{2,1,0:T(8,128)(2,1)S(1)}, bf16[64,80,128]{2,1,0:T(8,128)(2,1)S(1)}, u32[]{:S(2)}, u32[]{:S(2)}) collective-permute-start(bf16[64,80,128]{2,1,0:T(8,128)(2,1)S(1)} %get-tuple-element.25), channel_id=1, source_target_pairs={{0,64},{1,65},{2,66},{3,67},{4,68},{5,69},{6,70},{7,71},{8,72},{9,... | collective-permute-start | bytes 3932168 | tf_op jit(solution)/shard_map/ppermute | solution.py:431
  6.7 17.9 %collective-permute-start = (s32[1300]{0:T(1024)S(1)}, s32[1300]{0:T(1024)S(1)}, u32[]{:S(2)}, u32[]{:S(2)}) collective-permute-start(s32[1300]{0:T(1024)S(1)} %pad_add_fusion), channel_id=1, source_target_pairs={{0,64},{64,0},{1,65},{65,1},{2,66},{66,2},{3,67},{67,3},{4,68},{68... | collective-permute-start | bytes 15608 | tf_op jit(solution)/shard_map/ppermute | solution.py:434
  12.6 30.7 %all-to-all-start = ((bf16[64,80,128]{2,1,0:T(8,128)(2,1)}), bf16[64,80,128]{2,1,0:T(8,128)(2,1)S(1)}, u32[]{:S(2)}, u32[]{:S(2)}) async-start(bf16[64,80,128]{2,1,0:T(8,128)(2,1)} %broadcast_select_fusion), calls=%async_computation | async-start | bytes 2621440 | tf_op jit(solution)/shard_map/all_to_all | solution.py:412
  45.0 4.7 %collective-permute-start.2 = (f32[128,8,128]{2,1,0:T(8,128)S(1)}, f32[128,8,128]{2,1,0:T(8,128)S(1)}, u32[]{:S(2)}, u32[]{:S(2)}) collective-permute-start(f32[128,8,128]{2,1,0:T(8,128)S(1)} %add_up.2), channel_id=1, source_target_pairs={{0,64},{64,0},{1,65},{65,1},{2,66},{66,2},{3,67},{67,3},{4,68},{68... | collective-permute-start | bytes 1572872 | tf_op jit(solution)/shard_map/ppermute | solution.py:434
  49.7 19.2 %collective-permute-start.3 = (bf16[10,512,512]{2,1,0:T(8,128)(2,1)}, bf16[10,512,512]{2,1,0:T(8,128)(2,1)}, u32[]{:S(2)}, u32[]{:S(2)}) collective-permute-start(bf16[10,512,512]{2,1,0:T(8,128)(2,1)} %get-tuple-element.30), channel_id=1, source_target_pairs={{64,0},{65,1},{66,2},{67,3},{68,4},{69,5},{70,6},{71,7},{72,8},{73... | collective-permute-start | bytes 15728648 | tf_op jit(solution)/shard_map/ppermute | solution.py:431
  73.4 25.7 %all-to-all-start.2 = ((bf16[64,80,128]{2,1,0:T(8,128)(2,1)}), bf16[64,80,128]{2,1,0:T(8,128)(2,1)S(1)}, u32[]{:S(2)}, u32[]{:S(2)}) async-start(bf16[64,80,128]{2,1,0:T(8,128)(2,1)} %split_products.1), calls=%async_computation.2 | async-start | bytes 2621440 | tf_op jit(solution)/shard_map/all_to_all | solution.py:412
  100.7 2.0 %collective-permute-start.4 = (f32[128,8,128]{2,1,0:T(8,128)S(1)}, f32[128,8,128]{2,1,0:T(8,128)S(1)}, u32[]{:S(2)}, u32[]{:S(2)}) collective-permute-start(f32[128,8,128]{2,1,0:T(8,128)S(1)} %add_up.3.mine), channel_id=1, source_target_pairs={{0,64},{64,0},{1,65},{65,1},{2,66},{66,2},{3,67},{67,3},{4,68},{68... | collective-permute-start | bytes 1572872 | tf_op jit(solution)/shard_map/ppermute | solution.py:434
  132.2 4.3 %collective-permute-start.5 = (f32[2,512,128]{2,1,0:T(8,128)S(1)}, f32[2,512,128]{2,1,0:T(8,128)S(1)}, u32[]{:S(2)}, u32[]{:S(2)}) collective-permute-start(f32[2,512,128]{2,1,0:T(8,128)S(1)} %first_backward.1), channel_id=1, source_target_pairs={{0,64},{64,0},{1,65},{65,1},{2,66},{66,2},{3,67},{67,3},{4,68},{68... | collective-permute-start | bytes 1572872 | tf_op jit(solution)/shard_map/ppermute | solution.py:434
  152.5 23.4 %all-to-all-start.5 = ((bf16[64,80,128]{2,1,0:T(8,128)(2,1)}), bf16[64,80,128]{2,1,0:T(8,128)(2,1)S(1)}, u32[]{:S(2)}, u32[]{:S(2)}) async-start(bf16[64,80,128]{2,1,0:T(8,128)(2,1)} %hand_out.1), calls=%async_computation.5 | async-start | bytes 2621440 | tf_op jit(solution)/shard_map/all_to_all | solution.py:412
  157.4 25.7 %collective-permute-start.7 = (bf16[64,80,128]{2,1,0:T(8,128)(2,1)S(1)}, bf16[64,80,128]{2,1,0:T(8,128)(2,1)}, u32[]{:S(2)}, u32[]{:S(2)}) collective-permute-start(bf16[64,80,128]{2,1,0:T(8,128)(2,1)S(1)} %all_to_all.31.grads.grads1), channel_id=1, source_target_pairs={{0,64},{1,65},{2,66},{3,67},{4,68},{5,69},{6,70},{7,71},{8,72},{9,... | collective-permute-start | bytes 3932168 | tf_op jit(solution)/shard_map/ppermute | solution.py:431
  175.9 13.9 %collective-permute-start.6 = (bf16[64,80,128]{2,1,0:T(8,128)(2,1)S(1)}, bf16[64,80,128]{2,1,0:T(8,128)(2,1)}, u32[]{:S(2)}, u32[]{:S(2)}) collective-permute-start(bf16[64,80,128]{2,1,0:T(8,128)(2,1)S(1)} %all-to-all-done.5.grads0), channel_id=1, source_target_pairs={{64,0},{65,1},{66,2},{67,3},{68,4},{69,5},{70,6},{71,7},{72,8},{73... | collective-permute-start | bytes 3932168 | tf_op jit(solution)/shard_map/ppermute | solution.py:431

commit v6 on v5

--- a/solution.py
+++ b/solution.py
@@ -293,103 +293,81 @@
     )(meta, grads, tiles)
 
 
-def last_backward_body(meta, grads0, grads1, inputs, tiles, *rest, first):
-    if first:
-        earlier, _, sens, adjoint_out, *scratch, total, adjoint, adjoint_sem = rest
-    else:
-        sens, total, *scratch = rest
-    grads, grads_sems, stage, out_sems, held, sems = scratch
-    take = tile_copies(tiles, first, held, sems)
-
+def last_backward_body(
+    meta, low0, low1, high0, high1, inputs, tiles, sens, adjoint_out, *scratch
+):
+    grads, grads_sems, stage, out_sems, held, sems, total, adjoint, adjoint_sem = scratch
     pairs = stage.shape[0]
+    half = pairs // 2
+    take = tile_copies(tiles, 0, held, sems)
 
     def grads_copy(source, k):
-        rows = slice(2 * SLICE * k, 2 * SLICE * (k + 1))
-        return pltpu.make_async_copy(source.at[:, rows], grads.at[:, rows], grads_sems.at[k])
-
-    @pl.when(meta[0] == 0)
-    def _():
-        for k in range(pairs):
-            grads_copy(grads0, k).start()
-
-    @pl.when(meta[0] == 1)
-    def _():
-        for k in range(pairs):
-            grads_copy(grads1, k).start()
-
-    for k in range(pairs):
-        take(k).start()
-    total[...] = earlier[...] if first else jnp.zeros_like(total)
+        rows = slice(2 * SLICE * (k % half), 2 * SLICE * (k % half + 1))
+        return pltpu.make_async_copy(
+            source.at[:, rows], grads.at[k // half, :, rows], grads_sems.at[k]
+        )
 
     def put(k):
-        return pltpu.make_async_copy(
-            stage.at[k // 2, k % 2], sens.at[first + k], out_sems.at[k]
-        )
-
+        return pltpu.make_async_copy(stage.at[k // 2, k % 2], sens.at[k], out_sems.at[k])
+
+    for section, halves in ((0, (low0, high0)), (1, (low1, high1))):
+
+        @pl.when(meta[0] == section)
+        def _(halves=halves):
+            for k in range(pairs):
+                grads_copy(halves[k // half], k).start()
+                take(k).start()
+
+    total[...] = jnp.zeros_like(total)
     for k in range(pairs):
         take(k).wait()
-        grads_copy(grads0, k).wait()
-        for u, grad in enumerate(tile_grad_pair(grads, k)):
-            col = meta[1 + first + 2 * k + u]
+        grads_copy(low0, k).wait()
+        for u, grad in enumerate(tile_grad_pair(grads.at[k // half], k % half)):
+            col = meta[1 + 2 * k + u]
             total[col] += jnp.dot(held[2 * k + u], grad, preferred_element_type=jnp.float32)
             stage[k, u] = lax.dot_general(
                 inputs[col], grad, (((1,), (1,)), ((), ())), preferred_element_type=jnp.float32
             ).astype(jnp.bfloat16)
             put(2 * k + u).start()
 
-    if first:
-        width = total.shape[1]
-        for c in range(total.shape[0]):
-            adjoint[:, c * width : (c + 1) * width] = total[c].T.astype(jnp.bfloat16)
-        adjoint_copy = pltpu.make_async_copy(adjoint, adjoint_out, adjoint_sem)
-        adjoint_copy.start()
-        adjoint_copy.wait()
+    width = total.shape[1]
+    for c in range(total.shape[0]):
+        adjoint[:, c * width : (c + 1) * width] = total[c].T.astype(jnp.bfloat16)
+    adjoint_copy = pltpu.make_async_copy(adjoint, adjoint_out, adjoint_sem)
+    adjoint_copy.start()
+    adjoint_copy.wait()
     for k in range(2 * pairs):
         put(k).wait()
 
 
-def last_backward_calls(meta, grads, inputs, tiles):
+def last_backward(meta, low0, low1, high0, high1, inputs, tiles):
     slots, width, _ = tiles.shape
-    half = slots // 2
     blocks_dev, _, scen = inputs.shape
-    smem = pl.BlockSpec(memory_space=pltpu.SMEM)
-    vmem = pl.BlockSpec(memory_space=pltpu.VMEM)
     hbm = pl.BlockSpec(memory_space=pl.ANY)
-    sens_shape = jax.ShapeDtypeStruct((slots, width, width), jnp.bfloat16)
-    total_shape = jax.ShapeDtypeStruct(inputs.shape, jnp.float32)
-    sems = pltpu.SemaphoreType.DMA((half // 2,))
-    scratch = [
-        pltpu.VMEM(grads[0][0].shape, jnp.bfloat16),
-        sems,
-        pltpu.VMEM((half // 2, 2, width, width), jnp.bfloat16),
-        pltpu.SemaphoreType.DMA((half,)),
-        *tile_scratch(half, width),
-    ]
     adjoint_shape = (scen, blocks_dev * width)
-    sens, total = pl.pallas_call(
-        functools.partial(last_backward_body, first=0),
-        in_specs=[smem, hbm, hbm, vmem, hbm],
-        out_specs=[hbm, vmem],
-        out_shape=[sens_shape, total_shape],
-        scratch_shapes=scratch,
-        compiler_params=params(STREAM_LIMIT),
-        name="last_backward_low",
-    )(meta, *grads[0], inputs, tiles)
-    return pl.pallas_call(
-        functools.partial(last_backward_body, first=half),
-        in_specs=[smem, hbm, hbm, vmem, hbm, vmem, hbm],
+    return pl.pallas_call(
+        last_backward_body,
+        in_specs=[pl.BlockSpec(memory_space=pltpu.SMEM)]
+        + [hbm] * 4
+        + [pl.BlockSpec(memory_space=pltpu.VMEM), hbm],
         out_specs=[hbm, hbm],
-        out_shape=[sens_shape, jax.ShapeDtypeStruct(adjoint_shape, jnp.bfloat16)],
+        out_shape=[
+            jax.ShapeDtypeStruct(tiles.shape, jnp.bfloat16),
+            jax.ShapeDtypeStruct(adjoint_shape, jnp.bfloat16),
+        ],
         scratch_shapes=[
-            *scratch,
+            pltpu.VMEM((2, *low0.shape), jnp.bfloat16),
+            pltpu.SemaphoreType.DMA((slots // 2,)),
+            pltpu.VMEM((slots // 2, 2, width, width), jnp.bfloat16),
+            pltpu.SemaphoreType.DMA((slots,)),
+            *tile_scratch(slots, width),
             pltpu.VMEM(inputs.shape, jnp.float32),
             pltpu.VMEM(adjoint_shape, jnp.bfloat16),
             pltpu.SemaphoreType.DMA,
         ],
-        input_output_aliases={6: 0},
         compiler_params=params(STREAM_LIMIT),
-        name="last_backward_high",
-    )(meta, *grads[1], inputs, tiles, total, sens)
+        name="last_backward",
+    )(meta, low0, low1, high0, high1, inputs, tiles)
 
 
 def three_terms(values):
@@ -496,9 +474,7 @@
     inputs = of_core(normals_held, shocks)
     low0 = exchange(only_hand_out(split_rows[0], arrived, shards, half))
     high0 = send(low0, 1)
-    sens, adjoint = last_backward_calls(
-        meta, ((low0, low1), (high0, high1)), inputs, tiles
-    )
+    sens, adjoint = last_backward(meta, low0, low1, high0, high1, inputs, tiles)
     return sens[None], adjoint[None]
 
 

time: 197 us -> 196 us (level)
  Pallas kernels: 34.3 us -> 30.3 us
    pallas_call x2 -> x1, Pallas kernels: 13.2 us -> 10.3 us  [last_backward(): pl.pallas_call(last_backward_body, in_specs=[pl.BlockSpec(memory_space=pl...]
  transfers between devices with their start and end apart: 11 -> 11, of which waited for: 6 -> 7; matrix products, arithmetic and copies ran while one was open for 3% -> 3% of each run, Pallas kernels for 5% -> 1%
where the time goes in v6:
time: 196 us; the launch traced here: 195 us
  waiting for transfers between devices  60.7 us (31%)
  blocking collectives  51.9 us (26%)
  starting transfers between devices  42.9 us (22%)
  Pallas kernels  30.3 us (15%)
  local copies, waits for them, and re-layouts  5.96 us (3%)
    all_to_all x3, waiting for transfers between devices, exchange(): return lax.all_to_all(block, 'blk', split_axis=0, concat_axis=0, tiled=True)  55.9 us
    all_to_all x3, blocking collectives, exchange(): return lax.all_to_all(block, 'blk', split_axis=0, concat_axis=0, tiled=True)  51.9 us
    all_to_all x3, starting transfers between devices, exchange(): return lax.all_to_all(block, 'blk', split_axis=0, concat_axis=0, tiled=True)  21 us
    ppermute x4, starting transfers between devices, send(): return lax.ppermute(block, 'phase', [(source, 1 - source)])  14.1 us
    pallas_call x1, Pallas kernels, last_backward(): pl.pallas_call(last_backward_body, in_specs=[pl.BlockSpec(memory_space=pl...  10.3 us
    ppermute x4, starting transfers between devices, swap(): return lax.ppermute(block, 'phase', [(0, 1), (1, 0)])  7.87 us
    pallas_call x2, Pallas kernels, first_products(): pl.pallas_call(functools.partial(first_products_body, first=first, moved=...  5.73 us
    pallas_call x1, Pallas kernels, split_products(): pl.pallas_call(split_products_body, in_specs=[pl.BlockSpec(memory_space=p...  4.49 us
  transfers between devices with their start and end apart: 11, of which 7 were waited for; matrix products, arithmetic and copies ran while one was open for 3% of the time, Pallas kernels for 1%

profile of v6, /device:TPU:1, one launch (start us, length us, event | category | flops | bytes accessed | tf_op | source)
XLA Modules:
  0.0 194.9 jit_solution(12669468718703630803)
XLA Ops:
  0.6 0.9 copy-done.1
  1.6 0.7 copy-done.3
  2.3 3.1 %first_products.2 = (bf16[64,80,128]{2,1,0:T(8,128)(2,1)S(1)}, bf16[10,512,512]{2,1,0:T(8,128)(2,1)}) custom-call(s32[1,20]{1,0:T(1,128)S(1)} %copy-done.3, bf16[128,1024]{1,0:T(8,128)(2,1)S(1)} %copy-done.1, bf16[20,512,512]{2,1,0:T(8,128)(2,1)} %bitcast.51), custom_call_target="tpu_custom_call" | custom-call | tf_op jit(solution)/shard_map/first_products/pallas_call | solution.py:94
  5.3 1.3 collective-permute-start.1
  6.7 1.9 collective-permute-start
  8.7 2.7 %first_products.3 = (bf16[64,80,128]{2,1,0:T(8,128)(2,1)S(1)}, bf16[10,512,512]{2,1,0:T(8,128)(2,1)}) custom-call(s32[1,20]{1,0:T(1,128)S(1)} %copy-done.4, bf16[128,1024]{1,0:T(8,128)(2,1)S(1)} %copy-done.2, bf16[20,512,512]{2,1,0:T(8,128)(2,1)} %bitcast.52, bf16[10,512,512]{2,1,0:T(8,128)(2,1)} %get-tuple-element.21.rest_0_), custom_call_target="tpu_custom_call", output_to_operand_aliasing={{1}: (3, {})} | custom-call | tf_op jit(solution)/shard_map/first_products/pallas_call | solution.py:94
  11.4 1.3 broadcast_select_fusion
  12.6 11.4 %all-to-all-start = ((bf16[64,80,128]{2,1,0:T(8,128)(2,1)}), bf16[64,80,128]{2,1,0:T(8,128)(2,1)S(1)}, u32[]{:S(2)}, u32[]{:S(2)}) async-start(bf16[64,80,128]{2,1,0:T(8,128)(2,1)} %broadcast_select_fusion), calls=%async_computation | async-start | bytes 2621440 | tf_op jit(solution)/shard_map/all_to_all | solution.py:390
  24.1 0.3 convert_element_type.33
  24.4 0.1 copy.44
  24.6 0.1 slice.69
  24.7 0.1 slice.76
  24.8 0.1 slice_select_fusion
  24.9 0.1 reshape.75.idx
  25.2 18.1 %all-to-all-done.data = bf16[64,80,128]{2,1,0:T(8,128)(2,1)S(1)} async-done(((bf16[64,80,128]{2,1,0:T(8,128)(2,1)}), bf16[64,80,128]{2,1,0:T(8,128)(2,1)S(1)}, u32[]{:S(2)}, u32[]{:S(2)}) %all-to-all-start) | async-done | bytes 1310752 | tf_op jit(solution)/shard_map/all_to_all | solution.py:390
  43.3 1.6 add_up.2
  45.0 3.2 %collective-permute-start.2 = (f32[128,8,128]{2,1,0:T(8,128)S(1)}, f32[128,8,128]{2,1,0:T(8,128)S(1)}, u32[]{:S(2)}, u32[]{:S(2)}) collective-permute-start(f32[128,8,128]{2,1,0:T(8,128)S(1)} %add_up.2), channel_id=1, source_target_pairs={{0,64},{64,0},{1,65},{65,1},{2,66},{66,2},{3,67},{67,3},{4,68},{68... | collective-permute-start | bytes 1572872 | tf_op jit(solution)/shard_map/ppermute | solution.py:412
  48.1 1.5 collective-permute-done.2
  49.7 4.6 %collective-permute-start.3 = (bf16[10,512,512]{2,1,0:T(8,128)(2,1)}, bf16[10,512,512]{2,1,0:T(8,128)(2,1)}, u32[]{:S(2)}, u32[]{:S(2)}) collective-permute-start(bf16[10,512,512]{2,1,0:T(8,128)(2,1)} %get-tuple-element.28), channel_id=1, source_target_pairs={{64,0},{65,1},{66,2},{67,3},{68,4},{69,5},{70,6},{71,7},{72,8},{73... | collective-permute-start | bytes 15728648 | tf_op jit(solution)/shard_map/ppermute | solution.py:409
  54.3 0.2 copy.45
  54.6 14.1 %all_to_all.30 = bf16[64,24,128]{2,1,0:T(8,128)(2,1)S(1)} all-to-all(bf16[64,24,128]{2,1,0:T(8,128)(2,1)S(1)} %pad_maximum_fusion), channel_id=1, replica_groups=mesh['phase'=2,'blk'=64] {'blk'}, dimensions={0} | all-to-all | bytes 786432 | tf_op jit(solution)/shard_map/all_to_all | solution.py:390
  68.7 0.1 copy.49.x
  68.9 4.5 %split_products.1 = bf16[64,80,128]{2,1,0:T(8,128)(2,1)} custom-call(s32[11]{0:T(128)S(1)} %pad_add_fusion.1.meta, bf16[128,1024]{1,0:T(8,128)(2,1)S(1)} %copy.49.x, bf16[10,512,512]{2,1,0:T(8,128)(2,1)} %collective-permute-done.3.received, bf16[20,512,512]{2,1,0:T(8,128)(2,1)} %bitcast.53), custom_call_target="tpu_custom_call" | custom-call | tf_op jit(solution)/shard_map/split_products/pallas_call | solution.py:148
  73.4 4.7 %all-to-all-start.2 = ((bf16[64,80,128]{2,1,0:T(8,128)(2,1)}), bf16[64,80,128]{2,1,0:T(8,128)(2,1)S(1)}, u32[]{:S(2)}, u32[]{:S(2)}) async-start(bf16[64,80,128]{2,1,0:T(8,128)(2,1)} %split_products.1), calls=%async_computation.2 | async-start | bytes 2621440 | tf_op jit(solution)/shard_map/all_to_all | solution.py:390
  78.1 0.1 reshape.76.idx
  78.2 0.1 copy.60
  78.4 0.1 copy.47
  78.5 20.6 %all-to-all-done.2.data = bf16[64,80,128]{2,1,0:T(8,128)(2,1)S(1)} async-done(((bf16[64,80,128]{2,1,0:T(8,128)(2,1)}), bf16[64,80,128]{2,1,0:T(8,128)(2,1)S(1)}, u32[]{:S(2)}, u32[]{:S(2)}) %all-to-all-start.2) | async-done | bytes 1310752 | tf_op jit(solution)/shard_map/all_to_all | solution.py:390
  99.1 1.6 add_up.3.mine
  100.7 0.1 collective-permute-start.4
  100.8 0.8 copy.53.strike
  101.7 0.8 copy.52.notional
  102.5 0.2 collective-permute-done.4.other
  102.7 3.1 %value_and_hand_out.1 = (bf16[64,80,128]{2,1,0:T(8,128)(2,1)S(1)}, bf16[10,512,512]{2,1,0:T(8,128)(2,1)S(1)}) custom-call(s32[640]{0:T(1024)S(1)} %reshape.76.idx, f32[128,8,128]{2,1,0:T(8,128)S(1)} %add_up.3.mine, f32[128,8,128]{2,1,0:T(8,128)S(1)} %collective-permute-done.4.other, f32[128,8,1]{2,1,0:T(8,128)S(1)} %copy.52.notional, ...), custom_call_target="tpu_custom_call" | custom-call | tf_op jit(solution)/shard_map/value_and_hand_out/pallas_call | solution.py:231
  105.8 24.3 %all_to_all.31.grads.high1 = bf16[64,80,128]{2,1,0:T(8,128)(2,1)S(1)} all-to-all(bf16[64,80,128]{2,1,0:T(8,128)(2,1)S(1)} %get-tuple-element.30), channel_id=1, replica_groups=mesh['phase'=2,'blk'=64] {'blk'}, dimensions={0} | all-to-all | bytes 2621440 | tf_op jit(solution)/shard_map/all_to_all | solution.py:390
  130.1 2.1 %first_backward.1 = f32[2,512,128]{2,1,0:T(8,128)S(1)} custom-call(s32[11]{0:T(128)S(1)} %pad_add_fusion.1.meta, bf16[64,80,128]{2,1,0:T(8,128)(2,1)S(1)} %all_to_all.31.grads.high1, bf16[10,512,512]{2,1,0:T(8,128)(2,1)S(1)} %get-tuple-element.31.tiles), custom_call_target="tpu_custom_call" | custom-call | tf_op jit(solution)/shard_map/first_backward/pallas_call | solution.py:284
  132.2 2.7 %collective-permute-start.5 = (f32[2,512,128]{2,1,0:T(8,128)S(1)}, f32[2,512,128]{2,1,0:T(8,128)S(1)}, u32[]{:S(2)}, u32[]{:S(2)}) collective-permute-start(f32[2,512,128]{2,1,0:T(8,128)S(1)} %first_backward.1), channel_id=1, source_target_pairs={{0,64},{64,0},{1,65},{65,1},{2,66},{66,2},{3,67},{67,3},{4,68},{68... | collective-permute-start | bytes 1572872 | tf_op jit(solution)/shard_map/ppermute | solution.py:412
  135.0 1.5 collective-permute-done.5
  136.6 13.5 %all_to_all.32.blocks = bf16[64,16,128]{2,1,0:T(8,128)(2,1)S(1)} all-to-all(bf16[64,16,128]{2,1,0:T(8,128)(2,1)S(1)} %copy_bitcast_fusion), channel_id=1, replica_groups=mesh['phase'=2,'blk'=64] {'blk'}, dimensions={0} | all-to-all | bytes 524288 | tf_op jit(solution)/shard_map/all_to_all | solution.py:390
  150.0 1.4 hand_out.1
  151.4 1.0 copy-done
  152.5 4.9 %all-to-all-start.5 = ((bf16[64,80,128]{2,1,0:T(8,128)(2,1)}), bf16[64,80,128]{2,1,0:T(8,128)(2,1)S(1)}, u32[]{:S(2)}, u32[]{:S(2)}) async-start(bf16[64,80,128]{2,1,0:T(8,128)(2,1)} %copy-done), calls=%async_computation.5 | async-start | bytes 2621440 | tf_op jit(solution)/shard_map/all_to_all | solution.py:390
  157.4 1.3 collective-permute-start.6
  158.7 17.2 %all-to-all-done.5.low0 = bf16[64,80,128]{2,1,0:T(8,128)(2,1)S(1)} async-done(((bf16[64,80,128]{2,1,0:T(8,128)(2,1)}), bf16[64,80,128]{2,1,0:T(8,128)(2,1)S(1)}, u32[]{:S(2)}, u32[]{:S(2)}) %all-to-all-start.5) | async-done | bytes 1310752 | tf_op jit(solution)/shard_map/all_to_all | solution.py:390
  175.9 6.9 %collective-permute-start.7 = (bf16[64,80,128]{2,1,0:T(8,128)(2,1)S(1)}, bf16[64,80,128]{2,1,0:T(8,128)(2,1)}, u32[]{:S(2)}, u32[]{:S(2)}) collective-permute-start(bf16[64,80,128]{2,1,0:T(8,128)(2,1)S(1)} %all-to-all-done.5.low0), channel_id=1, source_target_pairs={{64,0},{65,1},{66,2},{67,3},{68,4},{69,5},{70,6},{71,7},{72,8},{73... | collective-permute-start | bytes 3932168 | tf_op jit(solution)/shard_map/ppermute | solution.py:409
  182.8 0.2 copy.55
  183.1 1.5 collective-permute-done.7.high0
  184.5 10.3 %last_backward.1 = (bf16[20,512,512]{2,1,0:T(8,128)(2,1)}, bf16[128,1024]{1,0:T(8,128)(2,1)}) custom-call(s32[21]{0:T(128)S(1)} %pad_add_fusion.2.meta, bf16[64,80,128]{2,1,0:T(8,128)(2,1)S(1)} %all-to-all-done.5.low0, bf16[64,80,128]{2,1,0:T(8,128)(2,1)} %collective-permute-done.6.low1, bf16[64,80,128]{2,1,0:T(8,128)(2,1)} %collective-permute-done.7.high0, ...), custom_call_target="tpu_custom_call" | custom-call | tf_op jit(solution)/shard_map/last_backward/pallas_call | solution.py:348
  (45 shorter events, 0.8 us)
Async XLA Ops:
  0.6 1.0 copy-start.1
  1.6 0.7 copy-start.3
  2.2 4.4 %copy-start.5 = (s32[1,1280]{1,0:T(1,128)S(1)}, s32[1,1280]{1,0:T(1,128)}, u32[]{:S(2)}) copy-start(s32[1,1280]{1,0:T(1,128)} %param.8) | copy-start | bytes 15364
  2.2 4.4 %copy-start.4 = (s32[1,20]{1,0:T(1,128)S(1)}, s32[1,20]{1,0:T(1,128)}, u32[]{:S(2)}) copy-start(s32[1,20]{1,0:T(1,128)} %cols_in.3) | copy-start | bytes 244
  2.2 6.3 %copy-start.6 = (f32[1024]{0:T(1024)S(1)}, f32[1024]{0:T(1024)}, u32[]{:S(2)}) copy-start(f32[1024]{0:T(1024)} %param.10) | copy-start | bytes 12292
  2.2 6.4 %copy-start.7 = (f32[1024]{0:T(1024)S(1)}, f32[1024]{0:T(1024)}, u32[]{:S(2)}) copy-start(f32[1024]{0:T(1024)} %param.11) | copy-start | bytes 12292
  2.2 6.4 %copy-start.2 = (bf16[128,1024]{1,0:T(8,128)(2,1)S(1)}, bf16[128,1024]{1,0:T(8,128)(2,1)}, u32[]{:S(2)}) copy-start(bf16[128,1024]{1,0:T(8,128)(2,1)} %x_in.3) | copy-start | bytes 786436
  5.3 6.0 %collective-permute-start.1 = (bf16[64,80,128]{2,1,0:T(8,128)(2,1)S(1)}, bf16[64,80,128]{2,1,0:T(8,128)(2,1)S(1)}, u32[]{:S(2)}, u32[]{:S(2)}) collective-permute-start(bf16[64,80,128]{2,1,0:T(8,128)(2,1)S(1)} %get-tuple-element.23), channel_id=1, source_target_pairs={{0,64},{1,65},{2,66},{3,67},{4,68},{5,69},{6,70},{7,71},{8,72},{9,... | collective-permute-start | bytes 3932168 | tf_op jit(solution)/shard_map/ppermute | solution.py:409
  6.7 17.9 %collective-permute-start = (s32[1300]{0:T(1024)S(1)}, s32[1300]{0:T(1024)S(1)}, u32[]{:S(2)}, u32[]{:S(2)}) collective-permute-start(s32[1300]{0:T(1024)S(1)} %pad_add_fusion), channel_id=1, source_target_pairs={{0,64},{64,0},{1,65},{65,1},{2,66},{66,2},{3,67},{67,3},{4,68},{68... | collective-permute-start | bytes 15608 | tf_op jit(solution)/shard_map/ppermute | solution.py:412
  12.6 30.7 %all-to-all-start = ((bf16[64,80,128]{2,1,0:T(8,128)(2,1)}), bf16[64,80,128]{2,1,0:T(8,128)(2,1)S(1)}, u32[]{:S(2)}, u32[]{:S(2)}) async-start(bf16[64,80,128]{2,1,0:T(8,128)(2,1)} %broadcast_select_fusion), calls=%async_computation | async-start | bytes 2621440 | tf_op jit(solution)/shard_map/all_to_all | solution.py:390
  45.0 4.7 %collective-permute-start.2 = (f32[128,8,128]{2,1,0:T(8,128)S(1)}, f32[128,8,128]{2,1,0:T(8,128)S(1)}, u32[]{:S(2)}, u32[]{:S(2)}) collective-permute-start(f32[128,8,128]{2,1,0:T(8,128)S(1)} %add_up.2), channel_id=1, source_target_pairs={{0,64},{64,0},{1,65},{65,1},{2,66},{66,2},{3,67},{67,3},{4,68},{68... | collective-permute-start | bytes 1572872 | tf_op jit(solution)/shard_map/ppermute | solution.py:412
  49.7 19.2 %collective-permute-start.3 = (bf16[10,512,512]{2,1,0:T(8,128)(2,1)}, bf16[10,512,512]{2,1,0:T(8,128)(2,1)}, u32[]{:S(2)}, u32[]{:S(2)}) collective-permute-start(bf16[10,512,512]{2,1,0:T(8,128)(2,1)} %get-tuple-element.28), channel_id=1, source_target_pairs={{64,0},{65,1},{66,2},{67,3},{68,4},{69,5},{70,6},{71,7},{72,8},{73... | collective-permute-start | bytes 15728648 | tf_op jit(solution)/shard_map/ppermute | solution.py:409
  73.4 25.7 %all-to-all-start.2 = ((bf16[64,80,128]{2,1,0:T(8,128)(2,1)}), bf16[64,80,128]{2,1,0:T(8,128)(2,1)S(1)}, u32[]{:S(2)}, u32[]{:S(2)}) async-start(bf16[64,80,128]{2,1,0:T(8,128)(2,1)} %split_products.1), calls=%async_computation.2 | async-start | bytes 2621440 | tf_op jit(solution)/shard_map/all_to_all | solution.py:390
  100.7 2.0 %collective-permute-start.4 = (f32[128,8,128]{2,1,0:T(8,128)S(1)}, f32[128,8,128]{2,1,0:T(8,128)S(1)}, u32[]{:S(2)}, u32[]{:S(2)}) collective-permute-start(f32[128,8,128]{2,1,0:T(8,128)S(1)} %add_up.3.mine), channel_id=1, source_target_pairs={{0,64},{64,0},{1,65},{65,1},{2,66},{66,2},{3,67},{67,3},{4,68},{68... | collective-permute-start | bytes 1572872 | tf_op jit(solution)/shard_map/ppermute | solution.py:412
  132.2 4.3 %collective-permute-start.5 = (f32[2,512,128]{2,1,0:T(8,128)S(1)}, f32[2,512,128]{2,1,0:T(8,128)S(1)}, u32[]{:S(2)}, u32[]{:S(2)}) collective-permute-start(f32[2,512,128]{2,1,0:T(8,128)S(1)} %first_backward.1), channel_id=1, source_target_pairs={{0,64},{64,0},{1,65},{65,1},{2,66},{66,2},{3,67},{67,3},{4,68},{68... | collective-permute-start | bytes 1572872 | tf_op jit(solution)/shard_map/ppermute | solution.py:412
  151.4 1.1 copy-start
  152.5 23.4 %all-to-all-start.5 = ((bf16[64,80,128]{2,1,0:T(8,128)(2,1)}), bf16[64,80,128]{2,1,0:T(8,128)(2,1)S(1)}, u32[]{:S(2)}, u32[]{:S(2)}) async-start(bf16[64,80,128]{2,1,0:T(8,128)(2,1)} %copy-done), calls=%async_computation.5 | async-start | bytes 2621440 | tf_op jit(solution)/shard_map/all_to_all | solution.py:390
  157.4 25.6 %collective-permute-start.6 = (bf16[64,80,128]{2,1,0:T(8,128)(2,1)S(1)}, bf16[64,80,128]{2,1,0:T(8,128)(2,1)}, u32[]{:S(2)}, u32[]{:S(2)}) collective-permute-start(bf16[64,80,128]{2,1,0:T(8,128)(2,1)S(1)} %all_to_all.31.grads.high1), channel_id=1, source_target_pairs={{0,64},{1,65},{2,66},{3,67},{4,68},{5,69},{6,70},{7,71},{8,72},{9,... | collective-permute-start | bytes 3932168 | tf_op jit(solution)/shard_map/ppermute | solution.py:409
  175.9 8.6 %collective-permute-start.7 = (bf16[64,80,128]{2,1,0:T(8,128)(2,1)S(1)}, bf16[64,80,128]{2,1,0:T(8,128)(2,1)}, u32[]{:S(2)}, u32[]{:S(2)}) collective-permute-start(bf16[64,80,128]{2,1,0:T(8,128)(2,1)S(1)} %all-to-all-done.5.low0), channel_id=1, source_target_pairs={{64,0},{65,1},{66,2},{67,3},{68,4},{69,5},{70,6},{71,7},{72,8},{73... | collective-permute-start | bytes 3932168 | tf_op jit(solution)/shard_map/ppermute | solution.py:409
